TPU v7x, 32 devices: a whole 2x2x4 slice. The times are simulated.
32 devices in a mesh: section: 4 (over y, x), expert: 8 (over z, core).
Axes of the slice: x: 2, y: 2, z: 4, core: 2. Of those that a mesh axis runs over, the one named last changes fastest.
Arguments:
- tokens: bfloat16 [4, 128, 7168], P('section', 'expert'), may hold values from -6 to 6
- route_experts: int32 [4, 128, 2], P('section', 'expert'), may hold values from 0 to 3, as said below
- route_slots: int32 [4, 128, 2], P('section', 'expert'), may hold values from 0 to 15, as said below
- route_weights: float32 [4, 128, 2], P('section', 'expert'), may hold values from 0.1 to 1
- gate_weight: bfloat16 [4, 7168, 8192], P('section', None, 'expert'), may hold values from -0.0625 to 0.0625
- up_weight: bfloat16 [4, 7168, 8192], P('section', None, 'expert'), may hold values from -0.0625 to 0.0625
- down_weight: bfloat16 [4, 8192, 7168], P('section', 'expert'), may hold values from -0.125 to 0.125
- query_nope: bfloat16 [4, 256, 2048], P('section', None, 'expert'), may hold values from -6 to 6
- query_rope: bfloat16 [4, 256, 1024], P('section', None, 'expert'), may hold values from -6 to 6
- key_nope: bfloat16 [4, 256, 2048], P('section', None, 'expert'), may hold values from -6 to 6
- key_rope: bfloat16 [4, 256, 64], P('section'), may hold values from -6 to 6
- value_heads: bfloat16 [4, 256, 2048], P('section', None, 'expert'), may hold values from -6 to 6
- upstream: bfloat16 [4, 256, 2048], P('section', None, 'expert'), may hold values from -24 to 24
Outputs:
- expert_mix: bfloat16 [4, 128, 7168], P('section', 'expert')
- query_grad: bfloat16 [4, 256, 2048], P('section', None, 'expert')
- rotary_grad: bfloat16 [4, 256, 1024], P('section', None, 'expert')
- key_grad: bfloat16 [4, 256, 2048], P('section', None, 'expert')
- value_grad: bfloat16 [4, 256, 2048], P('section', None, 'expert')
- shared_grad: float32 [4, 256, 64], P('section', 'expert')
Inputs may be any that keep to these rules, and one draw needn't show every extreme that they name: `route_experts`: each token names 2 different experts. The 16 tokens of one device name each expert at most 16 times, and in every section one expert is named by every token of every device. `route_slots`: for each device and expert, the choices that name the expert have distinct slots.
All inputs are finite; a program needn't handle non-finite values.
Results may differ from a plain program's by a relative error of at most 0.008.
Values may be sent and summed in bfloat16 or wider, within the bound.
No kernel may reach another device: no remote copies, remote signals or barrier semaphores. Data moves between devices by JAX's collectives and lax.ppermute only.
A program may use at most 128 MiB of HBM per device.

v0:
```python
import math

import jax
import jax.numpy as jnp
from jax import lax
from jax.sharding import PartitionSpec as P

EXPERTS = 4
TOP = 2
NOPE = 128
ROPE = 64
VDIM = 128
CAP = 16
QBLOCK = 256


yarn_factor = 40.0
yarn_base = 10000.0
yarn_initial = 4096.0
yarn_fast = 32.0
yarn_slow = 1.0
mask_fill = -1e30


def from_behind(array, axis, by):
    size = lax.axis_size(axis)
    pairs = [(i, i + by) for i in range(size) if 0 <= i + by < size]
    return lax.ppermute(array, axis, pairs)


def correction_point(rotations, rope_width):
    return (
        rope_width
        * math.log(yarn_initial / (rotations * 2.0 * math.pi))
        / (2.0 * math.log(yarn_base))
    )


def rotary_tables(length, rope_width):
    half_width = rope_width // 2
    lowest = max(math.floor(correction_point(yarn_fast, rope_width)), 0)
    highest = min(math.ceil(correction_point(yarn_slow, rope_width)), rope_width - 1)
    spread = max(highest - lowest, 0.001)
    unit_index = jnp.arange(half_width).astype(jnp.float32)
    extrapolated = 1.0 / yarn_base ** (2.0 * unit_index / rope_width)
    interpolated = extrapolated / yarn_factor
    ramp_value = jnp.clip((unit_index - lowest) / spread, 0.0, 1.0)
    frequency = interpolated * ramp_value + extrapolated * (1.0 - ramp_value)
    angles = jnp.arange(length).astype(jnp.float32)[:, None] * frequency[None, :]
    return (jnp.cos(angles), jnp.sin(angles))


def score_scale():
    magnitude = 0.1 * math.log(yarn_factor) + 1.0
    return (NOPE + ROPE) ** (-0.5) * magnitude * magnitude


def rotate(operand, cosine_table, sine_table):
    paired = operand.reshape(operand.shape[:-1] + (operand.shape[-1] // 2, 2))
    first_part = paired[..., 0]
    second = paired[..., 1]
    turned = jnp.stack(
        [
            first_part * cosine_table - second * sine_table,
            first_part * sine_table + second * cosine_table,
        ],
        axis=-1,
    )
    return turned.reshape(operand.shape)


def expert_rows(received, gate_part, up_part, down_part):
    leading = received.shape[:-1]
    flat_rows = received.reshape(-1, received.shape[-1])
    gate_value = jnp.dot(flat_rows, gate_part, preferred_element_type=jnp.float32)
    up_value = jnp.dot(flat_rows, up_part, preferred_element_type=jnp.float32)
    hidden = (jax.nn.silu(gate_value) * up_value).astype(jnp.bfloat16)
    partial_out = jnp.dot(hidden, down_part, preferred_element_type=jnp.float32).astype(
        jnp.bfloat16
    )
    return partial_out.reshape(leading + (down_part.shape[1],))


def mixture(tokens, route_experts, route_slots, route_weights, gate_part, up_part, down_part):
    tok_rows = tokens.shape[0]
    model_width = tokens.shape[1]
    devices = lax.axis_size("expert")
    group_size = devices // EXPERTS
    targets = route_experts * CAP + route_slots
    slot_index = lax.broadcasted_iota(jnp.int32, (EXPERTS * CAP, tok_rows, TOP), 0)
    placing = jnp.sum((slot_index == targets[None, :, :]).astype(jnp.float32), axis=2)
    placing = placing.astype(jnp.bfloat16).reshape(EXPERTS, CAP, tok_rows)
    column_index = lax.broadcasted_iota(jnp.int32, (tok_rows, EXPERTS * CAP, TOP), 1)
    mixing = jnp.sum(
        jnp.where(column_index == targets[:, None, :], route_weights[:, None, :], 0.0), axis=2
    )
    mixing = mixing.reshape(tok_rows, EXPERTS, CAP)
    send_rows = jnp.einsum(
        "ect,td->ecd", placing, tokens, preferred_element_type=jnp.float32
    ).astype(jnp.bfloat16)
    copies = jnp.repeat(send_rows, group_size, axis=0)
    partials = expert_rows(
        lax.all_to_all(copies, "expert", split_axis=0, concat_axis=0, tiled=True),
        gate_part,
        up_part,
        down_part,
    )
    returned = lax.all_to_all(partials, "expert", split_axis=0, concat_axis=0, tiled=True)
    summed = jnp.sum(
        returned.reshape(EXPERTS, group_size, CAP, model_width), axis=1, dtype=jnp.float32
    )
    expert_out = lax.optimization_barrier(summed.astype(jnp.bfloat16)).astype(jnp.float32)
    mixed = jnp.einsum("tec,ecd->td", mixing, expert_out, precision=lax.Precision.HIGHEST)
    return mixed.astype(jnp.bfloat16)


def attention_grads(query_nope, query_rope, key_nope, key_rope, value_heads, upstream):
    sequence = query_nope.shape[0]
    head_count = query_nope.shape[1] // NOPE
    scale_value = score_scale()
    cosine_table, sine_table = rotary_tables(sequence, ROPE)
    query_plain = query_nope.reshape(sequence, head_count, NOPE)
    query_turned = rotate(
        query_rope.reshape(sequence, head_count, ROPE).astype(jnp.float32),
        cosine_table[:, None, :],
        sine_table[:, None, :],
    ).astype(jnp.bfloat16)
    key_turned = rotate(key_rope.astype(jnp.float32), cosine_table, sine_table).astype(jnp.bfloat16)
    key_plain = key_nope.reshape(sequence, head_count, NOPE)
    value_split = value_heads.reshape(sequence, head_count, VDIM)
    upstream_split = upstream.reshape(sequence, head_count, VDIM)
    key_pos = lax.broadcasted_iota(jnp.int32, (1, 1, sequence), 2)
    block_stop = QBLOCK
    scores = (
        jnp.einsum("qhd,khd->hqk", query_plain, key_plain, preferred_element_type=jnp.float32)
        + jnp.einsum("qhr,kr->hqk", query_turned, key_turned, preferred_element_type=jnp.float32)
    ) * scale_value
    query_pos = 0 + lax.broadcasted_iota(jnp.int32, (1, QBLOCK, 1), 1)
    scores = jnp.where(key_pos <= query_pos, scores, mask_fill)
    row_top = jnp.max(scores, axis=2, keepdims=True)
    weights = jnp.exp(scores - row_top)
    softmaxed = weights / jnp.sum(weights, axis=2, keepdims=True)
    soft_low = softmaxed.astype(jnp.bfloat16)
    value_total = jnp.einsum(
        "hqk,qhd->khd", soft_low, upstream_split, preferred_element_type=jnp.float32
    )
    prob_grad = jnp.einsum(
        "qhd,khd->hqk", upstream_split, value_split, preferred_element_type=jnp.float32
    )
    row_sum = jnp.sum(softmaxed * prob_grad, axis=2, keepdims=True)
    score_grad = (scale_value * softmaxed * (prob_grad - row_sum)).astype(jnp.bfloat16)
    query_parts = jnp.einsum(
        "hqk,khd->qhd", score_grad, key_plain, preferred_element_type=jnp.float32
    ).astype(jnp.bfloat16)
    turned_query = jnp.einsum(
        "hqk,kr->qhr", score_grad, key_turned, preferred_element_type=jnp.float32
    )
    rotary_parts = rotate(
        turned_query, cosine_table[0:block_stop, None, :], -sine_table[0:block_stop, None, :]
    ).astype(jnp.bfloat16)
    plain_total = jnp.einsum(
        "hqk,qhd->khd", score_grad, query_plain, preferred_element_type=jnp.float32
    )
    turned_total = jnp.einsum(
        "hqk,qhr->kr", score_grad, query_turned, preferred_element_type=jnp.float32
    )
    query_here = query_parts.reshape(sequence, head_count * NOPE)
    rotary_here = rotary_parts.reshape(sequence, head_count * ROPE)
    key_here = plain_total.astype(jnp.bfloat16).reshape(sequence, head_count * NOPE)
    value_here = value_total.astype(jnp.bfloat16).reshape(sequence, head_count * VDIM)
    shared_turn = rotate(turned_total, cosine_table, -sine_table)
    return (query_here, rotary_here, key_here, value_here, shared_turn)


def per_device(
    tokens,
    route_experts,
    route_slots,
    route_weights,
    gate_weight,
    up_weight,
    down_weight,
    query_nope,
    query_rope,
    key_nope,
    key_rope,
    value_heads,
    upstream,
):
    expert_mix = mixture(
        tokens[0],
        route_experts[0],
        route_slots[0],
        route_weights[0],
        gate_weight[0],
        up_weight[0],
        down_weight[0],
    )
    query_here, rotary_here, key_here, value_here, shared_turn = attention_grads(
        query_nope[0], query_rope[0], key_nope[0], key_rope[0], value_heads[0], upstream[0]
    )
    shared_local = lax.psum_scatter(shared_turn, "expert", scatter_dimension=0, tiled=True)
    moved = from_behind((query_here, rotary_here, key_here, value_here), "section", -1)
    shared_grad = from_behind(shared_local, "section", -1)
    return (
        expert_mix[None],
        moved[0][None],
        moved[1][None],
        moved[2][None],
        moved[3][None],
        shared_grad[None],
    )


def solution(mesh):
    return jax.shard_map(
        per_device,
        mesh=mesh,
        in_specs=(
            P("section", "expert", None),
            P("section", "expert", None),
            P("section", "expert", None),
            P("section", "expert", None),
            P("section", None, "expert"),
            P("section", None, "expert"),
            P("section", "expert", None),
            P("section", None, "expert"),
            P("section", None, "expert"),
            P("section", None, "expert"),
            P("section", None, None),
            P("section", None, "expert"),
            P("section", None, "expert"),
        ),
        out_specs=(
            P("section", "expert", None),
            P("section", None, "expert"),
            P("section", None, "expert"),
            P("section", None, "expert"),
            P("section", None, "expert"),
            P("section", "expert", None),
        ),
        check_vma=False,
    )
```

profile of v0, /device:TPU:0, one launch (start us, length us, event | category | flops | bytes accessed | tf_op | source)
XLA Modules:
  0.0 150.2 jit_solution(10373211873279318758)
XLA Ops:
  7.2 0.7 add_bitcast_fusion
  9.1 1.4 broadcast_in_dim.61
  10.5 6.3 %all-to-all-start = ((bf16[8,16,7168]{2,1,0:T(8,128)(2,1)}), bf16[8,16,7168]{2,1,0:T(8,128)(2,1)}, u32[]{:S(2)}, u32[]{:S(2)}) async-start(bf16[8,16,7168]{2,1,0:T(8,128)(2,1)} %bitcast.5), calls=%async_computation | async-start | bytes 3670016 | tf_op jit(solution)/shard_map/all_to_all | solution.py:103
  16.8 0.8 copy.154
  18.0 0.8 fusion.43
  20.1 40.2 %all-to-all-done = bf16[8,16,7168]{2,1,0:T(8,128)(2,1)} async-done(((bf16[8,16,7168]{2,1,0:T(8,128)(2,1)}), bf16[8,16,7168]{2,1,0:T(8,128)(2,1)}, u32[]{:S(2)}, u32[]{:S(2)}) %all-to-all-start) | async-done | bytes 1835040 | tf_op jit(solution)/shard_map/all_to_all | solution.py:103
  60.4 7.9 %fusion.5 = f32[128,1024]{1,0:T(8,128)S(1)} fusion(bf16[128,7168]{1,0:T(8,128)(2,1)} %bitcast.6, bf16[1,7168,1024]{2,1,0:T(8,128)(2,1)} %param.17), kind=kOutput, calls=%fused_computation.5 | convolution fusion | flops 1879048192 | bytes 17039360 | tf_op jit(solution)/shard_map/dot_general | solution.py:75
  68.5 1.2 slice-done.3
  69.7 4.5 %fusion.19 = bf16[128,1024]{1,0:T(8,128)(2,1)S(1)} fusion(bf16[128,7168]{1,0:T(8,128)(2,1)} %bitcast.6, bf16[1,7168,1024]{2,1,0:T(8,128)(2,1)S(1)} %bitcast.106, f32[128,1024]{1,0:T(8,128)S(1)} %fusion.5), kind=kOutput, calls=%fused_computation.20 | convolution fusion | flops 1879834624 | bytes 17301504 | tf_op jit(solution)/shard_map/dot_general | solution.py:76
  74.7 3.4 %fusion.7 = bf16[128,7168]{1,0:T(8,128)(2,1)} fusion(bf16[128,1024]{1,0:T(8,128)(2,1)S(1)} %fusion.19, bf16[1,1024,7168]{2,1,0:T(8,128)(2,1)S(1)} %bitcast.108), kind=kOutput, calls=%fused_computation.7 | convolution fusion | flops 1879965696 | bytes 16777216 | tf_op jit(solution)/shard_map/dot_general | solution.py:78
  78.1 3.7 %all-to-all-start.1 = ((bf16[8,16,7168]{2,1,0:T(8,128)(2,1)}), bf16[8,16,7168]{2,1,0:T(8,128)(2,1)S(1)}, u32[]{:S(2)}, u32[]{:S(2)}) async-start(bf16[8,16,7168]{2,1,0:T(8,128)(2,1)} %bitcast.10), calls=%async_computation.1 | async-start | bytes 3670016 | tf_op jit(solution)/shard_map/all_to_all | solution.py:108
  82.2 1.0 copy.156
  83.2 1.0 reshape_squeeze.16
  85.2 1.1 convolution_convert_fusion.1
  86.3 0.8 copy.118
  87.0 1.3 collective-permute-start
  88.7 1.3 collective-permute-start.2
  90.0 1.2 convolution_convert_fusion.2
  91.3 1.3 collective-permute-start.3
  92.6 0.8 maximum_convert_fusion
  93.6 0.9 fusion.37
  94.7 0.8 copy.146
  95.4 0.7 maximum_convert_fusion.1
  96.6 0.8 subtract_convert_fusion
  97.5 1.3 collective-permute-start.1
  98.8 33.3 %reduce-scatter.4.cloned.1.call-done = f32[32,64]{1,0:T(8,128)} async-done(((f32[256,64]{1,0:T(8,128)}), f32[32,64]{1,0:T(8,128)}) %reduce-scatter.4.cloned.1.call-update) | async-done | bytes 8208
  132.1 0.8 copy.147
  132.9 1.3 collective-permute-start.4
  134.2 0.8 select_reduce_fusion
  135.0 0.7 copy.135
  135.8 2.9 %collective-permute-done.4 = f32[32,64]{0,1:T(8,128)S(1)} collective-permute-done((f32[32,64]{0,1:T(8,128)S(1)}, f32[32,64]{0,1:T(8,128)S(1)}, u32[]{:S(2)}, u32[]{:S(2)}) %collective-permute-start.4) | collective-permute-done | bytes 8224 | tf_op jit(solution)/shard_map/ppermute | solution.py:28
  139.6 1.8 %fusion.11 = bf16[1,16,7168]{2,1,0:T(8,128)(2,1)} fusion(bf16[4,16,7168]{2,1,0:T(8,128)(2,1)S(1)} %bitcast_reduce_fusion, f32[16,4,16]{2,1,0:T(4,128)S(1)} %reshape.338), kind=kOutput, calls=%fused_computation.11 | convolution fusion | flops 88195072 | bytes 1150976 | tf_op jit(solution)/shard_map/tec,ecd->td/dot_general | solution.py:113
  (97 shorter events, 9.0 us)
Async XLA Ops:
  7.2 1.5 copy-start
  7.9 0.5 copy-start.13
  8.6 8.1 %copy-start.7 = (bf16[1,256,256]{2,1,0:T(8,128)(2,1)S(1)}, bf16[1,256,256]{2,1,0:T(8,128)(2,1)}, u32[]{:S(2)}) copy-start(bf16[1,256,256]{2,1,0:T(8,128)(2,1)} %param.22) | copy-start | bytes 393220
  8.7 8.9 %copy-start.11 = (bf16[1,256,64]{1,2,0:T(8,128)(2,1)S(1)}, bf16[1,256,64]{1,2,0:T(8,128)(2,1)}, u32[]{:S(2)}) copy-start(bf16[1,256,64]{1,2,0:T(8,128)(2,1)} %param.23) | copy-start | bytes 98308
  9.0 8.6 %copy-start.10 = (bf16[1,256,128]{2,1,0:T(8,128)(2,1)S(1)}, bf16[1,256,128]{2,1,0:T(8,128)(2,1)}, u32[]{:S(2)}) copy-start(bf16[1,256,128]{2,1,0:T(8,128)(2,1)} %param.21) | copy-start | bytes 196612
  9.1 8.8 %copy-start.8 = (bf16[1,256,256]{2,1,0:T(8,128)(2,1)S(1)}, bf16[1,256,256]{2,1,0:T(8,128)(2,1)}, u32[]{:S(2)}) copy-start(bf16[1,256,256]{2,1,0:T(8,128)(2,1)} %param.20) | copy-start | bytes 393220
  10.5 49.9 %all-to-all-start = ((bf16[8,16,7168]{2,1,0:T(8,128)(2,1)}), bf16[8,16,7168]{2,1,0:T(8,128)(2,1)}, u32[]{:S(2)}, u32[]{:S(2)}) async-start(bf16[8,16,7168]{2,1,0:T(8,128)(2,1)} %bitcast.5), calls=%async_computation | async-start | bytes 3670016 | tf_op jit(solution)/shard_map/all_to_all | solution.py:103
  16.8 51.6 %slice-start = ((s8[14680064]{0:T(1024)(128)(4,1)}), s8[2097152]{0:T(1024)(128)(4,1)S(1)}, s32[]{:S(2)}) async-start(s8[14680064]{0:T(1024)(128)(4,1)} %bitcast.105), calls=%async_computation.4 | async-start | bytes 4194304
  17.9 0.9 copy-start.15
  18.0 0.9 copy-start.12
  18.8 41.6 %copy-start.3 = (f32[256,32]{0,1:T(8,128)}, f32[256,32]{0,1:T(8,128)S(1)}, u32[]{:S(2)}) copy-start(f32[256,32]{0,1:T(8,128)S(1)} %get-tuple-element.40) | copy-start | bytes 98308
  19.1 49.3 %copy-start.6 = (bf16[256,32,1]{0,1,2:T(8,128)(2,1)}, bf16[256,32,1]{0,1,2:T(8,128)(2,1)S(1)}, u32[]{:S(2)}) copy-start(bf16[256,32,1]{0,1,2:T(8,128)(2,1)S(1)} %get-tuple-element.35) | copy-start | bytes 49156
  19.2 41.1 %copy-start.2 = (bf16[256,2,32,1]{0,2,3,1:T(8,128)(2,1)}, bf16[256,2,32,1]{0,2,3,1:T(8,128)(2,1)S(1)}, u32[]{:S(2)}) copy-start(bf16[256,2,32,1]{0,2,3,1:T(8,128)(2,1)S(1)} %get-tuple-element.27) | copy-start | bytes 98308
  60.3 8.0 %slice-start.1 = ((s8[14680064]{0:T(1024)(128)(4,1)}), s8[4194304]{0:T(1024)(128)(4,1)S(1)}, s32[]{:S(2)}) async-start(s8[14680064]{0:T(1024)(128)(4,1)} %bitcast.105), calls=%async_computation.5 | async-start | bytes 8388608
  60.4 8.2 %slice-start.2 = ((s8[14680064]{0:T(1024)(128)(4,1)}), s8[4194304]{0:T(1024)(128)(4,1)S(1)}, s32[]{:S(2)}) async-start(s8[14680064]{0:T(1024)(128)(4,1)} %bitcast.105), calls=%async_computation.6 | async-start | bytes 8388608
  60.4 9.4 %slice-start.3 = ((s8[14680064]{0:T(1024)(128)(4,1)}), s8[4194304]{0:T(1024)(128)(4,1)S(1)}, s32[]{:S(2)}) async-start(s8[14680064]{0:T(1024)(128)(4,1)} %bitcast.105), calls=%async_computation.7 | async-start | bytes 8388608
  60.4 13.9 %slice-start.4 = ((s8[14680064]{0:T(1024)(128)(4,1)}), s8[4194304]{0:T(1024)(128)(4,1)S(1)}, s32[]{:S(2)}) async-start(s8[14680064]{0:T(1024)(128)(4,1)} %bitcast.107), calls=%async_computation.8 | async-start | bytes 8388608
  60.4 13.9 %slice-start.5 = ((s8[14680064]{0:T(1024)(128)(4,1)}), s8[4194304]{0:T(1024)(128)(4,1)S(1)}, s32[]{:S(2)}) async-start(s8[14680064]{0:T(1024)(128)(4,1)} %bitcast.107), calls=%async_computation.9 | async-start | bytes 8388608
  60.4 13.9 %slice-start.6 = ((s8[14680064]{0:T(1024)(128)(4,1)}), s8[4194304]{0:T(1024)(128)(4,1)S(1)}, s32[]{:S(2)}) async-start(s8[14680064]{0:T(1024)(128)(4,1)} %bitcast.107), calls=%async_computation.10 | async-start | bytes 8388608
  69.7 5.0 %slice-start.7 = ((s8[14680064]{0:T(1024)(128)(4,1)}), s8[2097152]{0:T(1024)(128)(4,1)S(1)}, s32[]{:S(2)}) async-start(s8[14680064]{0:T(1024)(128)(4,1)} %bitcast.107), calls=%async_computation.11 | async-start | bytes 4194304
  78.1 3.8 %copy-start.1 = (bf16[1,256,256]{1,2,0:T(8,128)(2,1)S(1)}, bf16[1,256,256]{1,2,0:T(8,128)(2,1)}, u32[]{:S(2)}) copy-start(bf16[1,256,256]{1,2,0:T(8,128)(2,1)} %copy.154) | copy-start | bytes 393220
  78.1 3.8 %copy-start.5 = (pred[256,256]{0,1:T(8,128)(4,1)S(1)}, pred[256,256]{0,1:T(8,128)(4,1)}, u32[]{:S(2)}) copy-start(pred[256,256]{0,1:T(8,128)(4,1)} %iota_compare_fusion) | copy-start | bytes 196612
  78.1 61.3 %all-to-all-start.1 = ((bf16[8,16,7168]{2,1,0:T(8,128)(2,1)}), bf16[8,16,7168]{2,1,0:T(8,128)(2,1)S(1)}, u32[]{:S(2)}, u32[]{:S(2)}) async-start(bf16[8,16,7168]{2,1,0:T(8,128)(2,1)} %bitcast.10), calls=%async_computation.1 | async-start | bytes 3670016 | tf_op jit(solution)/shard_map/all_to_all | solution.py:108
  81.8 50.3 %reduce-scatter.4.cloned.1.call-start = ((), (), s32[]{:S(2)}) async-start(), calls=%async_computation.3 | async-start | bytes 147456
  83.2 1.6 %copy-start.9 = (bf16[1,256,256]{1,2,0:T(8,128)(2,1)}, bf16[1,256,256]{1,2,0:T(8,128)(2,1)S(1)}, u32[]{:S(2)}) copy-start(bf16[1,256,256]{1,2,0:T(8,128)(2,1)S(1)} %copy.156) | copy-start | bytes 393220
  84.6 0.6 copy-start.14
  85.2 11.4 %copy-start.4 = (f32[256,32]{0,1:T(8,128)S(1)}, f32[256,32]{0,1:T(8,128)}, u32[]{:S(2)}) copy-start(f32[256,32]{0,1:T(8,128)} %copy-done.3) | copy-start | bytes 98308
  87.0 48.7 %collective-permute-start = (bf16[256,256]{1,0:T(8,128)(2,1)}, bf16[256,256]{1,0:T(8,128)(2,1)S(1)}, u32[]{:S(2)}, u32[]{:S(2)}) collective-permute-start(bf16[256,256]{1,0:T(8,128)(2,1)} %copy.118), channel_id=1, source_target_pairs={{8,0},{16,8},{24,16},{9,1},{17,9},{25,17},{10,2},{18,10},{26,18},{... | collective-permute-start | bytes 393224 | tf_op jit(solution)/shard_map/ppermute | solution.py:28
  88.7 47.1 %collective-permute-start.2 = (bf16[256,256]{1,0:T(8,128)(2,1)S(1)}, bf16[256,256]{1,0:T(8,128)(2,1)S(1)}, u32[]{:S(2)}, u32[]{:S(2)}) collective-permute-start(bf16[256,256]{1,0:T(8,128)(2,1)S(1)} %copy.127), channel_id=1, source_target_pairs={{8,0},{16,8},{24,16},{9,1},{17,9},{25,17},{10,2},{18,10},{26,18},{... | collective-permute-start | bytes 393224 | tf_op jit(solution)/shard_map/ppermute | solution.py:28
  91.3 44.5 %collective-permute-start.3 = (bf16[256,256]{1,0:T(8,128)(2,1)S(1)}, bf16[256,256]{1,0:T(8,128)(2,1)S(1)}, u32[]{:S(2)}, u32[]{:S(2)}) collective-permute-start(bf16[256,256]{1,0:T(8,128)(2,1)S(1)} %copy.130), channel_id=1, source_target_pairs={{8,0},{16,8},{24,16},{9,1},{17,9},{25,17},{10,2},{18,10},{26,18},{... | collective-permute-start | bytes 393224 | tf_op jit(solution)/shard_map/ppermute | solution.py:28
  97.5 37.6 %collective-permute-start.1 = (bf16[256,128]{0,1:T(8,128)(2,1)S(1)}, bf16[256,128]{0,1:T(8,128)(2,1)S(1)}, u32[]{:S(2)}, u32[]{:S(2)}) collective-permute-start(bf16[256,128]{0,1:T(8,128)(2,1)S(1)} %convert_element_type.181), channel_id=1, source_target_pairs={{8,0},{16,8},{24,16},{9,1},{17,9},{25,17},{10,2},{18,10},{26,18},{... | collective-permute-start | bytes 196616 | tf_op jit(solution)/shard_map/ppermute | solution.py:28
  132.9 5.8 %collective-permute-start.4 = (f32[32,64]{0,1:T(8,128)S(1)}, f32[32,64]{0,1:T(8,128)S(1)}, u32[]{:S(2)}, u32[]{:S(2)}) collective-permute-start(f32[32,64]{0,1:T(8,128)S(1)} %copy.147), channel_id=1, source_target_pairs={{8,0},{16,8},{24,16},{9,1},{17,9},{25,17},{10,2},{18,10},{26,18},{... | collective-permute-start | bytes 24584 | tf_op jit(solution)/shard_map/ppermute | solution.py:28
Sparse Core Ops, SparseCore 0:
  95.6 36.4 reduce-scatter.3
where the time goes:
time: 151 us; the launch traced here: 150 us
  waiting for transfers between devices  76.5 us (51%)
  matrix products  21.6 us (14%)
  starting transfers between devices  16.5 us (11%)
  between operations  14.6 us (10%)
  local copies, waits for them, and re-layouts  13.8 us (9%)
  other arithmetic  7.22 us (5%)
    all_to_all x1, waiting for transfers between devices, mixture(): lax.all_to_all(copies, 'expert', split_axis=0, concat_axis=0, tiled=True)  40.2 us
    unnamed x2, waiting for transfers between devices  33.3 us
    dot_general x1, matrix products, expert_rows(): jnp.dot(flat_rows, gate_part, preferred_element_type=jnp.float32)  7.93 us
    unnamed x55, local copies, waits for them, and re-layouts  7.62 us
    ppermute x5, starting transfers between devices, from_behind(): return lax.ppermute(array, axis, pairs)  6.44 us
    all_to_all x1, starting transfers between devices, mixture(): lax.all_to_all(copies, 'expert', split_axis=0, concat_axis=0, tiled=True)  6.32 us
    dot_general x1, matrix products, expert_rows(): up_value = jnp.dot(flat_rows, up_part, preferred_element_type=jnp.float32)  4.49 us
    all_to_all x1, starting transfers between devices, mixture(): lax.all_to_all(partials, 'expert', split_axis=0, concat_axis=0, tiled=True)  3.72 us
  transfers between devices with their start and end apart: 8, of which 3 were waited for; matrix products, arithmetic and copies ran while one was open for 12% of the time, Pallas kernels for 0%

commit v1 on v0

v1 whole, which is shorter than its diff:
```python
import functools
import math

import jax
import jax.numpy as jnp
import numpy as np
from jax import lax
from jax.experimental import pallas as pl
from jax.experimental.pallas import tpu as pltpu
from jax.sharding import PartitionSpec as P

EXPERTS = 4
TOP = 2
NOPE = 128
ROPE = 64
VDIM = 128

yarn_factor = 40.0
yarn_base = 10000.0
yarn_initial = 4096.0
yarn_fast = 32.0
yarn_slow = 1.0
mask_fill = -1e30

IN_CHUNKS = 2
OUT_CHUNKS = 2
VMEM = 32 * 1024 * 1024


def from_behind(array, axis, by):
    size = lax.axis_size(axis)
    pairs = [(i, i + by) for i in range(size) if 0 <= i + by < size]
    return lax.ppermute(array, axis, pairs)


def swap_xor(array, offset):
    size = lax.axis_size("expert")
    return lax.ppermute(array, "expert", [(i, i ^ offset) for i in range(size)])


def correction_point(rotations, rope_width):
    return (
        rope_width
        * math.log(yarn_initial / (rotations * 2.0 * math.pi))
        / (2.0 * math.log(yarn_base))
    )


def rotary_tables(length, rope_width):
    half_width = rope_width // 2
    lowest = max(math.floor(correction_point(yarn_fast, rope_width)), 0)
    highest = min(math.ceil(correction_point(yarn_slow, rope_width)), rope_width - 1)
    spread = np.float32(max(highest - lowest, 0.001))
    unit_index = np.arange(half_width).astype(np.float32)
    extrapolated = np.float32(1.0) / np.power(
        np.float32(yarn_base), np.float32(2.0) * unit_index / np.float32(rope_width)
    ).astype(np.float32)
    interpolated = extrapolated / np.float32(yarn_factor)
    ramp_value = np.clip((unit_index - np.float32(lowest)) / spread, 0.0, 1.0).astype(np.float32)
    frequency = interpolated * ramp_value + extrapolated * (np.float32(1.0) - ramp_value)
    angles = np.arange(length).astype(np.float32)[:, None] * frequency[None, :]
    cosine = np.cos(angles.astype(np.float64)).astype(np.float32)
    sine = np.sin(angles.astype(np.float64)).astype(np.float32)
    cosine = np.repeat(cosine, 2, axis=1)
    sine = np.repeat(sine, 2, axis=1) * np.tile(np.array([-1.0, 1.0], np.float32), half_width)
    return np.tile(cosine, (1, 2)), np.tile(sine, (1, 2))


def score_scale():
    magnitude = 0.1 * math.log(yarn_factor) + 1.0
    return (NOPE + ROPE) ** (-0.5) * magnitude * magnitude


def dot(left, right, left_dim, right_dim):
    return lax.dot_general(
        left, right, (((left_dim,), (right_dim,)), ((), ())), preferred_element_type=jnp.float32
    )


def swap_pairs(value):
    lanes = value.shape[1]
    lane = lax.broadcasted_iota(jnp.int32, value.shape, 1)
    return jnp.where(lane % 2 == 0, pltpu.roll(value, lanes - 1, 1), pltpu.roll(value, 1, 1))


def attention_kernel(
    query_ref,
    rope_ref,
    key_ref,
    key_rope_ref,
    value_ref,
    upstream_ref,
    cosine_ref,
    sine_ref,
    query_out,
    rotary_out,
    key_out,
    value_out,
    shared_out,
):
    length = query_ref.shape[0]
    head_count = query_ref.shape[1] // NOPE
    scale_value = score_scale()
    cosine = cosine_ref[...]
    sine = sine_ref[...]
    key_pair = key_rope_ref[...].astype(jnp.float32)
    key_pair = jnp.concatenate([key_pair, key_pair], axis=1)
    key_turned = (key_pair * cosine + swap_pairs(key_pair) * sine).astype(jnp.bfloat16)
    row_pos = lax.broadcasted_iota(jnp.int32, (length, length), 0)
    col_pos = lax.broadcasted_iota(jnp.int32, (length, length), 1)
    seen = col_pos <= row_pos
    low_half = lax.broadcasted_iota(jnp.int32, (length, 2 * ROPE), 1) < ROPE
    shared = jnp.zeros((length, 2 * ROPE), jnp.float32)
    for pair in range(head_count // 2):
        both = slice(pair * 2 * ROPE, (pair + 1) * 2 * ROPE)
        rope = rope_ref[:, both].astype(jnp.float32)
        turned = rope * cosine + swap_pairs(rope) * sine
        rotary = jnp.zeros((length, 2 * ROPE), jnp.float32)
        for side in range(2):
            own = low_half if side == 0 else jnp.logical_not(low_half)
            head = slice((pair * 2 + side) * NOPE, (pair * 2 + side + 1) * NOPE)
            mine = jnp.where(own, turned, 0.0).astype(jnp.bfloat16)
            query = jnp.concatenate([query_ref[:, head], mine], axis=1)
            key = jnp.concatenate([key_ref[:, head], key_turned], axis=1)
            upstream = upstream_ref[:, head]
            scores = dot(query, key, 1, 1) * scale_value
            scores = jnp.where(seen, scores, mask_fill)
            row_top = jnp.max(scores, axis=1, keepdims=True)
            weights = jnp.exp(scores - row_top)
            softmaxed = weights / jnp.sum(weights, axis=1, keepdims=True)
            value_out[:, head] = dot(softmaxed.astype(jnp.bfloat16), upstream, 0, 0).astype(
                jnp.bfloat16
            )
            prob_grad = dot(upstream, value_ref[:, head], 1, 1)
            row_sum = jnp.sum(softmaxed * prob_grad, axis=1, keepdims=True)
            score_grad = (scale_value * softmaxed * (prob_grad - row_sum)).astype(jnp.bfloat16)
            by_query = dot(score_grad, key, 1, 0)
            by_key = dot(score_grad, query, 0, 0)
            query_out[:, head] = by_query[:, :NOPE].astype(jnp.bfloat16)
            key_out[:, head] = by_key[:, :NOPE].astype(jnp.bfloat16)
            rotary = jnp.where(own, by_query[:, NOPE:], rotary)
            shared = shared + by_key[:, NOPE:]
        rotary_out[:, both] = (rotary * cosine - swap_pairs(rotary) * sine).astype(jnp.bfloat16)
    shared = shared + pltpu.roll(shared, ROPE, 1)
    shared_out[...] = (shared * cosine - swap_pairs(shared) * sine)[:, :ROPE]


def attention_grads(query_nope, query_rope, key_nope, key_rope, value_heads, upstream):
    length = query_nope.shape[0]
    cosine, sine = rotary_tables(length, ROPE)
    like = jax.ShapeDtypeStruct
    return pl.pallas_call(
        attention_kernel,
        out_shape=(
            like(query_nope.shape, jnp.bfloat16),
            like(query_rope.shape, jnp.bfloat16),
            like(key_nope.shape, jnp.bfloat16),
            like(value_heads.shape, jnp.bfloat16),
            like(key_rope.shape, jnp.float32),
        ),
        compiler_params=pltpu.CompilerParams(vmem_limit_bytes=VMEM),
        cost_estimate=pl.CostEstimate(
            flops=4_000_000_000, bytes_accessed=2_000_000, transcendentals=200_000
        ),
        name="attention_grads",
    )(
        query_nope,
        query_rope,
        key_nope,
        key_rope,
        value_heads,
        upstream,
        jnp.asarray(cosine),
        jnp.asarray(sine),
    )


def tile_of(extent, most):
    return max(t for t in range(128, most + 1, 128) if extent % t == 0)


def projection_kernel(count, first, last, *refs):
    blocks = refs[:count]
    gate_ref, up_ref = refs[count : count + 2]
    rest = refs[count + 2 :]
    step = pl.program_id(0)
    if first:
        before = None
    else:
        before, rest = rest[:2], rest[2:]
    if last:
        hidden_ref, gate_sum, up_sum = rest
    else:
        gate_sum, up_sum = rest
    rows = jnp.concatenate([b[...] for b in blocks], axis=0)
    gate = jnp.dot(rows, gate_ref[...], preferred_element_type=jnp.float32)
    up = jnp.dot(rows, up_ref[...], preferred_element_type=jnp.float32)

    @pl.when(step == 0)
    def _():
        gate_sum[...] = gate if first else gate + before[0][...]
        up_sum[...] = up if first else up + before[1][...]

    @pl.when(step > 0)
    def _():
        gate_sum[...] += gate
        up_sum[...] += up

    if last:

        @pl.when(step == pl.num_programs(0) - 1)
        def _():
            value = gate_sum[...]
            hidden_ref[...] = (value / (1.0 + jnp.exp(-value)) * up_sum[...]).astype(jnp.bfloat16)


def projections(blocks, gate_part, up_part, at, before, last):
    count = len(blocks)
    block_rows, width = blocks[0].shape
    rows, hidden_width = count * block_rows, gate_part.shape[1]
    tile = tile_of(width, 896)
    begin = at // tile
    whole = pl.BlockSpec((rows, hidden_width), lambda k: (0, 0))
    weight = pl.BlockSpec((tile, hidden_width), lambda k: (begin + k, 0))
    total = jax.ShapeDtypeStruct((rows, hidden_width), jnp.float32)
    first = before is None
    return pl.pallas_call(
        functools.partial(projection_kernel, count, first, last),
        grid=(width // tile,),
        in_specs=[pl.BlockSpec((block_rows, tile), lambda k: (0, k))] * count
        + [weight, weight]
        + ([] if first else [whole, whole]),
        out_specs=whole if last else (whole, whole),
        out_shape=jax.ShapeDtypeStruct((rows, hidden_width), jnp.bfloat16)
        if last
        else (total, total),
        scratch_shapes=[pltpu.VMEM((rows, hidden_width), jnp.float32)] * 2 if last else [],
        compiler_params=pltpu.CompilerParams(vmem_limit_bytes=VMEM),
        cost_estimate=pl.CostEstimate(
            flops=4 * rows * width * hidden_width,
            bytes_accessed=4 * width * hidden_width + 2 * rows * width,
            transcendentals=0,
        ),
        name="gate_and_up",
    )(*blocks, gate_part, up_part, *([] if first else before))


def down_kernel(hidden_ref, down_ref, keep_ref, send_ref):
    out = jnp.dot(hidden_ref[...], down_ref[...], preferred_element_type=jnp.float32)
    half = keep_ref.shape[0]
    keep_ref[...] = out[:half].astype(jnp.bfloat16)
    send_ref[...] = out[half:].astype(jnp.bfloat16)


def down_columns(hidden, down_part, at, width):
    rows, depth = hidden.shape
    tile = tile_of(width, 1024)
    begin = at // tile
    half = pl.BlockSpec((rows // 2, tile), lambda j: (0, j))
    out = jax.ShapeDtypeStruct((rows // 2, width), jnp.bfloat16)
    return pl.pallas_call(
        down_kernel,
        grid=(width // tile,),
        in_specs=[
            pl.BlockSpec((rows, depth), lambda j: (0, 0)),
            pl.BlockSpec((depth, tile), lambda j: (0, begin + j)),
        ],
        out_specs=(half, half),
        out_shape=(out, out),
        compiler_params=pltpu.CompilerParams(vmem_limit_bytes=VMEM),
        cost_estimate=pl.CostEstimate(
            flops=2 * rows * depth * width,
            bytes_accessed=2 * depth * width + 2 * rows * width,
            transcendentals=0,
        ),
        name="down",
    )(hidden, down_part)


def add_kernel(parts, kept_ref, came_ref, *outs):
    total = (kept_ref[...].astype(jnp.float32) + came_ref[...].astype(jnp.float32)).astype(
        jnp.bfloat16
    )
    rows = total.shape[0] // parts
    for i in range(parts):
        outs[i][...] = total[i * rows : (i + 1) * rows]


def add_parts(kept, came, parts):
    rows, width = kept.shape
    out = jax.ShapeDtypeStruct((rows // parts, width), jnp.bfloat16)
    return pl.pallas_call(
        functools.partial(add_kernel, parts),
        out_shape=(out,) * parts,
        compiler_params=pltpu.CompilerParams(vmem_limit_bytes=VMEM),
        cost_estimate=pl.CostEstimate(
            flops=rows * width, bytes_accessed=6 * rows * width, transcendentals=0
        ),
        name="add_slices",
    )(kept, came)


def mix_kernel(chunks, weights_ref, *refs):
    out_ref = refs[-1]
    at = 0
    for c in range(chunks):
        group = refs[c * EXPERTS : (c + 1) * EXPERTS]
        width = group[0].shape[1]
        total = weights_ref[:, 0:1] * group[0][...].astype(jnp.float32)
        for k in range(1, EXPERTS):
            total = total + weights_ref[:, k : k + 1] * group[k][...].astype(jnp.float32)
        out_ref[:, at : at + width] = total.astype(jnp.bfloat16)
        at += width


def mix(weights, blocks):
    rows = weights.shape[0]
    width = sum(b[0].shape[1] for b in blocks)
    flat = [b for group in blocks for b in group]
    return pl.pallas_call(
        functools.partial(mix_kernel, len(blocks)),
        out_shape=jax.ShapeDtypeStruct((rows, width), jnp.bfloat16),
        compiler_params=pltpu.CompilerParams(vmem_limit_bytes=VMEM),
        cost_estimate=pl.CostEstimate(
            flops=8 * rows * width, bytes_accessed=10 * rows * width, transcendentals=0
        ),
        name="mix",
    )(weights, *flat)


def gathered(rows, group):
    blocks = {0: rows}
    for k in range(1, EXPERTS):
        blocks[k * group] = swap_xor(rows, k * group)
    bit = 1
    while bit < group:
        for j in sorted(blocks):
            blocks[j + bit] = swap_xor(blocks[j], bit)
        bit *= 2
    return blocks


def order_of(group):
    order = [k * group for k in range(EXPERTS)]
    bit = 1
    while bit < group:
        order = order + [j + bit for j in order]
        bit *= 2
    return order


def mixture(tokens, route_experts, route_slots, route_weights, gate_part, up_part, down_part):
    model_width = tokens.shape[1]
    group = lax.axis_size("expert") // EXPERTS
    order = order_of(group)
    step = model_width // IN_CHUNKS
    sums = None
    for c in range(IN_CHUNKS):
        blocks = gathered(tokens[:, c * step : (c + 1) * step], group)
        sums = projections(
            [blocks[j] for j in order], gate_part, up_part, c * step, sums, c == IN_CHUNKS - 1
        )
    hidden = sums
    step = model_width // OUT_CHUNKS
    mixed = []
    for c in range(OUT_CHUNKS):
        kept, sent = down_columns(hidden, down_part, c * step, step)
        bit = group // 2
        while bit > 1:
            kept = kept.astype(jnp.float32) + swap_xor(sent, bit).astype(jnp.float32)
            kept = kept.astype(jnp.bfloat16)
            kept, sent = jnp.split(kept, 2)
            bit //= 2
        parts = add_parts(kept, swap_xor(sent, 1), EXPERTS)
        mixed.append(
            [parts[0]] + [swap_xor(parts[k], k * group) for k in range(1, EXPERTS)]
        )
    mine = lax.axis_index("expert") // group
    chosen = jnp.bitwise_xor(mine, jnp.arange(EXPERTS, dtype=jnp.int32))
    weights = jnp.sum(
        jnp.where(route_experts[:, :, None] == chosen, route_weights[:, :, None], 0.0), axis=1
    )
    return mix(weights, mixed)


def per_device(
    tokens,
    route_experts,
    route_slots,
    route_weights,
    gate_weight,
    up_weight,
    down_weight,
    query_nope,
    query_rope,
    key_nope,
    key_rope,
    value_heads,
    upstream,
):
    query_here, rotary_here, key_here, value_here, shared_turn = attention_grads(
        query_nope[0], query_rope[0], key_nope[0], key_rope[0], value_heads[0], upstream[0]
    )
    shared_local = lax.psum_scatter(shared_turn, "expert", scatter_dimension=0, tiled=True)
    moved = from_behind((query_here, rotary_here, key_here, value_here), "section", -1)
    shared_grad = from_behind(shared_local, "section", -1)
    expert_mix = mixture(
        tokens[0],
        route_experts[0],
        route_slots[0],
        route_weights[0],
        gate_weight[0],
        up_weight[0],
        down_weight[0],
    )
    return (
        expert_mix[None],
        moved[0][None],
        moved[1][None],
        moved[2][None],
        moved[3][None],
        shared_grad[None],
    )


def solution(mesh):
    return jax.shard_map(
        per_device,
        mesh=mesh,
        in_specs=(
            P("section", "expert", None),
            P("section", "expert", None),
            P("section", "expert", None),
            P("section", "expert", None),
            P("section", None, "expert"),
            P("section", None, "expert"),
            P("section", "expert", None),
            P("section", None, "expert"),
            P("section", None, "expert"),
            P("section", None, "expert"),
            P("section", None, None),
            P("section", None, "expert"),
            P("section", None, "expert"),
        ),
        out_specs=(
            P("section", "expert", None),
            P("section", None, "expert"),
            P("section", None, "expert"),
            P("section", None, "expert"),
            P("section", None, "expert"),
            P("section", "expert", None),
        ),
        check_vma=False,
    )
```

time: 151 us -> 132 us (0.87)
  waiting for transfers between devices: 76.5 us -> 46.5 us
  Pallas kernels: 0 us -> 23.1 us
  matrix products: 21.6 us -> 0 us
  starting transfers between devices: 16.5 us -> 31.4 us
  other arithmetic: 7.22 us -> 0.08 us
  local copies, waits for them, and re-layouts: 13.8 us -> 15.5 us
    all_to_all x2 -> x0, waiting for transfers between devices: 40.2 us -> none  [the longest x1 40.2 us: mixture(): lax.all_to_all(copies, 'expert', split_axis=0, concat_axis=0, tiled=True)]
    unnamed x2 -> x1, waiting for transfers between devices: 33.3 us -> 0.02 us
    reduce_scatter x0 -> x1, waiting for transfers between devices: none -> 25.4 us  [per_device(): lax.psum_scatter(shared_turn, 'expert', scatter_dimension=0, tiled=True)]
    ppermute x0 -> x22, starting transfers between devices: none -> 24.9 us  [swap_xor(): return lax.ppermute(array, 'expert', [(i, i ^ offset) for i in range(size)])]
    pallas_call x0 -> x8, Pallas kernels: none -> 23.1 us  [the longest x2 12.8 us: projections(): pl.pallas_call(functools.partial(projection_kernel, count, first, last),...]
    dot_general x13 -> x0, matrix products: 21.6 us -> none  [the longest x1 7.93 us: expert_rows(): jnp.dot(flat_rows, gate_part, preferred_element_type=jnp.float32)]
    ppermute x0 -> x22, waiting for transfers between devices: none -> 19.5 us  [swap_xor(): return lax.ppermute(array, 'expert', [(i, i ^ offset) for i in range(size)])]
    all_to_all x2 -> x0, starting transfers between devices: 10 us -> none  [the longest x1 6.32 us: mixture(): lax.all_to_all(copies, 'expert', split_axis=0, concat_axis=0, tiled=True)]
  transfers between devices with their start and end apart: 8 -> 28, of which waited for: 3 -> 7; matrix products, arithmetic and copies ran while one was open for 12% -> 1% of each run, Pallas kernels for 0% -> 10%
where the time goes in v1:
time: 132 us; the launch traced here: 131 us
  waiting for transfers between devices  46.5 us (35%)
  starting transfers between devices  31.4 us (24%)
  Pallas kernels  23.1 us (18%)
  local copies, waits for them, and re-layouts  15.5 us (12%)
  between operations  14.3 us (11%)
    reduce_scatter x1, waiting for transfers between devices, per_device(): lax.psum_scatter(shared_turn, 'expert', scatter_dimension=0, tiled=True)  25.4 us
    ppermute x22, starting transfers between devices, swap_xor(): return lax.ppermute(array, 'expert', [(i, i ^ offset) for i in range(size)])  24.9 us
    ppermute x22, waiting for transfers between devices, swap_xor(): return lax.ppermute(array, 'expert', [(i, i ^ offset) for i in range(size)])  19.5 us
    unnamed x36, local copies, waits for them, and re-layouts  14.5 us
    pallas_call x2, Pallas kernels, projections(): pl.pallas_call(functools.partial(projection_kernel, count, first, last),...  12.8 us
    pallas_call x2, Pallas kernels, down_columns(): pl.pallas_call(down_kernel, grid=(width // tile,), in_specs=[pl.BlockSpec...  6.5 us
    ppermute x5, starting transfers between devices, from_behind(): return lax.ppermute(array, axis, pairs)  6.44 us
    pallas_call x1, Pallas kernels, attention_grads(): pl.pallas_call(attention_kernel, out_shape=(like(query_nope.shape, jnp.bf...  2.65 us
  transfers between devices with their start and end apart: 28, of which 7 were waited for; matrix products, arithmetic and copies ran while one was open for 1% of the time, Pallas kernels for 10%

profile of v1, /device:TPU:0, one launch (start us, length us, event | category | flops | bytes accessed | tf_op | source)
XLA Modules:
  0.0 130.9 jit_solution(16684380979953691144)
XLA Ops:
  7.2 1.0 fusion
  8.2 3.1 %collective-permute-start.7 = (bf16[16,3584]{1,0:T(8,128)(2,1)S(1)}, bf16[16,3584]{1,0:T(8,128)(2,1)S(1)}, u32[]{:S(2)}, u32[]{:S(2)}) collective-permute-start(bf16[16,3584]{1,0:T(8,128)(2,1)S(1)} %get-tuple-element.44.refs_0_), channel_id=1, source_target_pairs={{0,2},{1,3},{2,0},{3,1},{4,6},{5,7},{6,4},{7,5},{8,10},{9,11},{10,... | collective-permute-start | bytes 344072 | tf_op jit(solution)/shard_map/ppermute | solution.py:38
  11.3 2.6 %collective-permute-start.8 = (bf16[16,3584]{1,0:T(8,128)(2,1)S(1)}, bf16[16,3584]{1,0:T(8,128)(2,1)S(1)}, u32[]{:S(2)}, u32[]{:S(2)}) collective-permute-start(bf16[16,3584]{1,0:T(8,128)(2,1)S(1)} %get-tuple-element.44.refs_0_), channel_id=1, source_target_pairs={{0,4},{1,5},{2,6},{3,7},{4,0},{5,1},{6,2},{7,3},{8,12},{9,13},{10,... | collective-permute-start | bytes 344072 | tf_op jit(solution)/shard_map/ppermute | solution.py:38
  13.9 0.9 collective-permute-start
  14.8 3.5 %collective-permute-start.1 = (bf16[16,3584]{1,0:T(8,128)(2,1)S(1)}, bf16[16,3584]{1,0:T(8,128)(2,1)S(1)}, u32[]{:S(2)}, u32[]{:S(2)}) collective-permute-start(bf16[16,3584]{1,0:T(8,128)(2,1)S(1)} %get-tuple-element.45.refs_0_), channel_id=1, source_target_pairs={{0,4},{1,5},{2,6},{3,7},{4,0},{5,1},{6,2},{7,3},{8,12},{9,13},{10,... | collective-permute-start | bytes 344072 | tf_op jit(solution)/shard_map/ppermute | solution.py:38
  18.3 4.8 %collective-permute-done.8.refs_2_ = bf16[16,3584]{1,0:T(8,128)(2,1)S(1)} collective-permute-done((bf16[16,3584]{1,0:T(8,128)(2,1)S(1)}, bf16[16,3584]{1,0:T(8,128)(2,1)S(1)}, u32[]{:S(2)}, u32[]{:S(2)}) %collective-permute-start.8) | collective-permute-done | bytes 114720 | tf_op jit(solution)/shard_map/ppermute | solution.py:38
  23.2 6.0 %collective-permute-start.2 = (bf16[16,3584]{1,0:T(8,128)(2,1)S(1)}, bf16[16,3584]{1,0:T(8,128)(2,1)S(1)}, u32[]{:S(2)}, u32[]{:S(2)}) collective-permute-start(bf16[16,3584]{1,0:T(8,128)(2,1)S(1)} %get-tuple-element.45.refs_0_), channel_id=1, source_target_pairs={{0,6},{1,7},{2,4},{3,5},{4,2},{5,3},{6,0},{7,1},{8,14},{9,15},{10,... | collective-permute-start | bytes 344072 | tf_op jit(solution)/shard_map/ppermute | solution.py:38
  29.8 0.9 copy.24
  30.6 2.2 %collective-permute-done.1.refs_2_ = bf16[16,3584]{1,0:T(8,128)(2,1)S(1)} collective-permute-done((bf16[16,3584]{1,0:T(8,128)(2,1)S(1)}, bf16[16,3584]{1,0:T(8,128)(2,1)S(1)}, u32[]{:S(2)}, u32[]{:S(2)}) %collective-permute-start.1) | collective-permute-done | bytes 114720 | tf_op jit(solution)/shard_map/ppermute | solution.py:38
  33.8 5.2 %copy-done = bf16[1,7168,1024]{2,1,0:T(8,128)(2,1)S(1)} copy-done((bf16[1,7168,1024]{2,1,0:T(8,128)(2,1)S(1)}, bf16[1,7168,1024]{2,1,0:T(8,128)(2,1)}, u32[]{:S(2)}) %copy-start) | copy-done | bytes 14680088
  39.0 6.4 %gate_and_up.2 = (f32[128,1024]{1,0:T(8,128)S(1)}, f32[128,1024]{1,0:T(8,128)S(1)}) custom-call(bf16[16,3584]{1,0:T(8,128)(2,1)S(1)} %get-tuple-element.44.refs_0_, bf16[16,3584]{1,0:T(8,128)(2,1)S(1)} %collective-permute-done.7.refs_1_, bf16[16,3584]{1,0:T(8,128)(2,1)S(1)} %collective-permute-done.8.refs_2_, ...), custom_call_target="tpu_custom_call" | custom-call | flops 1879048192 | bytes 15597568 | tf_op jit(solution)/shard_map/gate_and_up/pallas_call | solution.py:227
  45.5 5.2 %copy-done.1 = bf16[1,7168,1024]{2,1,0:T(8,128)(2,1)S(1)} copy-done((bf16[1,7168,1024]{2,1,0:T(8,128)(2,1)S(1)}, bf16[1,7168,1024]{2,1,0:T(8,128)(2,1)}, u32[]{:S(2)}) %copy-start.1) | copy-done | bytes 14680088
  50.7 6.3 %gate_and_up.3.hidden_ref = bf16[128,1024]{1,0:T(8,128)(2,1)S(1)} custom-call(bf16[16,3584]{1,0:T(8,128)(2,1)S(1)} %get-tuple-element.45.refs_0_, bf16[16,3584]{1,0:T(8,128)(2,1)S(1)} %collective-permute-done.refs_1_, bf16[16,3584]{1,0:T(8,128)(2,1)S(1)} %collective-permute-done.1.refs_2_, bf16[16,3584]{1,0:T(8,128)(2,1)S(1)} %collective-permute-done.2.refs_3_, ...), custom_call_target="tpu_custom_call" | custom-call | flops 1879048192 | bytes 15597568 | tf_op jit(solution)/shard_map/gate_and_up/pallas_call | solution.py:227
  57.1 3.2 %down.3 = (bf16[64,3584]{1,0:T(8,128)(2,1)S(1)}, bf16[64,3584]{1,0:T(8,128)(2,1)}) custom-call(bf16[128,1024]{1,0:T(8,128)(2,1)S(1)} %gate_and_up.3.hidden_ref, bf16[1024,7168]{1,0:T(8,128)(2,1)S(1)} %bitcast.20), custom_call_target="tpu_custom_call" | custom-call | flops 939524096 | bytes 8257536 | tf_op jit(solution)/shard_map/down/pallas_call | solution.py:261
  60.5 3.3 %down.2 = (bf16[64,3584]{1,0:T(8,128)(2,1)S(1)}, bf16[64,3584]{1,0:T(8,128)(2,1)}) custom-call(bf16[128,1024]{1,0:T(8,128)(2,1)S(1)} %gate_and_up.3.hidden_ref, bf16[1024,7168]{1,0:T(8,128)(2,1)S(1)} %bitcast.21), custom_call_target="tpu_custom_call" | custom-call | flops 939524096 | bytes 8257536 | tf_op jit(solution)/shard_map/down/pallas_call | solution.py:261
  64.2 2.7 %attention_grads.1 = (bf16[256,256]{1,0:T(8,128)(2,1)S(1)}, bf16[256,128]{1,0:T(8,128)(2,1)S(1)}, bf16[256,256]{1,0:T(8,128)(2,1)S(1)}, bf16[256,256]{1,0:T(8,128)(2,1)S(1)}, f32[256,64]{1,0:T(8,128)}) custom-call(bf16[256,256]{1,0:T(8,128)(2,1)S(1)} %bitcast.25, bf16[256,128]{1,0:T(8,128)(2,1)S(1)} %bitcast.29, bf16[256,256]{1,0:T(8,128)(2,1)S(1)} %bitcast.26, ...), custom_call_target="tpu_custom_call" | custom-call | flops 4000000000 | bytes 2000000 | tf_op jit(solution)/shard_map/attention_grads/pallas_call | solution.py:152
  66.9 1.3 collective-permute-start.23
  68.2 1.3 collective-permute-start.22
  69.5 1.3 collective-permute-start.24
  70.8 1.3 collective-permute-start.25
  72.2 0.8 collective-permute-done.23
  73.0 1.5 %collective-permute-start.19 = (bf16[16,3584]{1,0:T(8,128)(2,1)S(1)}, bf16[16,3584]{1,0:T(8,128)(2,1)S(1)}, u32[]{:S(2)}, u32[]{:S(2)}) collective-permute-start(bf16[16,3584]{1,0:T(8,128)(2,1)S(1)} %get-tuple-element.36), channel_id=1, source_target_pairs={{0,2},{1,3},{2,0},{3,1},{4,6},{5,7},{6,4},{7,5},{8,10},{9,11},{10,... | collective-permute-start | bytes 344072 | tf_op jit(solution)/shard_map/ppermute | solution.py:38
  74.5 25.4 %reduce-scatter.2.cloned.1.call-done = f32[32,64]{1,0:T(8,128)} async-done(((f32[256,64]{1,0:T(8,128)}), f32[32,64]{1,0:T(8,128)}) %reduce-scatter.2.cloned.1.call-update) | async-done | bytes 8208 | tf_op jit(solution)/shard_map/reduce_scatter | solution.py:404
  99.9 1.3 collective-permute-start.26
  101.7 3.2 %collective-permute-start.15 = (bf16[16,3584]{1,0:T(8,128)(2,1)S(1)}, bf16[16,3584]{1,0:T(8,128)(2,1)S(1)}, u32[]{:S(2)}, u32[]{:S(2)}) collective-permute-start(bf16[16,3584]{1,0:T(8,128)(2,1)S(1)} %get-tuple-element.30), channel_id=1, source_target_pairs={{0,2},{1,3},{2,0},{3,1},{4,6},{5,7},{6,4},{7,5},{8,10},{9,11},{10,... | collective-permute-start | bytes 344072 | tf_op jit(solution)/shard_map/ppermute | solution.py:38
  104.9 0.8 collective-permute-done.26
  105.9 1.4 %collective-permute-start.17 = (bf16[16,3584]{1,0:T(8,128)(2,1)S(1)}, bf16[16,3584]{1,0:T(8,128)(2,1)S(1)}, u32[]{:S(2)}, u32[]{:S(2)}) collective-permute-start(bf16[16,3584]{1,0:T(8,128)(2,1)S(1)} %get-tuple-element.32), channel_id=1, source_target_pairs={{0,6},{1,7},{2,4},{3,5},{4,2},{5,3},{6,0},{7,1},{8,14},{9,15},{10,... | collective-permute-start | bytes 344072 | tf_op jit(solution)/shard_map/ppermute | solution.py:38
  107.5 7.6 %collective-permute-done.20.refs_6_ = bf16[16,3584]{1,0:T(8,128)(2,1)S(1)} collective-permute-done((bf16[16,3584]{1,0:T(8,128)(2,1)S(1)}, bf16[16,3584]{1,0:T(8,128)(2,1)S(1)}, u32[]{:S(2)}, u32[]{:S(2)}) %collective-permute-start.20) | collective-permute-done | bytes 114720 | tf_op jit(solution)/shard_map/ppermute | solution.py:38
  115.1 4.8 %collective-permute-done.16.refs_2_ = bf16[16,3584]{1,0:T(8,128)(2,1)S(1)} collective-permute-done((bf16[16,3584]{1,0:T(8,128)(2,1)S(1)}, bf16[16,3584]{1,0:T(8,128)(2,1)S(1)}, u32[]{:S(2)}, u32[]{:S(2)}) %collective-permute-start.16) | collective-permute-done | bytes 114720 | tf_op jit(solution)/shard_map/ppermute | solution.py:38
  120.0 0.9 mix.1
  120.9 0.7 copy.30
  122.2 0.7 copy.32
  (74 shorter events, 5.0 us)
Async XLA Ops:
  7.2 92.8 %reduce-scatter.2.cloned.1.call-start = ((), (), s32[]{:S(2)}) async-start(), calls=%async_computation.1 | async-start | bytes 147456 | tf_op jit(solution)/shard_map/reduce_scatter | solution.py:404
  8.2 6.6 %collective-permute-start.7 = (bf16[16,3584]{1,0:T(8,128)(2,1)S(1)}, bf16[16,3584]{1,0:T(8,128)(2,1)S(1)}, u32[]{:S(2)}, u32[]{:S(2)}) collective-permute-start(bf16[16,3584]{1,0:T(8,128)(2,1)S(1)} %get-tuple-element.44.refs_0_), channel_id=1, source_target_pairs={{0,2},{1,3},{2,0},{3,1},{4,6},{5,7},{6,4},{7,5},{8,10},{9,11},{10,... | collective-permute-start | bytes 344072 | tf_op jit(solution)/shard_map/ppermute | solution.py:38
  11.3 11.9 %collective-permute-start.8 = (bf16[16,3584]{1,0:T(8,128)(2,1)S(1)}, bf16[16,3584]{1,0:T(8,128)(2,1)S(1)}, u32[]{:S(2)}, u32[]{:S(2)}) collective-permute-start(bf16[16,3584]{1,0:T(8,128)(2,1)S(1)} %get-tuple-element.44.refs_0_), channel_id=1, source_target_pairs={{0,4},{1,5},{2,6},{3,7},{4,0},{5,1},{6,2},{7,3},{8,12},{9,13},{10,... | collective-permute-start | bytes 344072 | tf_op jit(solution)/shard_map/ppermute | solution.py:38
  13.9 15.3 %collective-permute-start.9 = (bf16[16,3584]{1,0:T(8,128)(2,1)S(1)}, bf16[16,3584]{1,0:T(8,128)(2,1)S(1)}, u32[]{:S(2)}, u32[]{:S(2)}) collective-permute-start(bf16[16,3584]{1,0:T(8,128)(2,1)S(1)} %get-tuple-element.44.refs_0_), channel_id=1, source_target_pairs={{0,6},{1,7},{2,4},{3,5},{4,2},{5,3},{6,0},{7,1},{8,14},{9,15},{10,... | collective-permute-start | bytes 344072 | tf_op jit(solution)/shard_map/ppermute | solution.py:38
  13.9 15.3 %collective-permute-start.10 = (bf16[16,3584]{1,0:T(8,128)(2,1)S(1)}, bf16[16,3584]{1,0:T(8,128)(2,1)S(1)}, u32[]{:S(2)}, u32[]{:S(2)}) collective-permute-start(bf16[16,3584]{1,0:T(8,128)(2,1)S(1)} %get-tuple-element.44.refs_0_), channel_id=1, source_target_pairs={{0,1},{1,0},{2,3},{3,2},{4,5},{5,4},{6,7},{7,6},{8,9},{9,8},{10,11... | collective-permute-start | bytes 344072 | tf_op jit(solution)/shard_map/ppermute | solution.py:38
  13.9 15.8 %collective-permute-start = (bf16[16,3584]{1,0:T(8,128)(2,1)S(1)}, bf16[16,3584]{1,0:T(8,128)(2,1)S(1)}, u32[]{:S(2)}, u32[]{:S(2)}) collective-permute-start(bf16[16,3584]{1,0:T(8,128)(2,1)S(1)} %get-tuple-element.45.refs_0_), channel_id=1, source_target_pairs={{0,2},{1,3},{2,0},{3,1},{4,6},{5,7},{6,4},{7,5},{8,10},{9,11},{10,... | collective-permute-start | bytes 344072 | tf_op jit(solution)/shard_map/ppermute | solution.py:38
  14.8 18.0 %collective-permute-start.1 = (bf16[16,3584]{1,0:T(8,128)(2,1)S(1)}, bf16[16,3584]{1,0:T(8,128)(2,1)S(1)}, u32[]{:S(2)}, u32[]{:S(2)}) collective-permute-start(bf16[16,3584]{1,0:T(8,128)(2,1)S(1)} %get-tuple-element.45.refs_0_), channel_id=1, source_target_pairs={{0,4},{1,5},{2,6},{3,7},{4,0},{5,1},{6,2},{7,3},{8,12},{9,13},{10,... | collective-permute-start | bytes 344072 | tf_op jit(solution)/shard_map/ppermute | solution.py:38
  23.2 9.6 %collective-permute-start.2 = (bf16[16,3584]{1,0:T(8,128)(2,1)S(1)}, bf16[16,3584]{1,0:T(8,128)(2,1)S(1)}, u32[]{:S(2)}, u32[]{:S(2)}) collective-permute-start(bf16[16,3584]{1,0:T(8,128)(2,1)S(1)} %get-tuple-element.45.refs_0_), channel_id=1, source_target_pairs={{0,6},{1,7},{2,4},{3,5},{4,2},{5,3},{6,0},{7,1},{8,14},{9,15},{10,... | collective-permute-start | bytes 344072 | tf_op jit(solution)/shard_map/ppermute | solution.py:38
  29.2 4.1 %collective-permute-start.11 = (bf16[16,3584]{1,0:T(8,128)(2,1)S(1)}, bf16[16,3584]{1,0:T(8,128)(2,1)S(1)}, u32[]{:S(2)}, u32[]{:S(2)}) collective-permute-start(bf16[16,3584]{1,0:T(8,128)(2,1)S(1)} %collective-permute-done.7.refs_1_), channel_id=1, source_target_pairs={{0,1},{1,0},{2,3},{3,2},{4,5},{5,4},{6,7},{7,6},{8,9},{9,8},{10,11... | collective-permute-start | bytes 344072 | tf_op jit(solution)/shard_map/ppermute | solution.py:38
  29.2 4.2 %collective-permute-start.12 = (bf16[16,3584]{1,0:T(8,128)(2,1)S(1)}, bf16[16,3584]{1,0:T(8,128)(2,1)S(1)}, u32[]{:S(2)}, u32[]{:S(2)}) collective-permute-start(bf16[16,3584]{1,0:T(8,128)(2,1)S(1)} %collective-permute-done.8.refs_2_), channel_id=1, source_target_pairs={{0,1},{1,0},{2,3},{3,2},{4,5},{5,4},{6,7},{7,6},{8,9},{9,8},{10,11... | collective-permute-start | bytes 344072 | tf_op jit(solution)/shard_map/ppermute | solution.py:38
  29.7 4.1 %collective-permute-start.13 = (bf16[16,3584]{1,0:T(8,128)(2,1)S(1)}, bf16[16,3584]{1,0:T(8,128)(2,1)S(1)}, u32[]{:S(2)}, u32[]{:S(2)}) collective-permute-start(bf16[16,3584]{1,0:T(8,128)(2,1)S(1)} %collective-permute-done.9.refs_3_), channel_id=1, source_target_pairs={{0,1},{1,0},{2,3},{3,2},{4,5},{5,4},{6,7},{7,6},{8,9},{9,8},{10,11... | collective-permute-start | bytes 344072 | tf_op jit(solution)/shard_map/ppermute | solution.py:38
  32.8 12.7 %collective-permute-start.3 = (bf16[16,3584]{1,0:T(8,128)(2,1)S(1)}, bf16[16,3584]{1,0:T(8,128)(2,1)S(1)}, u32[]{:S(2)}, u32[]{:S(2)}) collective-permute-start(bf16[16,3584]{1,0:T(8,128)(2,1)S(1)} %get-tuple-element.45.refs_0_), channel_id=1, source_target_pairs={{0,1},{1,0},{2,3},{3,2},{4,5},{5,4},{6,7},{7,6},{8,9},{9,8},{10,11... | collective-permute-start | bytes 344072 | tf_op jit(solution)/shard_map/ppermute | solution.py:38
  32.8 12.7 %collective-permute-start.4 = (bf16[16,3584]{1,0:T(8,128)(2,1)S(1)}, bf16[16,3584]{1,0:T(8,128)(2,1)S(1)}, u32[]{:S(2)}, u32[]{:S(2)}) collective-permute-start(bf16[16,3584]{1,0:T(8,128)(2,1)S(1)} %collective-permute-done.refs_1_), channel_id=1, source_target_pairs={{0,1},{1,0},{2,3},{3,2},{4,5},{5,4},{6,7},{7,6},{8,9},{9,8},{10,11... | collective-permute-start | bytes 344072 | tf_op jit(solution)/shard_map/ppermute | solution.py:38
  33.3 12.2 %collective-permute-start.5 = (bf16[16,3584]{1,0:T(8,128)(2,1)S(1)}, bf16[16,3584]{1,0:T(8,128)(2,1)S(1)}, u32[]{:S(2)}, u32[]{:S(2)}) collective-permute-start(bf16[16,3584]{1,0:T(8,128)(2,1)S(1)} %collective-permute-done.1.refs_2_), channel_id=1, source_target_pairs={{0,1},{1,0},{2,3},{3,2},{4,5},{5,4},{6,7},{7,6},{8,9},{9,8},{10,11... | collective-permute-start | bytes 344072 | tf_op jit(solution)/shard_map/ppermute | solution.py:38
  33.4 12.1 %collective-permute-start.6 = (bf16[16,3584]{1,0:T(8,128)(2,1)S(1)}, bf16[16,3584]{1,0:T(8,128)(2,1)S(1)}, u32[]{:S(2)}, u32[]{:S(2)}) collective-permute-start(bf16[16,3584]{1,0:T(8,128)(2,1)S(1)} %collective-permute-done.2.refs_3_), channel_id=1, source_target_pairs={{0,1},{1,0},{2,3},{3,2},{4,5},{5,4},{6,7},{7,6},{8,9},{9,8},{10,11... | collective-permute-start | bytes 344072 | tf_op jit(solution)/shard_map/ppermute | solution.py:38
  39.0 18.0 %slice-start = ((s8[14680064]{0:T(1024)(128)(4,1)}), s8[4194304]{0:T(1024)(128)(4,1)S(1)}, s32[]{:S(2)}) async-start(s8[14680064]{0:T(1024)(128)(4,1)} %bitcast.18), calls=%async_computation.2 | async-start | bytes 8388608
  39.0 18.0 %slice-start.1 = ((s8[14680064]{0:T(1024)(128)(4,1)}), s8[4194304]{0:T(1024)(128)(4,1)S(1)}, s32[]{:S(2)}) async-start(s8[14680064]{0:T(1024)(128)(4,1)} %bitcast.18), calls=%async_computation.3 | async-start | bytes 8388608
  60.4 47.0 %copy-start.9 = (f32[1,16,2]{1,2,0:T(2,128)S(1)}, f32[1,16,2]{1,2,0:T(2,128)}, u32[]{:S(2)}) copy-start(f32[1,16,2]{1,2,0:T(2,128)} %param.17) | copy-start | bytes 388
  60.4 47.0 %copy-start.10 = (s32[1,16,2]{1,2,0:T(2,128)S(1)}, s32[1,16,2]{1,2,0:T(2,128)}, u32[]{:S(2)}) copy-start(s32[1,16,2]{1,2,0:T(2,128)} %param.16) | copy-start | bytes 388
  60.4 10.4 %collective-permute-start.18 = (bf16[64,3584]{1,0:T(8,128)(2,1)}, bf16[64,3584]{1,0:T(8,128)(2,1)S(1)}, u32[]{:S(2)}, u32[]{:S(2)}) collective-permute-start(bf16[64,3584]{1,0:T(8,128)(2,1)} %get-tuple-element.34), channel_id=1, source_target_pairs={{0,1},{1,0},{2,3},{3,2},{4,5},{5,4},{6,7},{7,6},{8,9},{9,8},{10,11... | collective-permute-start | bytes 1376264 | tf_op jit(solution)/shard_map/ppermute | solution.py:38
  63.7 36.2 %collective-permute-start.14 = (bf16[64,3584]{1,0:T(8,128)(2,1)}, bf16[64,3584]{1,0:T(8,128)(2,1)S(1)}, u32[]{:S(2)}, u32[]{:S(2)}) collective-permute-start(bf16[64,3584]{1,0:T(8,128)(2,1)} %get-tuple-element.28), channel_id=1, source_target_pairs={{0,1},{1,0},{2,3},{3,2},{4,5},{5,4},{6,7},{7,6},{8,9},{9,8},{10,11... | collective-permute-start | bytes 1376264 | tf_op jit(solution)/shard_map/ppermute | solution.py:38
  66.9 6.1 %collective-permute-start.23 = (bf16[256,128]{1,0:T(8,128)(2,1)S(1)}, bf16[256,128]{1,0:T(8,128)(2,1)S(1)}, u32[]{:S(2)}, u32[]{:S(2)}) collective-permute-start(bf16[256,128]{1,0:T(8,128)(2,1)S(1)} %get-tuple-element.40), channel_id=1, source_target_pairs={{8,0},{16,8},{24,16},{9,1},{17,9},{25,17},{10,2},{18,10},{26,18},{... | collective-permute-start | bytes 196616 | tf_op jit(solution)/shard_map/ppermute | solution.py:33
  68.2 33.2 %collective-permute-start.22 = (bf16[256,256]{1,0:T(8,128)(2,1)S(1)}, bf16[256,256]{1,0:T(8,128)(2,1)S(1)}, u32[]{:S(2)}, u32[]{:S(2)}) collective-permute-start(bf16[256,256]{1,0:T(8,128)(2,1)S(1)} %get-tuple-element.39), channel_id=1, source_target_pairs={{8,0},{16,8},{24,16},{9,1},{17,9},{25,17},{10,2},{18,10},{26,18},{... | collective-permute-start | bytes 393224 | tf_op jit(solution)/shard_map/ppermute | solution.py:33
  69.5 32.0 %collective-permute-start.24 = (bf16[256,256]{1,0:T(8,128)(2,1)S(1)}, bf16[256,256]{1,0:T(8,128)(2,1)S(1)}, u32[]{:S(2)}, u32[]{:S(2)}) collective-permute-start(bf16[256,256]{1,0:T(8,128)(2,1)S(1)} %get-tuple-element.41), channel_id=1, source_target_pairs={{8,0},{16,8},{24,16},{9,1},{17,9},{25,17},{10,2},{18,10},{26,18},{... | collective-permute-start | bytes 393224 | tf_op jit(solution)/shard_map/ppermute | solution.py:33
  70.8 30.9 %collective-permute-start.25 = (bf16[256,256]{1,0:T(8,128)(2,1)S(1)}, bf16[256,256]{1,0:T(8,128)(2,1)S(1)}, u32[]{:S(2)}, u32[]{:S(2)}) collective-permute-start(bf16[256,256]{1,0:T(8,128)(2,1)S(1)} %get-tuple-element.42), channel_id=1, source_target_pairs={{8,0},{16,8},{24,16},{9,1},{17,9},{25,17},{10,2},{18,10},{26,18},{... | collective-permute-start | bytes 393224 | tf_op jit(solution)/shard_map/ppermute | solution.py:33
  73.0 32.9 %collective-permute-start.19 = (bf16[16,3584]{1,0:T(8,128)(2,1)S(1)}, bf16[16,3584]{1,0:T(8,128)(2,1)S(1)}, u32[]{:S(2)}, u32[]{:S(2)}) collective-permute-start(bf16[16,3584]{1,0:T(8,128)(2,1)S(1)} %get-tuple-element.36), channel_id=1, source_target_pairs={{0,2},{1,3},{2,0},{3,1},{4,6},{5,7},{6,4},{7,5},{8,10},{9,11},{10,... | collective-permute-start | bytes 344072 | tf_op jit(solution)/shard_map/ppermute | solution.py:38
  99.9 5.8 %collective-permute-start.26 = (f32[32,64]{1,0:T(8,128)}, f32[32,64]{1,0:T(8,128)S(1)}, u32[]{:S(2)}, u32[]{:S(2)}) collective-permute-start(f32[32,64]{1,0:T(8,128)} %reduce-scatter.2.cloned.1.call-done), channel_id=1, source_target_pairs={{8,0},{16,8},{24,16},{9,1},{17,9},{25,17},{10,2},{18,10},{26,18},{... | collective-permute-start | bytes 24584 | tf_op jit(solution)/shard_map/ppermute | solution.py:33
  101.4 13.8 %collective-permute-start.20 = (bf16[16,3584]{1,0:T(8,128)(2,1)S(1)}, bf16[16,3584]{1,0:T(8,128)(2,1)S(1)}, u32[]{:S(2)}, u32[]{:S(2)}) collective-permute-start(bf16[16,3584]{1,0:T(8,128)(2,1)S(1)} %get-tuple-element.37), channel_id=1, source_target_pairs={{0,4},{1,5},{2,6},{3,7},{4,0},{5,1},{6,2},{7,3},{8,12},{9,13},{10,... | collective-permute-start | bytes 344072 | tf_op jit(solution)/shard_map/ppermute | solution.py:38
  101.4 13.7 %collective-permute-start.21 = (bf16[16,3584]{1,0:T(8,128)(2,1)S(1)}, bf16[16,3584]{1,0:T(8,128)(2,1)S(1)}, u32[]{:S(2)}, u32[]{:S(2)}) collective-permute-start(bf16[16,3584]{1,0:T(8,128)(2,1)S(1)} %get-tuple-element.38), channel_id=1, source_target_pairs={{0,6},{1,7},{2,4},{3,5},{4,2},{5,3},{6,0},{7,1},{8,14},{9,15},{10,... | collective-permute-start | bytes 344072 | tf_op jit(solution)/shard_map/ppermute | solution.py:38
  101.7 13.5 %collective-permute-start.15 = (bf16[16,3584]{1,0:T(8,128)(2,1)S(1)}, bf16[16,3584]{1,0:T(8,128)(2,1)S(1)}, u32[]{:S(2)}, u32[]{:S(2)}) collective-permute-start(bf16[16,3584]{1,0:T(8,128)(2,1)S(1)} %get-tuple-element.30), channel_id=1, source_target_pairs={{0,2},{1,3},{2,0},{3,1},{4,6},{5,7},{6,4},{7,5},{8,10},{9,11},{10,... | collective-permute-start | bytes 344072 | tf_op jit(solution)/shard_map/ppermute | solution.py:38
  105.8 14.2 %collective-permute-start.16 = (bf16[16,3584]{1,0:T(8,128)(2,1)S(1)}, bf16[16,3584]{1,0:T(8,128)(2,1)S(1)}, u32[]{:S(2)}, u32[]{:S(2)}) collective-permute-start(bf16[16,3584]{1,0:T(8,128)(2,1)S(1)} %get-tuple-element.31), channel_id=1, source_target_pairs={{0,4},{1,5},{2,6},{3,7},{4,0},{5,1},{6,2},{7,3},{8,12},{9,13},{10,... | collective-permute-start | bytes 344072 | tf_op jit(solution)/shard_map/ppermute | solution.py:38
  105.9 14.1 %collective-permute-start.17 = (bf16[16,3584]{1,0:T(8,128)(2,1)S(1)}, bf16[16,3584]{1,0:T(8,128)(2,1)S(1)}, u32[]{:S(2)}, u32[]{:S(2)}) collective-permute-start(bf16[16,3584]{1,0:T(8,128)(2,1)S(1)} %get-tuple-element.32), channel_id=1, source_target_pairs={{0,6},{1,7},{2,4},{3,5},{4,2},{5,3},{6,0},{7,1},{8,14},{9,15},{10,... | collective-permute-start | bytes 344072 | tf_op jit(solution)/shard_map/ppermute | solution.py:38
  (11 other events, 72.6 us)
Sparse Core Ops, SparseCore 0:
  68.3 31.5 reduce-scatter.1

commit v2 on v1

v2 whole, which is shorter than its diff:
```python
import functools
import math

import jax
import jax.numpy as jnp
import numpy as np
from jax import lax
from jax.experimental import pallas as pl
from jax.experimental.pallas import tpu as pltpu
from jax.sharding import PartitionSpec as P

EXPERTS = 4
TOP = 2
NOPE = 128
ROPE = 64
VDIM = 128

yarn_factor = 40.0
yarn_base = 10000.0
yarn_initial = 4096.0
yarn_fast = 32.0
yarn_slow = 1.0
mask_fill = -1e30

OUT_SPLIT = (1, 2)
TILE = 1024
LANES = 128
VMEM = 8 * 1024 * 1024
HEAD_VMEM = 8 * 1024 * 1024
HOLD_VMEM = 11 * 1024 * 1024


def in_hbm(array):
    return pltpu.with_memory_space_constraint(array, pltpu.HBM)


def in_vmem(array):
    return pltpu.with_memory_space_constraint(array, pltpu.VMEM)


def from_behind(array, axis, by):
    size = lax.axis_size(axis)
    pairs = [(i, i + by) for i in range(size) if 0 <= i + by < size]
    return lax.ppermute(array, axis, pairs)


def swap_xor(array, offset):
    size = lax.axis_size("expert")
    return lax.ppermute(array, "expert", [(i, i ^ offset) for i in range(size)])


def correction_point(rotations, rope_width):
    return (
        rope_width
        * math.log(yarn_initial / (rotations * 2.0 * math.pi))
        / (2.0 * math.log(yarn_base))
    )


def rotary_tables(length, rope_width):
    half_width = rope_width // 2
    lowest = max(math.floor(correction_point(yarn_fast, rope_width)), 0)
    highest = min(math.ceil(correction_point(yarn_slow, rope_width)), rope_width - 1)
    spread = np.float32(max(highest - lowest, 0.001))
    unit_index = np.arange(half_width).astype(np.float32)
    extrapolated = np.float32(1.0) / np.power(
        np.float32(yarn_base), np.float32(2.0) * unit_index / np.float32(rope_width)
    ).astype(np.float32)
    interpolated = extrapolated / np.float32(yarn_factor)
    ramp_value = np.clip((unit_index - np.float32(lowest)) / spread, 0.0, 1.0).astype(np.float32)
    frequency = interpolated * ramp_value + extrapolated * (np.float32(1.0) - ramp_value)
    angles = np.arange(length).astype(np.float32)[:, None] * frequency[None, :]
    cosine = np.cos(angles.astype(np.float64)).astype(np.float32)
    sine = np.sin(angles.astype(np.float64)).astype(np.float32)
    cosine = np.repeat(cosine, 2, axis=1)
    sine = np.repeat(sine, 2, axis=1) * np.tile(np.array([-1.0, 1.0], np.float32), half_width)
    return np.tile(cosine, (1, 2)), np.tile(sine, (1, 2))


def score_scale():
    magnitude = 0.1 * math.log(yarn_factor) + 1.0
    return (NOPE + ROPE) ** (-0.5) * magnitude * magnitude


def dot(left, right, left_dim, right_dim):
    return lax.dot_general(
        left, right, (((left_dim,), (right_dim,)), ((), ())), preferred_element_type=jnp.float32
    )


def fold_of(per_dest, block_rows):
    folds = max(per_dest // block_rows, 1)
    return folds, per_dest // folds


def swap_pairs(value):
    lanes = value.shape[1]
    lane = lax.broadcasted_iota(jnp.int32, value.shape, 1)
    return jnp.where(lane % 2 == 0, pltpu.roll(value, lanes - 1, 1), pltpu.roll(value, 1, 1))


def split_moving(ref, nope, values, rope):
    widths = (nope, nope, values, rope)
    views, at = [], 0
    for width in widths:
        views.append(ref.at[:, at : at + width])
        at += width
    return views


def attention_kernel(
    query_ref,
    rope_ref,
    key_ref,
    key_rope_ref,
    value_ref,
    upstream_ref,
    cosine_ref,
    sine_ref,
    me_ref,
    down_ref,
    moving_out,
    extra_out,
    down_out,
    shared_scratch,
    down_sem,
    *,
    order,
    block_rows,
):
    fetch = pltpu.make_async_copy(down_ref.at[:, : down_out.shape[1]], down_out, down_sem)
    fetch.start()
    length = query_ref.shape[0]
    head_count = query_ref.shape[1] // NOPE
    query_out, key_out, value_out, rotary_out = split_moving(
        moving_out, query_ref.shape[1], value_ref.shape[1], rope_ref.shape[1]
    )
    scale_value = score_scale()
    cosine = cosine_ref[...]
    sine = sine_ref[...]
    key_pair = key_rope_ref[...].astype(jnp.float32)
    key_pair = jnp.concatenate([key_pair, key_pair], axis=1)
    key_turned = (key_pair * cosine + swap_pairs(key_pair) * sine).astype(jnp.bfloat16)
    row_pos = lax.broadcasted_iota(jnp.int32, (length, length), 0)
    col_pos = lax.broadcasted_iota(jnp.int32, (length, length), 1)
    seen = col_pos <= row_pos
    low_half = lax.broadcasted_iota(jnp.int32, (length, 2 * ROPE), 1) < ROPE
    shared = jnp.zeros((length, 2 * ROPE), jnp.float32)
    for pair in range(head_count // 2):
        both = slice(pair * 2 * ROPE, (pair + 1) * 2 * ROPE)
        rope = rope_ref[:, both].astype(jnp.float32)
        turned = rope * cosine + swap_pairs(rope) * sine
        rotary = jnp.zeros((length, 2 * ROPE), jnp.float32)
        for side in range(2):
            own = low_half if side == 0 else jnp.logical_not(low_half)
            head = slice((pair * 2 + side) * NOPE, (pair * 2 + side + 1) * NOPE)
            mine = jnp.where(own, turned, 0.0).astype(jnp.bfloat16)
            query = jnp.concatenate([query_ref[:, head], mine], axis=1)
            key = jnp.concatenate([key_ref[:, head], key_turned], axis=1)
            upstream = upstream_ref[:, head]
            scores = dot(query, key, 1, 1) * scale_value
            scores = jnp.where(seen, scores, mask_fill)
            row_top = jnp.max(scores, axis=1, keepdims=True)
            weights = jnp.exp(scores - row_top)
            softmaxed = weights / jnp.sum(weights, axis=1, keepdims=True)
            value_out[:, head] = dot(softmaxed.astype(jnp.bfloat16), upstream, 0, 0).astype(
                jnp.bfloat16
            )
            prob_grad = dot(upstream, value_ref[:, head], 1, 1)
            row_sum = jnp.sum(softmaxed * prob_grad, axis=1, keepdims=True)
            score_grad = (scale_value * softmaxed * (prob_grad - row_sum)).astype(jnp.bfloat16)
            by_query = dot(score_grad, key, 1, 0)
            by_key = dot(score_grad, query, 0, 0)
            query_out[:, head] = by_query[:, :NOPE].astype(jnp.bfloat16)
            key_out[:, head] = by_key[:, :NOPE].astype(jnp.bfloat16)
            rotary = jnp.where(own, by_query[:, NOPE:], rotary)
            shared = shared + by_key[:, NOPE:]
        rotary_out[:, both] = (rotary * cosine - swap_pairs(rotary) * sine).astype(jnp.bfloat16)
    shared = shared + pltpu.roll(shared, ROPE, 1)
    shared = shared * cosine - swap_pairs(shared) * sine
    high = shared.astype(jnp.bfloat16).astype(jnp.float32)
    shared_scratch[...] = jnp.where(low_half, high, shared - high)
    per_dest = length // len(order)
    folds, rows = fold_of(per_dest, block_rows)
    if rows < block_rows:
        extra_out[...] = jnp.zeros_like(extra_out)
    for place, index in enumerate(order):
        begin = (me_ref[0] ^ index) * per_dest
        for fold in range(folds):
            piece = shared_scratch[pl.ds(pl.multiple_of(begin + fold * rows, 8), rows), :]
            if rows < block_rows:
                piece = jnp.concatenate(
                    [piece, jnp.zeros((block_rows - rows, LANES), jnp.float32)], axis=0
                )
            extra_out[
                place * block_rows : (place + 1) * block_rows, fold * LANES : (fold + 1) * LANES
            ] = piece.astype(jnp.bfloat16)
    fetch.wait()


def attention_grads(
    query_nope, query_rope, key_nope, key_rope, value_heads, upstream, me, order, block_rows,
    down_part, down_width,
):
    length = query_nope.shape[0]
    cosine, sine = rotary_tables(length, ROPE)
    like = jax.ShapeDtypeStruct
    width = 2 * query_nope.shape[1] + value_heads.shape[1] + query_rope.shape[1]
    folds, _ = fold_of(length // len(order), block_rows)
    here = pl.BlockSpec(memory_space=pltpu.VMEM)
    return pl.pallas_call(
        functools.partial(attention_kernel, order=order, block_rows=block_rows),
        in_specs=[here] * 8
        + [pl.BlockSpec(memory_space=pltpu.SMEM), pl.BlockSpec(memory_space=pl.ANY)],
        out_specs=(here, here, here),
        scratch_shapes=[pltpu.VMEM((length, 2 * ROPE), jnp.float32), pltpu.SemaphoreType.DMA(())],
        out_shape=(
            like((length, width), jnp.bfloat16),
            like((len(order) * block_rows, folds * LANES), jnp.bfloat16),
            pltpu.VMEM((down_part.shape[0], down_width), down_part.dtype),
        ),
        compiler_params=pltpu.CompilerParams(vmem_limit_bytes=HEAD_VMEM),
        cost_estimate=pl.CostEstimate(
            flops=4_000_000_000, bytes_accessed=2_000_000, transcendentals=200_000
        ),
        name="attention_grads",
    )(
        in_hbm(query_nope),
        in_hbm(query_rope),
        in_hbm(key_nope),
        in_hbm(key_rope),
        in_hbm(value_heads),
        in_hbm(upstream),
        in_hbm(jnp.asarray(cosine)),
        in_hbm(jnp.asarray(sine)),
        me,
        in_hbm(down_part),
    )


def settle_kernel(moved_ref, after_ref, query_out, key_out, value_out, rotary_out):
    del after_ref
    views = split_moving(moved_ref, query_out.shape[1], value_out.shape[1], rotary_out.shape[1])
    for view, out in zip(views, (query_out, key_out, value_out, rotary_out)):
        out[...] = view[...]


def settle(moved, nope, values, rope, after):
    length = moved.shape[0]
    out = [jax.ShapeDtypeStruct((length, w), moved.dtype) for w in (nope, nope, values, rope)]
    return pl.pallas_call(
        settle_kernel,
        in_specs=[pl.BlockSpec(memory_space=pltpu.VMEM), pl.BlockSpec(memory_space=pl.ANY)],
        out_shape=tuple(out),
        compiler_params=pltpu.CompilerParams(vmem_limit_bytes=VMEM),
        cost_estimate=pl.CostEstimate(
            flops=0, bytes_accessed=4 * moved.size, transcendentals=0
        ),
        name="settle",
    )(moved, after)


def tile_of(extent, most):
    return max(t for t in range(128, most + 1, 128) if extent % t == 0)


def hold_kernel(gate_ref, up_ref, after_ref, gate_out, up_out, token_out, sems):
    del after_ref
    token_out[...] = jnp.zeros_like(token_out)
    copies = [
        pltpu.make_async_copy(gate_ref, gate_out, sems.at[0]),
        pltpu.make_async_copy(up_ref, up_out, sems.at[1]),
    ]
    for copy in copies:
        copy.start()
    for copy in copies:
        copy.wait()


def hold(gate_part, up_part, after):
    here = pl.BlockSpec(memory_space=pltpu.VMEM)
    return pl.pallas_call(
        hold_kernel,
        in_specs=[pl.BlockSpec(memory_space=pl.ANY)] * 3,
        out_specs=(here, here, here),
        out_shape=(
            pltpu.VMEM(gate_part.shape, gate_part.dtype),
            pltpu.VMEM(up_part.shape, up_part.dtype),
            jax.ShapeDtypeStruct((8, LANES), jnp.float32),
        ),
        scratch_shapes=[pltpu.SemaphoreType.DMA((2,))],
        compiler_params=pltpu.CompilerParams(vmem_limit_bytes=HOLD_VMEM),
        cost_estimate=pl.CostEstimate(
            flops=0, bytes_accessed=4 * gate_part.size, transcendentals=0
        ),
        name="hold",
    )(in_hbm(gate_part), in_hbm(up_part), after)


def experts_kernel(count, *refs):
    blocks = refs[:count]
    gate_ref, up_ref, held_ref, down_ref, extra_ref = refs[count : count + 5]
    kept_refs, sent_refs = refs[count + 6 : count + 8], refs[count + 8 : count + 10]
    gate_sum, up_sum, hidden_ref, rest_ref, sem = refs[count + 10 :]
    first = held_ref.shape[1]
    fetch = pltpu.make_async_copy(down_ref.at[:, first:], rest_ref, sem)
    fetch.start()
    width = blocks[0].shape[1]
    tile = tile_of(width, TILE)
    for i in range(width // tile):
        there = slice(i * tile, (i + 1) * tile)
        rows = jnp.concatenate([b[:, there] for b in blocks], axis=0)
        gate = jnp.dot(rows, gate_ref[there], preferred_element_type=jnp.float32)
        up = jnp.dot(rows, up_ref[there], preferred_element_type=jnp.float32)
        if i > 0:
            gate, up = gate_sum[...] + gate, up_sum[...] + up
        gate_sum[...] = gate
        up_sum[...] = up
    gate = gate_sum[...]
    hidden_ref[...] = (gate / (1.0 + jnp.exp(-gate)) * up_sum[...]).astype(jnp.bfloat16)
    half = hidden_ref.shape[0] // 2
    for part, (weights, kept, sent) in enumerate(
        zip((held_ref, rest_ref), kept_refs, sent_refs)
    ):
        if part == 1:
            fetch.wait()
        width = weights.shape[1]
        tile = tile_of(width, TILE)
        for i in range(width // tile):
            there = slice(i * tile, (i + 1) * tile)
            out = jnp.dot(hidden_ref[...], weights[:, there], preferred_element_type=jnp.float32)
            kept[:, there] = out[:half].astype(jnp.bfloat16)
            sent[:, there] = out[half:].astype(jnp.bfloat16)
        if part == 0:
            kept[:, width:] = extra_ref[:half]
            sent[:, width:] = extra_ref[half:]


def experts(blocks, gate_held, up_held, down_held, down_part, extra, after):
    count = len(blocks)
    block_rows, width = blocks[0].shape
    rows, hidden_width = count * block_rows, gate_held.shape[1]
    first = down_held.shape[1]
    rest = width - first
    here = pl.BlockSpec(memory_space=pltpu.VMEM)
    anywhere = pl.BlockSpec(memory_space=pl.ANY)
    out = [
        jax.ShapeDtypeStruct((rows // 2, w), jnp.bfloat16)
        for w in (first + extra.shape[1], rest)
    ]
    return pl.pallas_call(
        functools.partial(experts_kernel, count),
        in_specs=[here] * (count + 3) + [anywhere, here, anywhere],
        out_shape=(*out, *out),
        scratch_shapes=[
            pltpu.VMEM((rows, hidden_width), jnp.float32),
            pltpu.VMEM((rows, hidden_width), jnp.float32),
            pltpu.VMEM((rows, hidden_width), jnp.bfloat16),
            pltpu.VMEM((hidden_width, rest), jnp.bfloat16),
            pltpu.SemaphoreType.DMA(()),
        ],
        compiler_params=pltpu.CompilerParams(vmem_limit_bytes=HOLD_VMEM),
        cost_estimate=pl.CostEstimate(
            flops=6 * rows * width * hidden_width,
            bytes_accessed=2 * rest * hidden_width,
            transcendentals=0,
        ),
        name="experts",
    )(
        *blocks,
        in_vmem(gate_held),
        in_vmem(up_held),
        in_vmem(down_held),
        in_hbm(down_part),
        extra,
        extra,
    )


def both_terms(value):
    return value + pltpu.roll(value, LANES // 2, 1)


def add_kernel(parts, extra, kept_ref, came_ref, *outs):
    width = kept_ref.shape[1] - extra
    rows = kept_ref.shape[0] // parts
    for i in range(parts):
        mine = slice(i * rows, (i + 1) * rows)
        total = kept_ref[mine, :width].astype(jnp.float32) + came_ref[mine, :width].astype(
            jnp.float32
        )
        outs[i][:, :width] = total.astype(jnp.bfloat16)
        for at in range(width, width + extra, LANES):
            there = slice(at, at + LANES)
            total = both_terms(
                kept_ref[mine, there].astype(jnp.float32)
                + came_ref[mine, there].astype(jnp.float32)
            )
            high = total.astype(jnp.bfloat16).astype(jnp.float32)
            lane = lax.broadcasted_iota(jnp.int32, total.shape, 1)
            outs[i][:, there] = jnp.where(lane < LANES // 2, high, total - high).astype(
                jnp.bfloat16
            )


def add_parts(kept, came, parts, extra):
    rows, width = kept.shape
    out = jax.ShapeDtypeStruct((rows // parts, width), jnp.bfloat16)
    return pl.pallas_call(
        functools.partial(add_kernel, parts, extra),
        out_shape=(out,) * parts,
        compiler_params=pltpu.CompilerParams(vmem_limit_bytes=VMEM),
        cost_estimate=pl.CostEstimate(
            flops=rows * width, bytes_accessed=6 * rows * width, transcendentals=0
        ),
        name="add_slices",
    )(kept, came)


def mix_kernel(folds, weights_ref, *refs):
    out_ref, shared_out = refs[-2:]
    at = 0
    for c in range(len(refs) // EXPERTS):
        group = refs[c * EXPERTS : (c + 1) * EXPERTS]
        width = group[0].shape[1] - (folds * LANES if c == 0 else 0)
        total = weights_ref[:, 0:1] * group[0][:, :width].astype(jnp.float32)
        for k in range(1, EXPERTS):
            total = total + weights_ref[:, k : k + 1] * group[k][:, :width].astype(jnp.float32)
        out_ref[:, at : at + width] = total.astype(jnp.bfloat16)
        at += width
        if c == 0:
            rows = shared_out.shape[0] // folds
            for fold in range(folds):
                there = slice(width + fold * LANES, width + (fold + 1) * LANES)
                total = group[0][:, there].astype(jnp.float32)
                for k in range(1, EXPERTS):
                    total = total + group[k][:, there].astype(jnp.float32)
                shared_out[fold * rows : (fold + 1) * rows, :] = both_terms(total)[:rows, :ROPE]


def mix(weights, blocks, folds, shared_rows):
    rows = weights.shape[0]
    width = sum(b[0].shape[1] for b in blocks) - folds * LANES
    flat = [b for group in blocks for b in group]
    return pl.pallas_call(
        functools.partial(mix_kernel, folds),
        out_shape=(
            jax.ShapeDtypeStruct((rows, width), jnp.bfloat16),
            jax.ShapeDtypeStruct((shared_rows, ROPE), jnp.float32),
        ),
        compiler_params=pltpu.CompilerParams(vmem_limit_bytes=VMEM),
        cost_estimate=pl.CostEstimate(
            flops=8 * rows * width, bytes_accessed=10 * rows * width, transcendentals=0
        ),
        name="mix",
    )(weights, *flat)


def pass_kernel(*refs):
    del refs


def once(arrays, after):
    anywhere = pl.BlockSpec(memory_space=pl.ANY)
    count = len(arrays)
    return pl.pallas_call(
        pass_kernel,
        in_specs=[anywhere] * (count + 1),
        out_specs=(anywhere,) * count,
        out_shape=tuple(jax.ShapeDtypeStruct(a.shape, a.dtype) for a in arrays),
        input_output_aliases={i: i for i in range(count)},
        compiler_params=pltpu.CompilerParams(vmem_limit_bytes=1024 * 1024),
        cost_estimate=pl.CostEstimate(flops=0, bytes_accessed=0, transcendentals=0),
        name="once",
    )(*arrays, after)


def gathered(rows, group, after):
    came = once([swap_xor(rows, k * group) for k in range(1, EXPERTS)], after)
    blocks = {0: rows, **{k * group: came[k - 1] for k in range(1, EXPERTS)}}
    bit = 1
    while bit < group:
        for j in sorted(blocks):
            blocks[j + bit] = swap_xor(blocks[j], bit)
        bit *= 2
    return blocks


def order_of(group):
    order = [k * group for k in range(EXPERTS)]
    bit = 1
    while bit < group:
        order = order + [j + bit for j in order]
        bit *= 2
    return order


def returned(kept, sent, group, extra=0):
    bit = group // 2
    while bit > 1:
        (kept,) = add_parts(kept, swap_xor(sent, bit), 1, extra)
        kept, sent = jnp.split(kept, 2)
        bit //= 2
    parts = add_parts(kept, swap_xor(sent, 1), EXPERTS, extra)
    return [parts[0]] + [swap_xor(parts[k], k * group) for k in range(1, EXPERTS)]


def per_device(
    tokens,
    route_experts,
    route_slots,
    route_weights,
    gate_weight,
    up_weight,
    down_weight,
    query_nope,
    query_rope,
    key_nope,
    key_rope,
    value_heads,
    upstream,
):
    tokens, route_experts, route_weights = tokens[0], route_experts[0], route_weights[0]
    gate_part, up_part, down_part = gate_weight[0], up_weight[0], down_weight[0]
    model_width = tokens.shape[1]
    group = lax.axis_size("expert") // EXPERTS
    order = order_of(group)

    me = lax.axis_index("expert").astype(jnp.int32)
    width = model_width * OUT_SPLIT[0] // OUT_SPLIT[1]
    moving, extra, down_held = attention_grads(
        query_nope[0],
        query_rope[0],
        key_nope[0],
        key_rope[0],
        value_heads[0],
        upstream[0],
        me.reshape(1),
        order,
        tokens.shape[0],
        down_part,
        width,
    )
    moved = from_behind(moving, "section", -1)
    extra_moved = from_behind(extra, "section", -1)
    gate_held, up_held, hold_token = hold(gate_part, up_part, extra)
    blocks = gathered(tokens, group, hold_token)
    folds = extra.shape[1] // LANES
    kept, kept_rest, sent, sent_rest = experts(
        [blocks[j] for j in order], gate_held, up_held, down_held, down_part, extra_moved, moved
    )
    mixed = [
        returned(kept, sent, group, folds * LANES),
        returned(kept_rest, sent_rest, group),
    ]
    query_grad, key_grad, value_grad, rotary_grad = settle(
        moved, query_nope.shape[2], value_heads.shape[2], query_rope.shape[2], mixed[-1][0]
    )
    mine = me // group
    chosen = jnp.bitwise_xor(mine, jnp.arange(EXPERTS, dtype=jnp.int32))
    weights = jnp.sum(
        jnp.where(route_experts[:, :, None] == chosen, route_weights[:, :, None], 0.0), axis=1
    )
    expert_mix, shared_grad = mix(
        weights, mixed, folds, key_rope.shape[1] // lax.axis_size("expert")
    )
    return (
        expert_mix[None],
        query_grad[None],
        rotary_grad[None],
        key_grad[None],
        value_grad[None],
        shared_grad[None],
    )


def solution(mesh):
    return jax.shard_map(
        per_device,
        mesh=mesh,
        in_specs=(
            P("section", "expert", None),
            P("section", "expert", None),
            P("section", "expert", None),
            P("section", "expert", None),
            P("section", None, "expert"),
            P("section", None, "expert"),
            P("section", "expert", None),
            P("section", None, "expert"),
            P("section", None, "expert"),
            P("section", None, "expert"),
            P("section", None, None),
            P("section", None, "expert"),
            P("section", None, "expert"),
        ),
        out_specs=(
            P("section", "expert", None),
            P("section", None, "expert"),
            P("section", None, "expert"),
            P("section", None, "expert"),
            P("section", None, "expert"),
            P("section", "expert", None),
        ),
        check_vma=False,
    )
```

time: 132 us -> 69.8 us (0.53)
  waiting for transfers between devices: 46.5 us -> 17.1 us
  between operations: 14.3 us -> 0.78 us
  local copies, waits for them, and re-layouts: 15.5 us -> 3.4 us
  starting transfers between devices: 31.4 us -> 21.4 us
  Pallas kernels: 23.1 us -> 25.9 us
    reduce_scatter x1 -> x0, waiting for transfers between devices: 25.4 us -> none  [per_device(): lax.psum_scatter(shared_turn, 'expert', scatter_dimension=0, tiled=True)]
    ppermute x22 -> x15, waiting for transfers between devices: 19.5 us -> 7.53 us  [swap_xor(): return lax.ppermute(array, 'expert', [(i, i ^ offset) for i in range(size)])]
    unnamed x36 -> x11, local copies, waits for them, and re-layouts: 14.5 us -> 3.31 us
    ppermute x5 -> x2, waiting for transfers between devices: 1.66 us -> 9.61 us  [from_behind(): return lax.ppermute(array, axis, pairs)]
    ppermute x22 -> x15, starting transfers between devices: 24.9 us -> 18.8 us  [swap_xor(): return lax.ppermute(array, 'expert', [(i, i ^ offset) for i in range(size)])]
    ppermute x5 -> x2, starting transfers between devices: 6.44 us -> 2.56 us  [from_behind(): return lax.ppermute(array, axis, pairs)]
    pallas_call x8, Pallas kernels: 23.1 us -> 25.9 us  [the longest x1 9.41 us: hold(): pl.pallas_call(hold_kernel, in_specs=[pl.BlockSpec(memory_space=pl.ANY)]...]
  transfers between devices with their start and end apart: 28 -> 17, of which waited for: 7 -> 5; matrix products, arithmetic and copies ran while one was open for 1% -> 2% of each run, Pallas kernels for 10% -> 25%
where the time goes in v2:
time: 69.8 us; the launch traced here: 68.7 us
  Pallas kernels  25.9 us (37%)
  starting transfers between devices  21.4 us (31%)
  waiting for transfers between devices  17.1 us (24%)
  local copies, waits for them, and re-layouts  3.4 us (5%)
  between operations  0.78 us (1%)
    ppermute x15, starting transfers between devices, swap_xor(): return lax.ppermute(array, 'expert', [(i, i ^ offset) for i in range(size)])  18.8 us
    ppermute x2, waiting for transfers between devices, from_behind(): return lax.ppermute(array, axis, pairs)  9.61 us
    pallas_call x1, Pallas kernels, hold(): pl.pallas_call(hold_kernel, in_specs=[pl.BlockSpec(memory_space=pl.ANY)]...  9.41 us
    pallas_call x1, Pallas kernels, experts(): pl.pallas_call(functools.partial(experts_kernel, count), in_specs=[here]...  7.55 us
    ppermute x15, waiting for transfers between devices, swap_xor(): return lax.ppermute(array, 'expert', [(i, i ^ offset) for i in range(size)])  7.53 us
    pallas_call x1, Pallas kernels, attention_grads(): pl.pallas_call(functools.partial(attention_kernel, order=order, block_row...  6.96 us
    unnamed x11, local copies, waits for them, and re-layouts  3.31 us
    ppermute x2, starting transfers between devices, from_behind(): return lax.ppermute(array, axis, pairs)  2.56 us
  transfers between devices with their start and end apart: 17, of which 5 were waited for; matrix products, arithmetic and copies ran while one was open for 2% of the time, Pallas kernels for 25%

profile of v2, /device:TPU:0, one launch (start us, length us, event | category | flops | bytes accessed | tf_op | source)
XLA Modules:
  0.0 68.7 jit_solution(742348489425012677)
XLA Ops:
  0.6 3.1 %collective-permute-start = (bf16[16,7168]{1,0:T(8,128)(2,1)}, bf16[16,7168]{1,0:T(8,128)(2,1)S(1)}, u32[]{:S(2)}, u32[]{:S(2)}) collective-permute-start(bf16[16,7168]{1,0:T(8,128)(2,1)} %bitcast.19), channel_id=1, source_target_pairs={{0,2},{1,3},{2,0},{3,1},{4,6},{5,7},{6,4},{7,5},{8,10},{9,11},{10,... | collective-permute-start | bytes 688136 | tf_op jit(solution)/shard_map/ppermute | solution.py:49
  3.7 2.6 %collective-permute-start.1 = (bf16[16,7168]{1,0:T(8,128)(2,1)}, bf16[16,7168]{1,0:T(8,128)(2,1)}, u32[]{:S(2)}, u32[]{:S(2)}) collective-permute-start(bf16[16,7168]{1,0:T(8,128)(2,1)} %bitcast.20), channel_id=1, source_target_pairs={{0,4},{1,5},{2,6},{3,7},{4,0},{5,1},{6,2},{7,3},{8,12},{9,13},{10,... | collective-permute-start | bytes 688136 | tf_op jit(solution)/shard_map/ppermute | solution.py:49
  6.3 1.5 %copy.26 = bf16[1,256,64]{2,1,0:T(8,128)(2,1)} copy(bf16[1,256,64]{1,2,0:T(8,128)(2,1)} %param.24) | data formatting | bytes 65536 | tf_op args[10]
  7.8 7.0 %attention_grads.1 = (bf16[256,896]{1,0:T(8,128)(2,1)}, bf16[128,256]{1,0:T(8,128)(2,1)S(1)}, bf16[1024,3584]{1,0:T(8,128)(2,1)S(1)}) custom-call(bf16[256,256]{1,0:T(8,128)(2,1)} %bitcast.29, bf16[256,128]{1,0:T(8,128)(2,1)} %bitcast.33, bf16[256,256]{1,0:T(8,128)(2,1)} %bitcast.30, bf16[256,64]{1,0:T(8,128)(2,1)} %bitcast.28, bf16[256,256]{1,0:T(8,128)(2,1)} %bitcast.31, ...), custom_call_target="tpu_custom_call" | custom-call | flops 4000000000 | bytes 2000000 | tf_op jit(solution)/shard_map/attention_grads/pallas_call | solution.py:211
  14.8 0.0 copy-start.2
  14.8 9.4 %hold.1 = (bf16[7168,1024]{1,0:T(8,128)(2,1)S(1)}, bf16[7168,1024]{1,0:T(8,128)(2,1)S(1)}, f32[8,128]{1,0:T(8,128)S(1)}) custom-call(bf16[7168,1024]{1,0:T(8,128)(2,1)} %bitcast.26, bf16[7168,1024]{1,0:T(8,128)(2,1)} %bitcast.27, bf16[128,256]{1,0:T(8,128)(2,1)S(1)} %get-tuple-element.33.after_ref), custom_call_target="tpu_custom_call" | custom-call | bytes 29360128 | tf_op jit(solution)/shard_map/hold/pallas_call | solution.py:282
  24.3 0.6 collective-permute-start.4
  24.8 0.1 collective-permute-start.5
  24.9 0.4 collective-permute-start.6
  25.3 1.3 %collective-permute-start.7 = (bf16[128,256]{1,0:T(8,128)(2,1)S(1)}, bf16[128,256]{1,0:T(8,128)(2,1)S(1)}, u32[]{:S(2)}, u32[]{:S(2)}) collective-permute-start(bf16[128,256]{1,0:T(8,128)(2,1)S(1)} %get-tuple-element.33.after_ref), channel_id=1, source_target_pairs={{8,0},{16,8},{24,16},{9,1},{17,9},{25,17},{10,2},{18,10},{26,18},{... | collective-permute-start | bytes 196616 | tf_op jit(solution)/shard_map/ppermute | solution.py:44
  26.6 4.9 %collective-permute-done.7.refs_12_.refs_13_ = bf16[128,256]{1,0:T(8,128)(2,1)S(1)} collective-permute-done((bf16[128,256]{1,0:T(8,128)(2,1)S(1)}, bf16[128,256]{1,0:T(8,128)(2,1)S(1)}, u32[]{:S(2)}, u32[]{:S(2)}) %collective-permute-start.7) | collective-permute-done | bytes 65568 | tf_op jit(solution)/shard_map/ppermute | solution.py:44
  31.5 7.5 %experts.1 = (bf16[64,3840]{1,0:T(8,128)(2,1)S(1)}, bf16[64,3584]{1,0:T(8,128)(2,1)S(1)}, bf16[64,3840]{1,0:T(8,128)(2,1)}, bf16[64,3584]{1,0:T(8,128)(2,1)S(1)}) custom-call(bf16[16,7168]{1,0:T(8,128)(2,1)S(1)} %bitcast.23, bf16[16,7168]{1,0:T(8,128)(2,1)S(1)} %get-tuple-element.35.refs_1_, bf16[16,7168]{1,0:T(8,128)(2,1)} %get-tuple-element.36.refs_2_, ...), custom_call_target="tpu_custom_call" | custom-call | flops 5637144576 | bytes 7340032 | tf_op jit(solution)/shard_map/experts/pallas_call | solution.py:351
  39.1 0.8 %copy-done = bf16[64,3840]{1,0:T(8,128)(2,1)} copy-done((bf16[64,3840]{1,0:T(8,128)(2,1)}, bf16[64,3840]{1,0:T(8,128)(2,1)S(1)}, u32[]{:S(2)}) %copy-start) | copy-done | bytes 491544
  39.9 0.5 collective-permute-start.8
  40.4 1.3 %collective-permute-start.16 = (bf16[256,896]{1,0:T(8,128)(2,1)}, bf16[256,896]{1,0:T(8,128)(2,1)S(1)}, u32[]{:S(2)}, u32[]{:S(2)}) collective-permute-start(bf16[256,896]{1,0:T(8,128)(2,1)} %get-tuple-element.54), channel_id=1, source_target_pairs={{8,0},{16,8},{24,16},{9,1},{17,9},{25,17},{10,2},{18,10},{26,18},{... | collective-permute-start | bytes 1376264 | tf_op jit(solution)/shard_map/ppermute | solution.py:44
  41.7 0.6 collective-permute-done.12.came_ref
  42.3 0.1 add_slices.3
  42.4 2.9 %collective-permute-start.13 = (bf16[16,3584]{1,0:T(8,128)(2,1)S(1)}, bf16[16,3584]{1,0:T(8,128)(2,1)S(1)}, u32[]{:S(2)}, u32[]{:S(2)}) collective-permute-start(bf16[16,3584]{1,0:T(8,128)(2,1)S(1)} %get-tuple-element.50), channel_id=1, source_target_pairs={{0,2},{1,3},{2,0},{3,1},{4,6},{5,7},{6,4},{7,5},{8,10},{9,11},{10,... | collective-permute-start | bytes 344072 | tf_op jit(solution)/shard_map/ppermute | solution.py:49
  45.3 1.6 %collective-permute-start.14 = (bf16[16,3584]{1,0:T(8,128)(2,1)S(1)}, bf16[16,3584]{1,0:T(8,128)(2,1)S(1)}, u32[]{:S(2)}, u32[]{:S(2)}) collective-permute-start(bf16[16,3584]{1,0:T(8,128)(2,1)S(1)} %get-tuple-element.51), channel_id=1, source_target_pairs={{0,4},{1,5},{2,6},{3,7},{4,0},{5,1},{6,2},{7,3},{8,12},{9,13},{10,... | collective-permute-start | bytes 344072 | tf_op jit(solution)/shard_map/ppermute | solution.py:49
  46.9 0.9 %collective-permute-start.15 = (bf16[16,3584]{1,0:T(8,128)(2,1)S(1)}, bf16[16,3584]{1,0:T(8,128)(2,1)S(1)}, u32[]{:S(2)}, u32[]{:S(2)}) collective-permute-start(bf16[16,3584]{1,0:T(8,128)(2,1)S(1)} %get-tuple-element.52), channel_id=1, source_target_pairs={{0,6},{1,7},{2,4},{3,5},{4,2},{5,3},{6,0},{7,1},{8,14},{9,15},{10,... | collective-permute-start | bytes 344072 | tf_op jit(solution)/shard_map/ppermute | solution.py:49
  47.7 1.0 %copy-done.1 = bf16[64,3840]{1,0:T(8,128)(2,1)S(1)} copy-done((bf16[64,3840]{1,0:T(8,128)(2,1)S(1)}, bf16[64,3840]{1,0:T(8,128)(2,1)}, u32[]{:S(2)}) %copy-start.1) | copy-done | bytes 491544
  48.8 0.2 add_slices.2
  48.9 2.1 %collective-permute-start.10 = (bf16[16,3840]{1,0:T(8,128)(2,1)S(1)}, bf16[16,3840]{1,0:T(8,128)(2,1)S(1)}, u32[]{:S(2)}, u32[]{:S(2)}) collective-permute-start(bf16[16,3840]{1,0:T(8,128)(2,1)S(1)} %get-tuple-element.45), channel_id=1, source_target_pairs={{0,4},{1,5},{2,6},{3,7},{4,0},{5,1},{6,2},{7,3},{8,12},{9,13},{10,... | collective-permute-start | bytes 368648 | tf_op jit(solution)/shard_map/ppermute | solution.py:49
  51.0 4.7 %collective-permute-done.16.moved_ref = bf16[256,896]{1,0:T(8,128)(2,1)S(1)} collective-permute-done((bf16[256,896]{1,0:T(8,128)(2,1)}, bf16[256,896]{1,0:T(8,128)(2,1)S(1)}, u32[]{:S(2)}, u32[]{:S(2)}) %collective-permute-start.16) | collective-permute-done | bytes 458784 | tf_op jit(solution)/shard_map/ppermute | solution.py:44
  55.8 3.6 %collective-permute-start.11 = (bf16[16,3840]{1,0:T(8,128)(2,1)S(1)}, bf16[16,3840]{1,0:T(8,128)(2,1)S(1)}, u32[]{:S(2)}, u32[]{:S(2)}) collective-permute-start(bf16[16,3840]{1,0:T(8,128)(2,1)S(1)} %get-tuple-element.46), channel_id=1, source_target_pairs={{0,6},{1,7},{2,4},{3,5},{4,2},{5,3},{6,0},{7,1},{8,14},{9,15},{10,... | collective-permute-start | bytes 368648 | tf_op jit(solution)/shard_map/ppermute | solution.py:49
  59.4 0.5 collective-permute-start.9
  59.9 0.1 select_reduce_fusion
  60.0 0.1 copy.27.weights_ref
  60.1 0.8 %settle.1 = (bf16[256,256]{1,0:T(8,128)(2,1)}, bf16[256,256]{1,0:T(8,128)(2,1)}, bf16[256,256]{1,0:T(8,128)(2,1)}, bf16[256,128]{1,0:T(8,128)(2,1)}) custom-call(bf16[256,896]{1,0:T(8,128)(2,1)S(1)} %collective-permute-done.16.moved_ref, bf16[16,3584]{1,0:T(8,128)(2,1)S(1)} %get-tuple-element.49.refs_4_.after_ref), custom_call_target="tpu_custom_call" | custom-call | bytes 917504 | tf_op jit(solution)/shard_map/settle/pallas_call | solution.py:251
  60.9 6.6 %collective-permute-done.10.refs_2_ = bf16[16,3840]{1,0:T(8,128)(2,1)S(1)} collective-permute-done((bf16[16,3840]{1,0:T(8,128)(2,1)S(1)}, bf16[16,3840]{1,0:T(8,128)(2,1)S(1)}, u32[]{:S(2)}, u32[]{:S(2)}) %collective-permute-start.10) | collective-permute-done | bytes 122912 | tf_op jit(solution)/shard_map/ppermute | solution.py:49
  67.5 0.3 collective-permute-done.9.refs_1_
  67.8 0.9 %mix.1 = (bf16[16,7168]{1,0:T(8,128)(2,1)}, f32[32,64]{1,0:T(8,128)}) custom-call(f32[16,4]{1,0:T(8,128)S(1)} %copy.27.weights_ref, bf16[16,3840]{1,0:T(8,128)(2,1)S(1)} %get-tuple-element.43.refs_0_, bf16[16,3840]{1,0:T(8,128)(2,1)S(1)} %collective-permute-done.9.refs_1_, bf16[16,3840]{1,0:T(8,128)(2,1)S(1)} %collective-permute-done.10.refs_2_, ...), custom_call_target="tpu_custom_call" | custom-call | flops 917504 | bytes 1146880 | tf_op jit(solution)/shard_map/mix/pallas_call | solution.py:445
  (24 shorter events, 0.1 us)
Async XLA Ops:
  0.6 23.6 %collective-permute-start = (bf16[16,7168]{1,0:T(8,128)(2,1)}, bf16[16,7168]{1,0:T(8,128)(2,1)S(1)}, u32[]{:S(2)}, u32[]{:S(2)}) collective-permute-start(bf16[16,7168]{1,0:T(8,128)(2,1)} %bitcast.19), channel_id=1, source_target_pairs={{0,2},{1,3},{2,0},{3,1},{4,6},{5,7},{6,4},{7,5},{8,10},{9,11},{10,... | collective-permute-start | bytes 688136 | tf_op jit(solution)/shard_map/ppermute | solution.py:49
  3.7 20.5 %collective-permute-start.1 = (bf16[16,7168]{1,0:T(8,128)(2,1)}, bf16[16,7168]{1,0:T(8,128)(2,1)}, u32[]{:S(2)}, u32[]{:S(2)}) collective-permute-start(bf16[16,7168]{1,0:T(8,128)(2,1)} %bitcast.20), channel_id=1, source_target_pairs={{0,4},{1,5},{2,6},{3,7},{4,0},{5,1},{6,2},{7,3},{8,12},{9,13},{10,... | collective-permute-start | bytes 688136 | tf_op jit(solution)/shard_map/ppermute | solution.py:49
  6.3 17.9 %collective-permute-start.2 = (bf16[16,7168]{1,0:T(8,128)(2,1)}, bf16[16,7168]{1,0:T(8,128)(2,1)}, u32[]{:S(2)}, u32[]{:S(2)}) collective-permute-start(bf16[16,7168]{1,0:T(8,128)(2,1)} %bitcast.21), channel_id=1, source_target_pairs={{0,6},{1,7},{2,4},{3,5},{4,2},{5,3},{6,0},{7,1},{8,14},{9,15},{10,... | collective-permute-start | bytes 688136 | tf_op jit(solution)/shard_map/ppermute | solution.py:49
  6.3 25.2 %collective-permute-start.3 = (bf16[16,7168]{1,0:T(8,128)(2,1)}, bf16[16,7168]{1,0:T(8,128)(2,1)}, u32[]{:S(2)}, u32[]{:S(2)}) collective-permute-start(bf16[16,7168]{1,0:T(8,128)(2,1)} %bitcast.22), channel_id=1, source_target_pairs={{0,1},{1,0},{2,3},{3,2},{4,5},{5,4},{6,7},{7,6},{8,9},{9,8},{10,11... | collective-permute-start | bytes 688136 | tf_op jit(solution)/shard_map/ppermute | solution.py:49
  14.8 16.7 %copy-start.2 = (bf16[1,16,7168]{2,1,0:T(8,128)(2,1)S(1)}, bf16[1,16,7168]{2,1,0:T(8,128)(2,1)}, u32[]{:S(2)}) copy-start(bf16[1,16,7168]{2,1,0:T(8,128)(2,1)} %param.15) | copy-start | bytes 688132
  24.3 7.2 %collective-permute-start.4 = (bf16[16,7168]{1,0:T(8,128)(2,1)S(1)}, bf16[16,7168]{1,0:T(8,128)(2,1)S(1)}, u32[]{:S(2)}, u32[]{:S(2)}) collective-permute-start(bf16[16,7168]{1,0:T(8,128)(2,1)S(1)} %get-tuple-element.35.refs_1_), channel_id=1, source_target_pairs={{0,1},{1,0},{2,3},{3,2},{4,5},{5,4},{6,7},{7,6},{8,9},{9,8},{10,11... | collective-permute-start | bytes 688136 | tf_op jit(solution)/shard_map/ppermute | solution.py:49
  24.8 6.7 %collective-permute-start.5 = (bf16[16,7168]{1,0:T(8,128)(2,1)}, bf16[16,7168]{1,0:T(8,128)(2,1)S(1)}, u32[]{:S(2)}, u32[]{:S(2)}) collective-permute-start(bf16[16,7168]{1,0:T(8,128)(2,1)} %get-tuple-element.36.refs_2_), channel_id=1, source_target_pairs={{0,1},{1,0},{2,3},{3,2},{4,5},{5,4},{6,7},{7,6},{8,9},{9,8},{10,11... | collective-permute-start | bytes 688136 | tf_op jit(solution)/shard_map/ppermute | solution.py:49
  24.9 6.6 %collective-permute-start.6 = (bf16[16,7168]{1,0:T(8,128)(2,1)}, bf16[16,7168]{1,0:T(8,128)(2,1)S(1)}, u32[]{:S(2)}, u32[]{:S(2)}) collective-permute-start(bf16[16,7168]{1,0:T(8,128)(2,1)} %get-tuple-element.37.refs_3_), channel_id=1, source_target_pairs={{0,1},{1,0},{2,3},{3,2},{4,5},{5,4},{6,7},{7,6},{8,9},{9,8},{10,11... | collective-permute-start | bytes 688136 | tf_op jit(solution)/shard_map/ppermute | solution.py:49
  25.3 6.1 %collective-permute-start.7 = (bf16[128,256]{1,0:T(8,128)(2,1)S(1)}, bf16[128,256]{1,0:T(8,128)(2,1)S(1)}, u32[]{:S(2)}, u32[]{:S(2)}) collective-permute-start(bf16[128,256]{1,0:T(8,128)(2,1)S(1)} %get-tuple-element.33.after_ref), channel_id=1, source_target_pairs={{8,0},{16,8},{24,16},{9,1},{17,9},{25,17},{10,2},{18,10},{26,18},{... | collective-permute-start | bytes 196616 | tf_op jit(solution)/shard_map/ppermute | solution.py:44
  31.5 28.4 %copy-start.3 = (f32[1,16,2]{1,2,0:T(2,128)S(1)}, f32[1,16,2]{1,2,0:T(2,128)}, u32[]{:S(2)}) copy-start(f32[1,16,2]{1,2,0:T(2,128)} %param.17) | copy-start | bytes 388
  31.5 28.4 %copy-start.4 = (s32[1,16,2]{1,2,0:T(2,128)S(1)}, s32[1,16,2]{1,2,0:T(2,128)}, u32[]{:S(2)}) copy-start(s32[1,16,2]{1,2,0:T(2,128)} %param.16) | copy-start | bytes 388
  39.1 0.8 %copy-start = (bf16[64,3840]{1,0:T(8,128)(2,1)}, bf16[64,3840]{1,0:T(8,128)(2,1)S(1)}, u32[]{:S(2)}) copy-start(bf16[64,3840]{1,0:T(8,128)(2,1)S(1)} %get-tuple-element.41.kept_ref) | copy-start | bytes 1474564
  39.9 2.4 %collective-permute-start.12 = (bf16[64,3584]{1,0:T(8,128)(2,1)S(1)}, bf16[64,3584]{1,0:T(8,128)(2,1)S(1)}, u32[]{:S(2)}, u32[]{:S(2)}) collective-permute-start(bf16[64,3584]{1,0:T(8,128)(2,1)S(1)} %get-tuple-element.48), channel_id=1, source_target_pairs={{0,1},{1,0},{2,3},{3,2},{4,5},{5,4},{6,7},{7,6},{8,9},{9,8},{10,11... | collective-permute-start | bytes 1376264 | tf_op jit(solution)/shard_map/ppermute | solution.py:49
  39.9 7.9 %collective-permute-start.8 = (bf16[64,3840]{1,0:T(8,128)(2,1)}, bf16[64,3840]{1,0:T(8,128)(2,1)S(1)}, u32[]{:S(2)}, u32[]{:S(2)}) collective-permute-start(bf16[64,3840]{1,0:T(8,128)(2,1)} %get-tuple-element.42), channel_id=1, source_target_pairs={{0,1},{1,0},{2,3},{3,2},{4,5},{5,4},{6,7},{7,6},{8,9},{9,8},{10,11... | collective-permute-start | bytes 1474568 | tf_op jit(solution)/shard_map/ppermute | solution.py:49
  40.4 15.4 %collective-permute-start.16 = (bf16[256,896]{1,0:T(8,128)(2,1)}, bf16[256,896]{1,0:T(8,128)(2,1)S(1)}, u32[]{:S(2)}, u32[]{:S(2)}) collective-permute-start(bf16[256,896]{1,0:T(8,128)(2,1)} %get-tuple-element.54), channel_id=1, source_target_pairs={{8,0},{16,8},{24,16},{9,1},{17,9},{25,17},{10,2},{18,10},{26,18},{... | collective-permute-start | bytes 1376264 | tf_op jit(solution)/shard_map/ppermute | solution.py:44
  42.4 17.0 %collective-permute-start.13 = (bf16[16,3584]{1,0:T(8,128)(2,1)S(1)}, bf16[16,3584]{1,0:T(8,128)(2,1)S(1)}, u32[]{:S(2)}, u32[]{:S(2)}) collective-permute-start(bf16[16,3584]{1,0:T(8,128)(2,1)S(1)} %get-tuple-element.50), channel_id=1, source_target_pairs={{0,2},{1,3},{2,0},{3,1},{4,6},{5,7},{6,4},{7,5},{8,10},{9,11},{10,... | collective-permute-start | bytes 344072 | tf_op jit(solution)/shard_map/ppermute | solution.py:49
  45.3 15.6 %collective-permute-start.14 = (bf16[16,3584]{1,0:T(8,128)(2,1)S(1)}, bf16[16,3584]{1,0:T(8,128)(2,1)S(1)}, u32[]{:S(2)}, u32[]{:S(2)}) collective-permute-start(bf16[16,3584]{1,0:T(8,128)(2,1)S(1)} %get-tuple-element.51), channel_id=1, source_target_pairs={{0,4},{1,5},{2,6},{3,7},{4,0},{5,1},{6,2},{7,3},{8,12},{9,13},{10,... | collective-permute-start | bytes 344072 | tf_op jit(solution)/shard_map/ppermute | solution.py:49
  46.9 14.0 %collective-permute-start.15 = (bf16[16,3584]{1,0:T(8,128)(2,1)S(1)}, bf16[16,3584]{1,0:T(8,128)(2,1)S(1)}, u32[]{:S(2)}, u32[]{:S(2)}) collective-permute-start(bf16[16,3584]{1,0:T(8,128)(2,1)S(1)} %get-tuple-element.52), channel_id=1, source_target_pairs={{0,6},{1,7},{2,4},{3,5},{4,2},{5,3},{6,0},{7,1},{8,14},{9,15},{10,... | collective-permute-start | bytes 344072 | tf_op jit(solution)/shard_map/ppermute | solution.py:49
  47.7 1.0 %copy-start.1 = (bf16[64,3840]{1,0:T(8,128)(2,1)S(1)}, bf16[64,3840]{1,0:T(8,128)(2,1)}, u32[]{:S(2)}) copy-start(bf16[64,3840]{1,0:T(8,128)(2,1)} %copy-done) | copy-start | bytes 1474564
  48.9 18.5 %collective-permute-start.10 = (bf16[16,3840]{1,0:T(8,128)(2,1)S(1)}, bf16[16,3840]{1,0:T(8,128)(2,1)S(1)}, u32[]{:S(2)}, u32[]{:S(2)}) collective-permute-start(bf16[16,3840]{1,0:T(8,128)(2,1)S(1)} %get-tuple-element.45), channel_id=1, source_target_pairs={{0,4},{1,5},{2,6},{3,7},{4,0},{5,1},{6,2},{7,3},{8,12},{9,13},{10,... | collective-permute-start | bytes 368648 | tf_op jit(solution)/shard_map/ppermute | solution.py:49
  55.8 11.7 %collective-permute-start.11 = (bf16[16,3840]{1,0:T(8,128)(2,1)S(1)}, bf16[16,3840]{1,0:T(8,128)(2,1)S(1)}, u32[]{:S(2)}, u32[]{:S(2)}) collective-permute-start(bf16[16,3840]{1,0:T(8,128)(2,1)S(1)} %get-tuple-element.46), channel_id=1, source_target_pairs={{0,6},{1,7},{2,4},{3,5},{4,2},{5,3},{6,0},{7,1},{8,14},{9,15},{10,... | collective-permute-start | bytes 368648 | tf_op jit(solution)/shard_map/ppermute | solution.py:49
  59.4 8.4 %collective-permute-start.9 = (bf16[16,3840]{1,0:T(8,128)(2,1)S(1)}, bf16[16,3840]{1,0:T(8,128)(2,1)S(1)}, u32[]{:S(2)}, u32[]{:S(2)}) collective-permute-start(bf16[16,3840]{1,0:T(8,128)(2,1)S(1)} %get-tuple-element.44), channel_id=1, source_target_pairs={{0,2},{1,3},{2,0},{3,1},{4,6},{5,7},{6,4},{7,5},{8,10},{9,11},{10,... | collective-permute-start | bytes 368648 | tf_op jit(solution)/shard_map/ppermute | solution.py:49

commit v3 on v2

--- a/solution.py
+++ b/solution.py
@@ -22,12 +22,14 @@
 yarn_slow = 1.0
 mask_fill = -1e30
 
-OUT_SPLIT = (1, 2)
+SPLITS = (0, 1, 2)
 TILE = 1024
+FETCHES = 2
+DOWN_TILE = 896
+AFTER = False
 LANES = 128
 VMEM = 8 * 1024 * 1024
-HEAD_VMEM = 8 * 1024 * 1024
-HOLD_VMEM = 11 * 1024 * 1024
+HELD_VMEM = 17 * 1024 * 1024
 
 
 def in_hbm(array):
@@ -93,6 +95,14 @@
     return folds, per_dest // folds
 
 
+def extra_lanes(length, devices, folds, block_rows):
+    return -(-devices * folds * block_rows // length) * LANES
+
+
+def place_of(piece, length, block_rows):
+    return piece * block_rows % length, piece * block_rows // length * LANES
+
+
 def swap_pairs(value):
     lanes = value.shape[1]
     lane = lax.broadcasted_iota(jnp.int32, value.shape, 1)
@@ -118,18 +128,13 @@
     cosine_ref,
     sine_ref,
     me_ref,
-    down_ref,
     moving_out,
     extra_out,
-    down_out,
     shared_scratch,
-    down_sem,
     *,
     order,
     block_rows,
 ):
-    fetch = pltpu.make_async_copy(down_ref.at[:, : down_out.shape[1]], down_out, down_sem)
-    fetch.start()
     length = query_ref.shape[0]
     head_count = query_ref.shape[1] // NOPE
     query_out, key_out, value_out, rotary_out = split_moving(
@@ -138,7 +143,7 @@
     scale_value = score_scale()
     cosine = cosine_ref[...]
     sine = sine_ref[...]
-    key_pair = key_rope_ref[...].astype(jnp.float32)
+    key_pair = key_rope_ref[...].astype(jnp.float32).T
     key_pair = jnp.concatenate([key_pair, key_pair], axis=1)
     key_turned = (key_pair * cosine + swap_pairs(key_pair) * sine).astype(jnp.bfloat16)
     row_pos = lax.broadcasted_iota(jnp.int32, (length, length), 0)
@@ -182,8 +187,6 @@
     shared_scratch[...] = jnp.where(low_half, high, shared - high)
     per_dest = length // len(order)
     folds, rows = fold_of(per_dest, block_rows)
-    if rows < block_rows:
-        extra_out[...] = jnp.zeros_like(extra_out)
     for place, index in enumerate(order):
         begin = (me_ref[0] ^ index) * per_dest
         for fold in range(folds):
@@ -192,34 +195,32 @@
                 piece = jnp.concatenate(
                     [piece, jnp.zeros((block_rows - rows, LANES), jnp.float32)], axis=0
                 )
-            extra_out[
-                place * block_rows : (place + 1) * block_rows, fold * LANES : (fold + 1) * LANES
-            ] = piece.astype(jnp.bfloat16)
-    fetch.wait()
+            row, lane = place_of(place * folds + fold, length, block_rows)
+            extra_out[row : row + block_rows, lane : lane + LANES] = piece.astype(jnp.bfloat16)
 
 
 def attention_grads(
-    query_nope, query_rope, key_nope, key_rope, value_heads, upstream, me, order, block_rows,
-    down_part, down_width,
+    query_nope, query_rope, key_nope, key_rope, value_heads, upstream, me, order, block_rows
 ):
     length = query_nope.shape[0]
     cosine, sine = rotary_tables(length, ROPE)
     like = jax.ShapeDtypeStruct
+    folds, _ = fold_of(length // len(order), block_rows)
     width = 2 * query_nope.shape[1] + value_heads.shape[1] + query_rope.shape[1]
-    folds, _ = fold_of(length // len(order), block_rows)
     here = pl.BlockSpec(memory_space=pltpu.VMEM)
     return pl.pallas_call(
         functools.partial(attention_kernel, order=order, block_rows=block_rows),
         in_specs=[here] * 8
-        + [pl.BlockSpec(memory_space=pltpu.SMEM), pl.BlockSpec(memory_space=pl.ANY)],
-        out_specs=(here, here, here),
-        scratch_shapes=[pltpu.VMEM((length, 2 * ROPE), jnp.float32), pltpu.SemaphoreType.DMA(())],
+        + [pl.BlockSpec(memory_space=pltpu.SMEM)],
+        out_specs=(here, here),
+        scratch_shapes=[pltpu.VMEM((length, 2 * ROPE), jnp.float32)],
         out_shape=(
-            like((length, width), jnp.bfloat16),
-            like((len(order) * block_rows, folds * LANES), jnp.bfloat16),
-            pltpu.VMEM((down_part.shape[0], down_width), down_part.dtype),
-        ),
-        compiler_params=pltpu.CompilerParams(vmem_limit_bytes=HEAD_VMEM),
+            pltpu.HBM((length, width), jnp.bfloat16),
+            like(
+                (length, extra_lanes(length, len(order), folds, block_rows)), jnp.bfloat16
+            ),
+        ),
+        compiler_params=pltpu.CompilerParams(vmem_limit_bytes=HELD_VMEM),
         cost_estimate=pl.CostEstimate(
             flops=4_000_000_000, bytes_accessed=2_000_000, transcendentals=200_000
         ),
@@ -228,13 +229,12 @@
         in_hbm(query_nope),
         in_hbm(query_rope),
         in_hbm(key_nope),
-        in_hbm(key_rope),
+        in_hbm(key_rope.T),
         in_hbm(value_heads),
         in_hbm(upstream),
         in_hbm(jnp.asarray(cosine)),
         in_hbm(jnp.asarray(sine)),
         me,
-        in_hbm(down_part),
     )
 
 
@@ -257,7 +257,7 @@
             flops=0, bytes_accessed=4 * moved.size, transcendentals=0
         ),
         name="settle",
-    )(moved, after)
+    )(in_hbm(moved), after)
 
 
 def tile_of(extent, most):
@@ -289,7 +289,7 @@
             jax.ShapeDtypeStruct((8, LANES), jnp.float32),
         ),
         scratch_shapes=[pltpu.SemaphoreType.DMA((2,))],
-        compiler_params=pltpu.CompilerParams(vmem_limit_bytes=HOLD_VMEM),
+        compiler_params=pltpu.CompilerParams(vmem_limit_bytes=HELD_VMEM),
         cost_estimate=pl.CostEstimate(
             flops=0, bytes_accessed=4 * gate_part.size, transcendentals=0
         ),
@@ -297,16 +297,24 @@
     )(in_hbm(gate_part), in_hbm(up_part), after)
 
 
-def experts_kernel(count, *refs):
+def experts_kernel(count, folds, splits, *refs):
     blocks = refs[:count]
-    gate_ref, up_ref, held_ref, down_ref, extra_ref = refs[count : count + 5]
-    kept_refs, sent_refs = refs[count + 6 : count + 8], refs[count + 8 : count + 10]
-    gate_sum, up_sum, hidden_ref, rest_ref, sem = refs[count + 10 :]
-    first = held_ref.shape[1]
-    fetch = pltpu.make_async_copy(down_ref.at[:, first:], rest_ref, sem)
-    fetch.start()
+    gate_ref, up_ref, down_ref, extra_ref, _ = refs[count : count + 5]
+    rest = refs[count + 5 :]
+    parts = len(splits) - 1
+    kept_refs, sent_refs, rest = rest[:parts], rest[parts : 2 * parts], rest[2 * parts :]
+    gate_sum, up_sum, hidden_ref, held_ref, down_sems = rest
     width = blocks[0].shape[1]
     tile = tile_of(width, TILE)
+    share = width // FETCHES
+    fetches = []
+    for i in range(FETCHES):
+        there = slice(i * share, (i + 1) * share)
+        fetches.append(
+            pltpu.make_async_copy(down_ref.at[:, there], held_ref.at[:, there], down_sems.at[i])
+        )
+    for fetch in fetches:
+        fetch.start()
     for i in range(width // tile):
         there = slice(i * tile, (i + 1) * tile)
         rows = jnp.concatenate([b[:, there] for b in blocks], axis=0)
@@ -319,62 +327,57 @@
     gate = gate_sum[...]
     hidden_ref[...] = (gate / (1.0 + jnp.exp(-gate)) * up_sum[...]).astype(jnp.bfloat16)
     half = hidden_ref.shape[0] // 2
-    for part, (weights, kept, sent) in enumerate(
-        zip((held_ref, rest_ref), kept_refs, sent_refs)
-    ):
-        if part == 1:
-            fetch.wait()
-        width = weights.shape[1]
-        tile = tile_of(width, TILE)
-        for i in range(width // tile):
-            there = slice(i * tile, (i + 1) * tile)
-            out = jnp.dot(hidden_ref[...], weights[:, there], preferred_element_type=jnp.float32)
-            kept[:, there] = out[:half].astype(jnp.bfloat16)
-            sent[:, there] = out[half:].astype(jnp.bfloat16)
-        if part == 0:
-            kept[:, width:] = extra_ref[:half]
-            sent[:, width:] = extra_ref[half:]
-
-
-def experts(blocks, gate_held, up_held, down_held, down_part, extra, after):
+    block_rows = blocks[0].shape[0]
+    for piece in range(count * folds):
+        row, lane = place_of(piece, extra_ref.shape[0], block_rows)
+        at = piece // folds * block_rows
+        out = (kept_refs if at < half else sent_refs)[0]
+        begin = splits[1] + piece % folds * LANES
+        out[at % half : at % half + block_rows, begin : begin + LANES] = extra_ref[
+            row : row + block_rows, lane : lane + LANES
+        ]
+    part = 0
+    tile = tile_of(share, DOWN_TILE)
+    for i in range(width // tile):
+        if i * tile % share == 0:
+            fetches[i * tile // share].wait()
+        there = slice(i * tile, (i + 1) * tile)
+        out = jnp.dot(hidden_ref[...], held_ref[:, there], preferred_element_type=jnp.float32)
+        while splits[part + 1] <= i * tile:
+            part += 1
+        mine = slice(i * tile - splits[part], (i + 1) * tile - splits[part])
+        kept_refs[part][:, mine] = out[:half].astype(jnp.bfloat16)
+        sent_refs[part][:, mine] = out[half:].astype(jnp.bfloat16)
+
+
+def experts(blocks, gate_held, up_held, down_part, extra, folds, splits, after):
     count = len(blocks)
     block_rows, width = blocks[0].shape
     rows, hidden_width = count * block_rows, gate_held.shape[1]
-    first = down_held.shape[1]
-    rest = width - first
     here = pl.BlockSpec(memory_space=pltpu.VMEM)
     anywhere = pl.BlockSpec(memory_space=pl.ANY)
-    out = [
-        jax.ShapeDtypeStruct((rows // 2, w), jnp.bfloat16)
-        for w in (first + extra.shape[1], rest)
-    ]
+    widths = [end - begin for begin, end in zip(splits, splits[1:])]
+    widths[0] += folds * LANES
+    out = [jax.ShapeDtypeStruct((rows // 2, w), jnp.bfloat16) for w in widths]
     return pl.pallas_call(
-        functools.partial(experts_kernel, count),
-        in_specs=[here] * (count + 3) + [anywhere, here, anywhere],
+        functools.partial(experts_kernel, count, folds, splits),
+        in_specs=[here] * (count + 2) + [anywhere, here, anywhere],
         out_shape=(*out, *out),
         scratch_shapes=[
             pltpu.VMEM((rows, hidden_width), jnp.float32),
             pltpu.VMEM((rows, hidden_width), jnp.float32),
             pltpu.VMEM((rows, hidden_width), jnp.bfloat16),
-            pltpu.VMEM((hidden_width, rest), jnp.bfloat16),
-            pltpu.SemaphoreType.DMA(()),
+            pltpu.VMEM((hidden_width, width), jnp.bfloat16),
+            pltpu.SemaphoreType.DMA((FETCHES,)),
         ],
-        compiler_params=pltpu.CompilerParams(vmem_limit_bytes=HOLD_VMEM),
+        compiler_params=pltpu.CompilerParams(vmem_limit_bytes=HELD_VMEM),
         cost_estimate=pl.CostEstimate(
             flops=6 * rows * width * hidden_width,
-            bytes_accessed=2 * rest * hidden_width,
+            bytes_accessed=2 * width * hidden_width,
             transcendentals=0,
         ),
         name="experts",
-    )(
-        *blocks,
-        in_vmem(gate_held),
-        in_vmem(up_held),
-        in_vmem(down_held),
-        in_hbm(down_part),
-        extra,
-        extra,
-    )
+    )(*blocks, in_vmem(gate_held), in_vmem(up_held), in_hbm(down_part), extra, after)
 
 
 def both_terms(value):
@@ -382,6 +385,7 @@
 
 
 def add_kernel(parts, extra, kept_ref, came_ref, *outs):
+    outs = outs[-parts:]
     width = kept_ref.shape[1] - extra
     rows = kept_ref.shape[0] // parts
     for i in range(parts):
@@ -403,18 +407,20 @@
             )
 
 
-def add_parts(kept, came, parts, extra):
+def add_parts(kept, came, parts, extra, after=()):
     rows, width = kept.shape
     out = jax.ShapeDtypeStruct((rows // parts, width), jnp.bfloat16)
     return pl.pallas_call(
         functools.partial(add_kernel, parts, extra),
+        in_specs=[pl.BlockSpec(memory_space=pltpu.VMEM)] * 2
+        + [pl.BlockSpec(memory_space=pl.ANY)] * len(after),
         out_shape=(out,) * parts,
         compiler_params=pltpu.CompilerParams(vmem_limit_bytes=VMEM),
         cost_estimate=pl.CostEstimate(
             flops=rows * width, bytes_accessed=6 * rows * width, transcendentals=0
         ),
         name="add_slices",
-    )(kept, came)
+    )(kept, came, *after)
 
 
 def mix_kernel(folds, weights_ref, *refs):
@@ -495,13 +501,13 @@
     return order
 
 
-def returned(kept, sent, group, extra=0):
+def returned(kept, sent, group, extra=0, after=()):
     bit = group // 2
     while bit > 1:
         (kept,) = add_parts(kept, swap_xor(sent, bit), 1, extra)
         kept, sent = jnp.split(kept, 2)
         bit //= 2
-    parts = add_parts(kept, swap_xor(sent, 1), EXPERTS, extra)
+    parts = add_parts(kept, swap_xor(sent, 1), EXPERTS, extra, after)
     return [parts[0]] + [swap_xor(parts[k], k * group) for k in range(1, EXPERTS)]
 
 
@@ -527,8 +533,7 @@
     order = order_of(group)
 
     me = lax.axis_index("expert").astype(jnp.int32)
-    width = model_width * OUT_SPLIT[0] // OUT_SPLIT[1]
-    moving, extra, down_held = attention_grads(
+    moving, extra = attention_grads(
         query_nope[0],
         query_rope[0],
         key_nope[0],
@@ -538,20 +543,27 @@
         me.reshape(1),
         order,
         tokens.shape[0],
-        down_part,
-        width,
-    )
+    )
+    extra_moved = from_behind(extra, "section", -1)
     moved = from_behind(moving, "section", -1)
-    extra_moved = from_behind(extra, "section", -1)
-    gate_held, up_held, hold_token = hold(gate_part, up_part, extra)
-    blocks = gathered(tokens, group, hold_token)
-    folds = extra.shape[1] // LANES
-    kept, kept_rest, sent, sent_rest = experts(
-        [blocks[j] for j in order], gate_held, up_held, down_held, down_part, extra_moved, moved
-    )
+    gate_held, up_held, token = hold(gate_part, up_part, extra)
+    blocks = gathered(tokens, group, token)
+    shared_rows = key_rope.shape[1] // lax.axis_size("expert")
+    folds, _ = fold_of(shared_rows, tokens.shape[0])
+    splits = tuple(model_width * part // SPLITS[-1] for part in SPLITS)
+    outs = experts(
+        [blocks[j] for j in order], gate_held, up_held, down_part, extra_moved, folds, splits, in_hbm(moved)
+    )
+    parts = len(splits) - 1
     mixed = [
-        returned(kept, sent, group, folds * LANES),
-        returned(kept_rest, sent_rest, group),
+        returned(
+            outs[c],
+            outs[parts + c],
+            group,
+            folds * LANES if c == 0 else 0,
+            (in_hbm(moved),) if c == parts - 1 and AFTER else (),
+        )
+        for c in range(parts)
     ]
     query_grad, key_grad, value_grad, rotary_grad = settle(
         moved, query_nope.shape[2], value_heads.shape[2], query_rope.shape[2], mixed[-1][0]
@@ -561,9 +573,7 @@
     weights = jnp.sum(
         jnp.where(route_experts[:, :, None] == chosen, route_weights[:, :, None], 0.0), axis=1
     )
-    expert_mix, shared_grad = mix(
-        weights, mixed, folds, key_rope.shape[1] // lax.axis_size("expert")
-    )
+    expert_mix, shared_grad = mix(weights, mixed, folds, shared_rows)
     return (
         expert_mix[None],
         query_grad[None],

time: 69.8 us -> 65.5 us (0.938); the launches traced: 68.7 us -> 65.3 us
  local copies, waits for them, and re-layouts: 3.4 us -> 0.88 us
  starting transfers between devices: 21.4 us -> 19 us
  waiting for transfers between devices: 17.1 us -> 18.2 us
    ppermute x15, waiting for transfers between devices: 7.53 us -> 16.4 us  [swap_xor(): return lax.ppermute(array, 'expert', [(i, i ^ offset) for i in range(size)])]
    ppermute x2, waiting for transfers between devices: 9.61 us -> 1.87 us  [from_behind(): return lax.ppermute(array, axis, pairs)]
    pallas_call x1, Pallas kernels: 6.96 us -> 4.07 us  [attention_grads(): pl.pallas_call(functools.partial(attention_kernel, order=order, block_row...]
    unnamed x11 -> x8, local copies, waits for them, and re-layouts: 3.31 us -> 0.79 us
    ppermute x15, starting transfers between devices: 18.8 us -> 16.4 us  [swap_xor(): return lax.ppermute(array, 'expert', [(i, i ^ offset) for i in range(size)])]
    pallas_call x3, Pallas kernels: 7.82 us -> 10.2 us  [the longest x1 9.89 us: experts(): pl.pallas_call(functools.partial(experts_kernel, count, folds, splits), i...]
    pallas_call x1, Pallas kernels: 0.8 us -> 1.79 us  [settle(): pl.pallas_call(settle_kernel, in_specs=[pl.BlockSpec(memory_space=pltpu.V...]
  transfers between devices with their start and end apart: 17 -> 17, of which waited for: 5 -> 6; matrix products, arithmetic and copies ran while one was open for 2% -> 0% of each run, Pallas kernels for 25% -> 24%
where the time goes in v3:
time: 65.5 us; the launch traced here: 65.3 us
  Pallas kernels  26.4 us (40%)
  starting transfers between devices  19 us (29%)
  waiting for transfers between devices  18.2 us (28%)
  local copies, waits for them, and re-layouts  0.88 us (1%)
  between operations  0.74 us (1%)
    ppermute x15, starting transfers between devices, swap_xor(): return lax.ppermute(array, 'expert', [(i, i ^ offset) for i in range(size)])  16.4 us
    ppermute x15, waiting for transfers between devices, swap_xor(): return lax.ppermute(array, 'expert', [(i, i ^ offset) for i in range(size)])  16.4 us
    pallas_call x1, Pallas kernels, experts(): pl.pallas_call(functools.partial(experts_kernel, count, folds, splits), i...  9.89 us
    pallas_call x1, Pallas kernels, hold(): pl.pallas_call(hold_kernel, in_specs=[pl.BlockSpec(memory_space=pl.ANY)]...  9.41 us
    pallas_call x1, Pallas kernels, attention_grads(): pl.pallas_call(functools.partial(attention_kernel, order=order, block_row...  4.07 us
    ppermute x2, starting transfers between devices, from_behind(): return lax.ppermute(array, axis, pairs)  2.57 us
    ppermute x2, waiting for transfers between devices, from_behind(): return lax.ppermute(array, axis, pairs)  1.87 us
    pallas_call x1, Pallas kernels, settle(): pl.pallas_call(settle_kernel, in_specs=[pl.BlockSpec(memory_space=pltpu.V...  1.79 us
  transfers between devices with their start and end apart: 17, of which 6 were waited for; matrix products, arithmetic and copies ran while one was open for 0% of the time, Pallas kernels for 24%

profile of v3, /device:TPU:0, one launch (start us, length us, event | category | flops | bytes accessed | tf_op | source)
XLA Modules:
  0.0 65.3 jit_solution(10173311039219321543)
XLA Ops:
  0.6 3.1 %collective-permute-start = (bf16[16,7168]{1,0:T(8,128)(2,1)}, bf16[16,7168]{1,0:T(8,128)(2,1)S(1)}, u32[]{:S(2)}, u32[]{:S(2)}) collective-permute-start(bf16[16,7168]{1,0:T(8,128)(2,1)} %bitcast.21), channel_id=1, source_target_pairs={{0,2},{1,3},{2,0},{3,1},{4,6},{5,7},{6,4},{7,5},{8,10},{9,11},{10,... | collective-permute-start | bytes 688136 | tf_op jit(solution)/shard_map/ppermute | solution.py:51
  3.7 2.6 %collective-permute-start.1 = (bf16[16,7168]{1,0:T(8,128)(2,1)}, bf16[16,7168]{1,0:T(8,128)(2,1)S(1)}, u32[]{:S(2)}, u32[]{:S(2)}) collective-permute-start(bf16[16,7168]{1,0:T(8,128)(2,1)} %bitcast.22), channel_id=1, source_target_pairs={{0,4},{1,5},{2,6},{3,7},{4,0},{5,1},{6,2},{7,3},{8,12},{9,13},{10,... | collective-permute-start | bytes 688136 | tf_op jit(solution)/shard_map/ppermute | solution.py:51
  6.3 4.1 %attention_grads.1 = (bf16[256,896]{1,0:T(8,128)(2,1)}, bf16[256,128]{1,0:T(8,128)(2,1)S(1)}) custom-call(bf16[256,256]{1,0:T(8,128)(2,1)} %bitcast.32, bf16[256,128]{1,0:T(8,128)(2,1)} %bitcast.39, bf16[256,256]{1,0:T(8,128)(2,1)} %bitcast.33, bf16[64,256]{1,0:T(8,128)(2,1)} %bitcast.41, bf16[256,256]{1,0:T(8,128)(2,1)} %bitcast.34, ...), custom_call_target="tpu_custom_call" | custom-call | flops 4000000000 | bytes 2000000 | tf_op jit(solution)/shard_map/attention_grads/pallas_call | solution.py:211
  10.4 1.3 %collective-permute-start.8 = (bf16[256,896]{1,0:T(8,128)(2,1)}, bf16[256,896]{1,0:T(8,128)(2,1)S(1)}, u32[]{:S(2)}, u32[]{:S(2)}) collective-permute-start(bf16[256,896]{1,0:T(8,128)(2,1)} %get-tuple-element.39), channel_id=1, source_target_pairs={{8,0},{16,8},{24,16},{9,1},{17,9},{25,17},{10,2},{18,10},{26,18},{... | collective-permute-start | bytes 1376264 | tf_op jit(solution)/shard_map/ppermute | solution.py:46
  11.7 1.3 %collective-permute-start.7 = (bf16[256,128]{1,0:T(8,128)(2,1)S(1)}, bf16[256,128]{1,0:T(8,128)(2,1)S(1)}, u32[]{:S(2)}, u32[]{:S(2)}) collective-permute-start(bf16[256,128]{1,0:T(8,128)(2,1)S(1)} %get-tuple-element.32.after_ref), channel_id=1, source_target_pairs={{8,0},{16,8},{24,16},{9,1},{17,9},{25,17},{10,2},{18,10},{26,18},{... | collective-permute-start | bytes 196616 | tf_op jit(solution)/shard_map/ppermute | solution.py:46
  13.0 0.0 copy-start
  13.0 9.4 %hold.1 = (bf16[7168,1024]{1,0:T(8,128)(2,1)S(1)}, bf16[7168,1024]{1,0:T(8,128)(2,1)S(1)}, f32[8,128]{1,0:T(8,128)S(1)}) custom-call(bf16[7168,1024]{1,0:T(8,128)(2,1)} %bitcast.26, bf16[7168,1024]{1,0:T(8,128)(2,1)} %bitcast.27, bf16[256,128]{1,0:T(8,128)(2,1)S(1)} %get-tuple-element.32.after_ref), custom_call_target="tpu_custom_call" | custom-call | bytes 29360128 | tf_op jit(solution)/shard_map/hold/pallas_call | solution.py:282
  22.4 0.1 collective-permute-start.3
  22.5 0.7 %collective-permute-done.1.refs_1_ = bf16[16,7168]{1,0:T(8,128)(2,1)S(1)} collective-permute-done((bf16[16,7168]{1,0:T(8,128)(2,1)}, bf16[16,7168]{1,0:T(8,128)(2,1)S(1)}, u32[]{:S(2)}, u32[]{:S(2)}) %collective-permute-start.1) | collective-permute-done | bytes 229408 | tf_op jit(solution)/shard_map/ppermute | solution.py:51
  23.2 0.0 collective-permute-done.2.refs_2_
  23.2 0.5 collective-permute-start.5
  23.7 1.9 %collective-permute-done.7.refs_11_ = bf16[256,128]{1,0:T(8,128)(2,1)S(1)} collective-permute-done((bf16[256,128]{1,0:T(8,128)(2,1)S(1)}, bf16[256,128]{1,0:T(8,128)(2,1)S(1)}, u32[]{:S(2)}, u32[]{:S(2)}) %collective-permute-start.7) | collective-permute-done | bytes 65568 | tf_op jit(solution)/shard_map/ppermute | solution.py:46
  25.6 1.5 %collective-permute-done.6.refs_7_ = bf16[16,7168]{1,0:T(8,128)(2,1)S(1)} collective-permute-done((bf16[16,7168]{1,0:T(8,128)(2,1)S(1)}, bf16[16,7168]{1,0:T(8,128)(2,1)S(1)}, u32[]{:S(2)}, u32[]{:S(2)}) %collective-permute-start.6) | collective-permute-done | bytes 229408 | tf_op jit(solution)/shard_map/ppermute | solution.py:51
  27.1 0.8 %copy-done.1 = bf16[256,896]{1,0:T(8,128)(2,1)} copy-done((bf16[256,896]{1,0:T(8,128)(2,1)}, bf16[256,896]{1,0:T(8,128)(2,1)S(1)}, u32[]{:S(2)}) %copy-start.1) | copy-done | bytes 458776
  27.9 9.9 %experts.1 = (bf16[64,3840]{1,0:T(8,128)(2,1)S(1)}, bf16[64,3584]{1,0:T(8,128)(2,1)S(1)}, bf16[64,3840]{1,0:T(8,128)(2,1)}, bf16[64,3584]{1,0:T(8,128)(2,1)S(1)}) custom-call(bf16[16,7168]{1,0:T(8,128)(2,1)S(1)} %bitcast.25, bf16[16,7168]{1,0:T(8,128)(2,1)S(1)} %get-tuple-element.34.refs_1_, bf16[16,7168]{1,0:T(8,128)(2,1)S(1)} %get-tuple-element.35.refs_2_, ...), custom_call_target="tpu_custom_call" | custom-call | flops 5637144576 | bytes 14680064 | tf_op jit(solution)/shard_map/experts/pallas_call | solution.py:362
  37.8 0.2 collective-permute-start.13
  38.0 0.4 collective-permute-start.9
  38.3 1.3 %collective-permute-done.13.came_ref = bf16[64,3584]{1,0:T(8,128)(2,1)S(1)} collective-permute-done((bf16[64,3584]{1,0:T(8,128)(2,1)S(1)}, bf16[64,3584]{1,0:T(8,128)(2,1)S(1)}, u32[]{:S(2)}, u32[]{:S(2)}) %collective-permute-start.13) | collective-permute-done | bytes 458784 | tf_op jit(solution)/shard_map/ppermute | solution.py:51
  39.6 0.1 add_slices.3
  39.7 2.4 %collective-permute-start.14 = (bf16[16,3584]{1,0:T(8,128)(2,1)S(1)}, bf16[16,3584]{1,0:T(8,128)(2,1)S(1)}, u32[]{:S(2)}, u32[]{:S(2)}) collective-permute-start(bf16[16,3584]{1,0:T(8,128)(2,1)S(1)} %get-tuple-element.49), channel_id=1, source_target_pairs={{0,2},{1,3},{2,0},{3,1},{4,6},{5,7},{6,4},{7,5},{8,10},{9,11},{10,... | collective-permute-start | bytes 344072 | tf_op jit(solution)/shard_map/ppermute | solution.py:51
  42.2 1.8 %collective-permute-start.15 = (bf16[16,3584]{1,0:T(8,128)(2,1)S(1)}, bf16[16,3584]{1,0:T(8,128)(2,1)S(1)}, u32[]{:S(2)}, u32[]{:S(2)}) collective-permute-start(bf16[16,3584]{1,0:T(8,128)(2,1)S(1)} %get-tuple-element.50), channel_id=1, source_target_pairs={{0,4},{1,5},{2,6},{3,7},{4,0},{5,1},{6,2},{7,3},{8,12},{9,13},{10,... | collective-permute-start | bytes 344072 | tf_op jit(solution)/shard_map/ppermute | solution.py:51
  43.9 0.7 %collective-permute-start.16 = (bf16[16,3584]{1,0:T(8,128)(2,1)S(1)}, bf16[16,3584]{1,0:T(8,128)(2,1)S(1)}, u32[]{:S(2)}, u32[]{:S(2)}) collective-permute-start(bf16[16,3584]{1,0:T(8,128)(2,1)S(1)} %get-tuple-element.51), channel_id=1, source_target_pairs={{0,6},{1,7},{2,4},{3,5},{4,2},{5,3},{6,0},{7,1},{8,14},{9,15},{10,... | collective-permute-start | bytes 344072 | tf_op jit(solution)/shard_map/ppermute | solution.py:51
  44.6 0.2 add_slices.2
  44.8 1.1 %collective-permute-start.10 = (bf16[16,3840]{1,0:T(8,128)(2,1)S(1)}, bf16[16,3840]{1,0:T(8,128)(2,1)S(1)}, u32[]{:S(2)}, u32[]{:S(2)}) collective-permute-start(bf16[16,3840]{1,0:T(8,128)(2,1)S(1)} %get-tuple-element.43), channel_id=1, source_target_pairs={{0,2},{1,3},{2,0},{3,1},{4,6},{5,7},{6,4},{7,5},{8,10},{9,11},{10,... | collective-permute-start | bytes 368648 | tf_op jit(solution)/shard_map/ppermute | solution.py:51
  45.9 2.7 %collective-permute-start.11 = (bf16[16,3840]{1,0:T(8,128)(2,1)S(1)}, bf16[16,3840]{1,0:T(8,128)(2,1)S(1)}, u32[]{:S(2)}, u32[]{:S(2)}) collective-permute-start(bf16[16,3840]{1,0:T(8,128)(2,1)S(1)} %get-tuple-element.44), channel_id=1, source_target_pairs={{0,4},{1,5},{2,6},{3,7},{4,0},{5,1},{6,2},{7,3},{8,12},{9,13},{10,... | collective-permute-start | bytes 368648 | tf_op jit(solution)/shard_map/ppermute | solution.py:51
  48.6 1.0 %collective-permute-start.12 = (bf16[16,3840]{1,0:T(8,128)(2,1)S(1)}, bf16[16,3840]{1,0:T(8,128)(2,1)S(1)}, u32[]{:S(2)}, u32[]{:S(2)}) collective-permute-start(bf16[16,3840]{1,0:T(8,128)(2,1)S(1)} %get-tuple-element.45), channel_id=1, source_target_pairs={{0,6},{1,7},{2,4},{3,5},{4,2},{5,3},{6,0},{7,1},{8,14},{9,15},{10,... | collective-permute-start | bytes 368648 | tf_op jit(solution)/shard_map/ppermute | solution.py:51
  49.5 0.1 select_reduce_fusion
  49.6 0.1 copy.25.weights_ref
  49.7 1.8 %settle.1 = (bf16[256,256]{1,0:T(8,128)(2,1)}, bf16[256,256]{1,0:T(8,128)(2,1)}, bf16[256,256]{1,0:T(8,128)(2,1)}, bf16[256,128]{1,0:T(8,128)(2,1)}) custom-call(bf16[256,896]{1,0:T(8,128)(2,1)} %copy-done.1, bf16[16,3584]{1,0:T(8,128)(2,1)S(1)} %get-tuple-element.48.refs_4_.after_ref), custom_call_target="tpu_custom_call" | custom-call | bytes 917504 | tf_op jit(solution)/shard_map/settle/pallas_call | solution.py:251
  51.5 2.5 %collective-permute-done.15.refs_6_ = bf16[16,3584]{1,0:T(8,128)(2,1)S(1)} collective-permute-done((bf16[16,3584]{1,0:T(8,128)(2,1)S(1)}, bf16[16,3584]{1,0:T(8,128)(2,1)S(1)}, u32[]{:S(2)}, u32[]{:S(2)}) %collective-permute-start.15) | collective-permute-done | bytes 114720 | tf_op jit(solution)/shard_map/ppermute | solution.py:51
  54.0 10.4 %collective-permute-done.11.refs_2_ = bf16[16,3840]{1,0:T(8,128)(2,1)S(1)} collective-permute-done((bf16[16,3840]{1,0:T(8,128)(2,1)S(1)}, bf16[16,3840]{1,0:T(8,128)(2,1)S(1)}, u32[]{:S(2)}, u32[]{:S(2)}) %collective-permute-start.11) | collective-permute-done | bytes 122912 | tf_op jit(solution)/shard_map/ppermute | solution.py:51
  64.4 0.9 %mix.1 = (bf16[16,7168]{1,0:T(8,128)(2,1)}, f32[32,64]{1,0:T(8,128)}) custom-call(f32[16,4]{1,0:T(8,128)S(1)} %copy.25.weights_ref, bf16[16,3840]{1,0:T(8,128)(2,1)S(1)} %get-tuple-element.42.refs_0_, bf16[16,3840]{1,0:T(8,128)(2,1)S(1)} %collective-permute-done.10.refs_1_, bf16[16,3840]{1,0:T(8,128)(2,1)S(1)} %collective-permute-done.11.refs_2_, ...), custom_call_target="tpu_custom_call" | custom-call | flops 917504 | bytes 1146880 | tf_op jit(solution)/shard_map/mix/pallas_call | solution.py:451
  (21 shorter events, 0.0 us)
Async XLA Ops:
  0.6 21.8 %collective-permute-start = (bf16[16,7168]{1,0:T(8,128)(2,1)}, bf16[16,7168]{1,0:T(8,128)(2,1)S(1)}, u32[]{:S(2)}, u32[]{:S(2)}) collective-permute-start(bf16[16,7168]{1,0:T(8,128)(2,1)} %bitcast.21), channel_id=1, source_target_pairs={{0,2},{1,3},{2,0},{3,1},{4,6},{5,7},{6,4},{7,5},{8,10},{9,11},{10,... | collective-permute-start | bytes 688136 | tf_op jit(solution)/shard_map/ppermute | solution.py:51
  3.7 19.5 %collective-permute-start.1 = (bf16[16,7168]{1,0:T(8,128)(2,1)}, bf16[16,7168]{1,0:T(8,128)(2,1)S(1)}, u32[]{:S(2)}, u32[]{:S(2)}) collective-permute-start(bf16[16,7168]{1,0:T(8,128)(2,1)} %bitcast.22), channel_id=1, source_target_pairs={{0,4},{1,5},{2,6},{3,7},{4,0},{5,1},{6,2},{7,3},{8,12},{9,13},{10,... | collective-permute-start | bytes 688136 | tf_op jit(solution)/shard_map/ppermute | solution.py:51
  6.3 16.9 %collective-permute-start.2 = (bf16[16,7168]{1,0:T(8,128)(2,1)}, bf16[16,7168]{1,0:T(8,128)(2,1)S(1)}, u32[]{:S(2)}, u32[]{:S(2)}) collective-permute-start(bf16[16,7168]{1,0:T(8,128)(2,1)} %bitcast.23), channel_id=1, source_target_pairs={{0,6},{1,7},{2,4},{3,5},{4,2},{5,3},{6,0},{7,1},{8,14},{9,15},{10,... | collective-permute-start | bytes 688136 | tf_op jit(solution)/shard_map/ppermute | solution.py:51
  10.4 16.7 %collective-permute-start.8 = (bf16[256,896]{1,0:T(8,128)(2,1)}, bf16[256,896]{1,0:T(8,128)(2,1)S(1)}, u32[]{:S(2)}, u32[]{:S(2)}) collective-permute-start(bf16[256,896]{1,0:T(8,128)(2,1)} %get-tuple-element.39), channel_id=1, source_target_pairs={{8,0},{16,8},{24,16},{9,1},{17,9},{25,17},{10,2},{18,10},{26,18},{... | collective-permute-start | bytes 1376264 | tf_op jit(solution)/shard_map/ppermute | solution.py:46
  11.7 13.9 %collective-permute-start.7 = (bf16[256,128]{1,0:T(8,128)(2,1)S(1)}, bf16[256,128]{1,0:T(8,128)(2,1)S(1)}, u32[]{:S(2)}, u32[]{:S(2)}) collective-permute-start(bf16[256,128]{1,0:T(8,128)(2,1)S(1)} %get-tuple-element.32.after_ref), channel_id=1, source_target_pairs={{8,0},{16,8},{24,16},{9,1},{17,9},{25,17},{10,2},{18,10},{26,18},{... | collective-permute-start | bytes 196616 | tf_op jit(solution)/shard_map/ppermute | solution.py:46
  13.0 9.4 %copy-start = (bf16[1,16,7168]{2,1,0:T(8,128)(2,1)S(1)}, bf16[1,16,7168]{2,1,0:T(8,128)(2,1)}, u32[]{:S(2)}) copy-start(bf16[1,16,7168]{2,1,0:T(8,128)(2,1)} %param.15) | copy-start | bytes 688132
  22.4 3.2 %collective-permute-start.3 = (bf16[16,7168]{1,0:T(8,128)(2,1)S(1)}, bf16[16,7168]{1,0:T(8,128)(2,1)S(1)}, u32[]{:S(2)}, u32[]{:S(2)}) collective-permute-start(bf16[16,7168]{1,0:T(8,128)(2,1)S(1)} %bitcast.24), channel_id=1, source_target_pairs={{0,1},{1,0},{2,3},{3,2},{4,5},{5,4},{6,7},{7,6},{8,9},{9,8},{10,11... | collective-permute-start | bytes 688136 | tf_op jit(solution)/shard_map/ppermute | solution.py:51
  23.2 2.4 %collective-permute-start.4 = (bf16[16,7168]{1,0:T(8,128)(2,1)S(1)}, bf16[16,7168]{1,0:T(8,128)(2,1)S(1)}, u32[]{:S(2)}, u32[]{:S(2)}) collective-permute-start(bf16[16,7168]{1,0:T(8,128)(2,1)S(1)} %get-tuple-element.34.refs_1_), channel_id=1, source_target_pairs={{0,1},{1,0},{2,3},{3,2},{4,5},{5,4},{6,7},{7,6},{8,9},{9,8},{10,11... | collective-permute-start | bytes 688136 | tf_op jit(solution)/shard_map/ppermute | solution.py:51
  23.2 2.4 %collective-permute-start.5 = (bf16[16,7168]{1,0:T(8,128)(2,1)S(1)}, bf16[16,7168]{1,0:T(8,128)(2,1)S(1)}, u32[]{:S(2)}, u32[]{:S(2)}) collective-permute-start(bf16[16,7168]{1,0:T(8,128)(2,1)S(1)} %get-tuple-element.35.refs_2_), channel_id=1, source_target_pairs={{0,1},{1,0},{2,3},{3,2},{4,5},{5,4},{6,7},{7,6},{8,9},{9,8},{10,11... | collective-permute-start | bytes 688136 | tf_op jit(solution)/shard_map/ppermute | solution.py:51
  25.6 1.5 %collective-permute-start.6 = (bf16[16,7168]{1,0:T(8,128)(2,1)S(1)}, bf16[16,7168]{1,0:T(8,128)(2,1)S(1)}, u32[]{:S(2)}, u32[]{:S(2)}) collective-permute-start(bf16[16,7168]{1,0:T(8,128)(2,1)S(1)} %get-tuple-element.36.refs_3_), channel_id=1, source_target_pairs={{0,1},{1,0},{2,3},{3,2},{4,5},{5,4},{6,7},{7,6},{8,9},{9,8},{10,11... | collective-permute-start | bytes 688136 | tf_op jit(solution)/shard_map/ppermute | solution.py:51
  27.1 0.8 %copy-start.1 = (bf16[256,896]{1,0:T(8,128)(2,1)}, bf16[256,896]{1,0:T(8,128)(2,1)S(1)}, u32[]{:S(2)}) copy-start(bf16[256,896]{1,0:T(8,128)(2,1)S(1)} %collective-permute-done.8.refs_12_.moved_ref) | copy-start | bytes 1376260
  27.8 21.7 %copy-start.2 = (f32[1,16,2]{1,2,0:T(2,128)S(1)}, f32[1,16,2]{1,2,0:T(2,128)}, u32[]{:S(2)}) copy-start(f32[1,16,2]{1,2,0:T(2,128)} %param.17) | copy-start | bytes 388
  27.9 21.7 %copy-start.3 = (s32[1,16,2]{1,2,0:T(2,128)S(1)}, s32[1,16,2]{1,2,0:T(2,128)}, u32[]{:S(2)}) copy-start(s32[1,16,2]{1,2,0:T(2,128)} %param.16) | copy-start | bytes 388
  37.8 1.9 %collective-permute-start.13 = (bf16[64,3584]{1,0:T(8,128)(2,1)S(1)}, bf16[64,3584]{1,0:T(8,128)(2,1)S(1)}, u32[]{:S(2)}, u32[]{:S(2)}) collective-permute-start(bf16[64,3584]{1,0:T(8,128)(2,1)S(1)} %get-tuple-element.47), channel_id=1, source_target_pairs={{0,1},{1,0},{2,3},{3,2},{4,5},{5,4},{6,7},{7,6},{8,9},{9,8},{10,11... | collective-permute-start | bytes 1376264 | tf_op jit(solution)/shard_map/ppermute | solution.py:51
  38.0 6.7 %collective-permute-start.9 = (bf16[64,3840]{1,0:T(8,128)(2,1)}, bf16[64,3840]{1,0:T(8,128)(2,1)S(1)}, u32[]{:S(2)}, u32[]{:S(2)}) collective-permute-start(bf16[64,3840]{1,0:T(8,128)(2,1)} %get-tuple-element.41), channel_id=1, source_target_pairs={{0,1},{1,0},{2,3},{3,2},{4,5},{5,4},{6,7},{7,6},{8,9},{9,8},{10,11... | collective-permute-start | bytes 1474568 | tf_op jit(solution)/shard_map/ppermute | solution.py:51
  39.7 8.8 %collective-permute-start.14 = (bf16[16,3584]{1,0:T(8,128)(2,1)S(1)}, bf16[16,3584]{1,0:T(8,128)(2,1)S(1)}, u32[]{:S(2)}, u32[]{:S(2)}) collective-permute-start(bf16[16,3584]{1,0:T(8,128)(2,1)S(1)} %get-tuple-element.49), channel_id=1, source_target_pairs={{0,2},{1,3},{2,0},{3,1},{4,6},{5,7},{6,4},{7,5},{8,10},{9,11},{10,... | collective-permute-start | bytes 344072 | tf_op jit(solution)/shard_map/ppermute | solution.py:51
  42.2 11.8 %collective-permute-start.15 = (bf16[16,3584]{1,0:T(8,128)(2,1)S(1)}, bf16[16,3584]{1,0:T(8,128)(2,1)S(1)}, u32[]{:S(2)}, u32[]{:S(2)}) collective-permute-start(bf16[16,3584]{1,0:T(8,128)(2,1)S(1)} %get-tuple-element.50), channel_id=1, source_target_pairs={{0,4},{1,5},{2,6},{3,7},{4,0},{5,1},{6,2},{7,3},{8,12},{9,13},{10,... | collective-permute-start | bytes 344072 | tf_op jit(solution)/shard_map/ppermute | solution.py:51
  43.9 10.1 %collective-permute-start.16 = (bf16[16,3584]{1,0:T(8,128)(2,1)S(1)}, bf16[16,3584]{1,0:T(8,128)(2,1)S(1)}, u32[]{:S(2)}, u32[]{:S(2)}) collective-permute-start(bf16[16,3584]{1,0:T(8,128)(2,1)S(1)} %get-tuple-element.51), channel_id=1, source_target_pairs={{0,6},{1,7},{2,4},{3,5},{4,2},{5,3},{6,0},{7,1},{8,14},{9,15},{10,... | collective-permute-start | bytes 344072 | tf_op jit(solution)/shard_map/ppermute | solution.py:51
  44.8 9.2 %collective-permute-start.10 = (bf16[16,3840]{1,0:T(8,128)(2,1)S(1)}, bf16[16,3840]{1,0:T(8,128)(2,1)S(1)}, u32[]{:S(2)}, u32[]{:S(2)}) collective-permute-start(bf16[16,3840]{1,0:T(8,128)(2,1)S(1)} %get-tuple-element.43), channel_id=1, source_target_pairs={{0,2},{1,3},{2,0},{3,1},{4,6},{5,7},{6,4},{7,5},{8,10},{9,11},{10,... | collective-permute-start | bytes 368648 | tf_op jit(solution)/shard_map/ppermute | solution.py:51
  45.9 18.5 %collective-permute-start.11 = (bf16[16,3840]{1,0:T(8,128)(2,1)S(1)}, bf16[16,3840]{1,0:T(8,128)(2,1)S(1)}, u32[]{:S(2)}, u32[]{:S(2)}) collective-permute-start(bf16[16,3840]{1,0:T(8,128)(2,1)S(1)} %get-tuple-element.44), channel_id=1, source_target_pairs={{0,4},{1,5},{2,6},{3,7},{4,0},{5,1},{6,2},{7,3},{8,12},{9,13},{10,... | collective-permute-start | bytes 368648 | tf_op jit(solution)/shard_map/ppermute | solution.py:51
  48.6 15.8 %collective-permute-start.12 = (bf16[16,3840]{1,0:T(8,128)(2,1)S(1)}, bf16[16,3840]{1,0:T(8,128)(2,1)S(1)}, u32[]{:S(2)}, u32[]{:S(2)}) collective-permute-start(bf16[16,3840]{1,0:T(8,128)(2,1)S(1)} %get-tuple-element.45), channel_id=1, source_target_pairs={{0,6},{1,7},{2,4},{3,5},{4,2},{5,3},{6,0},{7,1},{8,14},{9,15},{10,... | collective-permute-start | bytes 368648 | tf_op jit(solution)/shard_map/ppermute | solution.py:51

commit v4 on v3

--- a/solution.py
+++ b/solution.py
@@ -29,7 +29,7 @@
 AFTER = False
 LANES = 128
 VMEM = 8 * 1024 * 1024
-HELD_VMEM = 17 * 1024 * 1024
+HELD_VMEM = 16 * 1024 * 1024
 
 
 def in_hbm(array):
@@ -215,7 +215,7 @@
         out_specs=(here, here),
         scratch_shapes=[pltpu.VMEM((length, 2 * ROPE), jnp.float32)],
         out_shape=(
-            pltpu.HBM((length, width), jnp.bfloat16),
+            like((length, width), jnp.bfloat16),
             like(
                 (length, extra_lanes(length, len(order), folds, block_rows)), jnp.bfloat16
             ),
@@ -257,7 +257,7 @@
             flops=0, bytes_accessed=4 * moved.size, transcendentals=0
         ),
         name="settle",
-    )(in_hbm(moved), after)
+    )(moved, after)
 
 
 def tile_of(extent, most):
@@ -552,7 +552,7 @@
     folds, _ = fold_of(shared_rows, tokens.shape[0])
     splits = tuple(model_width * part // SPLITS[-1] for part in SPLITS)
     outs = experts(
-        [blocks[j] for j in order], gate_held, up_held, down_part, extra_moved, folds, splits, in_hbm(moved)
+        [blocks[j] for j in order], gate_held, up_held, down_part, extra_moved, folds, splits, moved
     )
     parts = len(splits) - 1
     mixed = [

time: 65.5 us -> 64.7 us (0.988)
  Pallas kernels: 26.4 us -> 24.7 us
  waiting for transfers between devices: 18.2 us -> 19.3 us
  local copies, waits for them, and re-layouts: 0.88 us -> 0.1 us
  starting transfers between devices: 19 us -> 19.7 us
    ppermute x15, waiting for transfers between devices: 16.4 us -> 18.4 us  [swap_xor(): return lax.ppermute(array, 'expert', [(i, i ^ offset) for i in range(size)])]
    pallas_call x1, Pallas kernels: 1.79 us -> 0.8 us  [settle(): pl.pallas_call(settle_kernel, in_specs=[pl.BlockSpec(memory_space=pltpu.V...]
    ppermute x2, waiting for transfers between devices: 1.87 us -> 0.94 us  [from_behind(): return lax.ppermute(array, axis, pairs)]
    unnamed x8 -> x6, local copies, waits for them, and re-layouts: 0.79 us -> 0.01 us
    pallas_call x1, Pallas kernels: 4.07 us -> 3.32 us  [attention_grads(): pl.pallas_call(functools.partial(attention_kernel, order=order, block_row...]
    ppermute x15, starting transfers between devices: 16.4 us -> 17.1 us  [swap_xor(): return lax.ppermute(array, 'expert', [(i, i ^ offset) for i in range(size)])]
  transfers between devices with their start and end apart: 17 -> 17, of which waited for: 6 -> 7; matrix products, arithmetic and copies ran while one was open for 0% -> 0% of each run, Pallas kernels for 24% -> 21%
where the time goes in v4:
time: 64.7 us; the launch traced here: 64.5 us
  Pallas kernels  24.7 us (38%)
  starting transfers between devices  19.7 us (30%)
  waiting for transfers between devices  19.3 us (30%)
  between operations  0.74 us (1%)
    ppermute x15, waiting for transfers between devices, swap_xor(): return lax.ppermute(array, 'expert', [(i, i ^ offset) for i in range(size)])  18.4 us
    ppermute x15, starting transfers between devices, swap_xor(): return lax.ppermute(array, 'expert', [(i, i ^ offset) for i in range(size)])  17.1 us
    pallas_call x1, Pallas kernels, experts(): pl.pallas_call(functools.partial(experts_kernel, count, folds, splits), i...  9.93 us
    pallas_call x1, Pallas kernels, hold(): pl.pallas_call(hold_kernel, in_specs=[pl.BlockSpec(memory_space=pl.ANY)]...  9.41 us
    pallas_call x1, Pallas kernels, attention_grads(): pl.pallas_call(functools.partial(attention_kernel, order=order, block_row...  3.32 us
    ppermute x2, starting transfers between devices, from_behind(): return lax.ppermute(array, axis, pairs)  2.58 us
  transfers between devices with their start and end apart: 17, of which 7 were waited for; matrix products, arithmetic and copies ran while one was open for 0% of the time, Pallas kernels for 21%

profile of v4, /device:TPU:0, one launch (start us, length us, event | category | flops | bytes accessed | tf_op | source)
XLA Modules:
  0.0 64.5 jit_solution(1959109907546482338)
XLA Ops:
  0.6 3.1 %collective-permute-start = (bf16[16,7168]{1,0:T(8,128)(2,1)}, bf16[16,7168]{1,0:T(8,128)(2,1)S(1)}, u32[]{:S(2)}, u32[]{:S(2)}) collective-permute-start(bf16[16,7168]{1,0:T(8,128)(2,1)} %bitcast.21), channel_id=1, source_target_pairs={{0,2},{1,3},{2,0},{3,1},{4,6},{5,7},{6,4},{7,5},{8,10},{9,11},{10,... | collective-permute-start | bytes 688136 | tf_op jit(solution)/shard_map/ppermute | solution.py:51
  3.7 2.6 %collective-permute-start.1 = (bf16[16,7168]{1,0:T(8,128)(2,1)}, bf16[16,7168]{1,0:T(8,128)(2,1)S(1)}, u32[]{:S(2)}, u32[]{:S(2)}) collective-permute-start(bf16[16,7168]{1,0:T(8,128)(2,1)} %bitcast.22), channel_id=1, source_target_pairs={{0,4},{1,5},{2,6},{3,7},{4,0},{5,1},{6,2},{7,3},{8,12},{9,13},{10,... | collective-permute-start | bytes 688136 | tf_op jit(solution)/shard_map/ppermute | solution.py:51
  6.3 3.3 %attention_grads.1 = (bf16[256,896]{1,0:T(8,128)(2,1)S(1)}, bf16[256,128]{1,0:T(8,128)(2,1)S(1)}) custom-call(bf16[256,256]{1,0:T(8,128)(2,1)} %bitcast.32, bf16[256,128]{1,0:T(8,128)(2,1)} %bitcast.39, bf16[256,256]{1,0:T(8,128)(2,1)} %bitcast.33, bf16[64,256]{1,0:T(8,128)(2,1)} %bitcast.41, bf16[256,256]{1,0:T(8,128)(2,1)} %bitcast.34, ...), custom_call_target="tpu_custom_call" | custom-call | flops 4000000000 | bytes 2000000 | tf_op jit(solution)/shard_map/attention_grads/pallas_call | solution.py:211
  9.6 1.3 %collective-permute-start.8 = (bf16[256,896]{1,0:T(8,128)(2,1)S(1)}, bf16[256,896]{1,0:T(8,128)(2,1)S(1)}, u32[]{:S(2)}, u32[]{:S(2)}) collective-permute-start(bf16[256,896]{1,0:T(8,128)(2,1)S(1)} %get-tuple-element.39), channel_id=1, source_target_pairs={{8,0},{16,8},{24,16},{9,1},{17,9},{25,17},{10,2},{18,10},{26,18},{... | collective-permute-start | bytes 1376264 | tf_op jit(solution)/shard_map/ppermute | solution.py:46
  10.9 1.3 %collective-permute-start.7 = (bf16[256,128]{1,0:T(8,128)(2,1)S(1)}, bf16[256,128]{1,0:T(8,128)(2,1)S(1)}, u32[]{:S(2)}, u32[]{:S(2)}) collective-permute-start(bf16[256,128]{1,0:T(8,128)(2,1)S(1)} %get-tuple-element.32.after_ref), channel_id=1, source_target_pairs={{8,0},{16,8},{24,16},{9,1},{17,9},{25,17},{10,2},{18,10},{26,18},{... | collective-permute-start | bytes 196616 | tf_op jit(solution)/shard_map/ppermute | solution.py:46
  12.2 0.0 copy-start
  12.3 9.4 %hold.1 = (bf16[7168,1024]{1,0:T(8,128)(2,1)S(1)}, bf16[7168,1024]{1,0:T(8,128)(2,1)S(1)}, f32[8,128]{1,0:T(8,128)S(1)}) custom-call(bf16[7168,1024]{1,0:T(8,128)(2,1)} %bitcast.26, bf16[7168,1024]{1,0:T(8,128)(2,1)} %bitcast.27, bf16[256,128]{1,0:T(8,128)(2,1)S(1)} %get-tuple-element.32.after_ref), custom_call_target="tpu_custom_call" | custom-call | bytes 29360128 | tf_op jit(solution)/shard_map/hold/pallas_call | solution.py:282
  21.7 0.1 collective-permute-start.3
  21.8 1.4 %collective-permute-done.1.refs_1_ = bf16[16,7168]{1,0:T(8,128)(2,1)S(1)} collective-permute-done((bf16[16,7168]{1,0:T(8,128)(2,1)}, bf16[16,7168]{1,0:T(8,128)(2,1)S(1)}, u32[]{:S(2)}, u32[]{:S(2)}) %collective-permute-start.1) | collective-permute-done | bytes 229408 | tf_op jit(solution)/shard_map/ppermute | solution.py:51
  23.2 0.5 collective-permute-start.5
  23.7 0.9 %collective-permute-done.7.refs_11_ = bf16[256,128]{1,0:T(8,128)(2,1)S(1)} collective-permute-done((bf16[256,128]{1,0:T(8,128)(2,1)S(1)}, bf16[256,128]{1,0:T(8,128)(2,1)S(1)}, u32[]{:S(2)}, u32[]{:S(2)}) %collective-permute-start.7) | collective-permute-done | bytes 65568 | tf_op jit(solution)/shard_map/ppermute | solution.py:46
  24.7 0.0 collective-permute-done.4.refs_5_
  24.7 0.3 collective-permute-done.5.refs_6_
  25.0 1.1 %collective-permute-done.6.refs_7_ = bf16[16,7168]{1,0:T(8,128)(2,1)S(1)} collective-permute-done((bf16[16,7168]{1,0:T(8,128)(2,1)S(1)}, bf16[16,7168]{1,0:T(8,128)(2,1)S(1)}, u32[]{:S(2)}, u32[]{:S(2)}) %collective-permute-start.6) | collective-permute-done | bytes 229408 | tf_op jit(solution)/shard_map/ppermute | solution.py:51
  26.1 9.9 %experts.1 = (bf16[64,3840]{1,0:T(8,128)(2,1)S(1)}, bf16[64,3584]{1,0:T(8,128)(2,1)S(1)}, bf16[64,3840]{1,0:T(8,128)(2,1)}, bf16[64,3584]{1,0:T(8,128)(2,1)S(1)}) custom-call(bf16[16,7168]{1,0:T(8,128)(2,1)S(1)} %bitcast.25, bf16[16,7168]{1,0:T(8,128)(2,1)S(1)} %get-tuple-element.34.refs_1_, bf16[16,7168]{1,0:T(8,128)(2,1)S(1)} %get-tuple-element.35.refs_2_, ...), custom_call_target="tpu_custom_call" | custom-call | flops 5637144576 | bytes 14680064 | tf_op jit(solution)/shard_map/experts/pallas_call | solution.py:362
  36.1 0.2 collective-permute-start.13
  36.3 0.4 collective-permute-start.9
  36.7 1.3 %collective-permute-done.13.came_ref = bf16[64,3584]{1,0:T(8,128)(2,1)S(1)} collective-permute-done((bf16[64,3584]{1,0:T(8,128)(2,1)S(1)}, bf16[64,3584]{1,0:T(8,128)(2,1)S(1)}, u32[]{:S(2)}, u32[]{:S(2)}) %collective-permute-start.13) | collective-permute-done | bytes 458784 | tf_op jit(solution)/shard_map/ppermute | solution.py:51
  38.0 0.1 add_slices.3
  38.1 3.3 %collective-permute-start.14 = (bf16[16,3584]{1,0:T(8,128)(2,1)S(1)}, bf16[16,3584]{1,0:T(8,128)(2,1)S(1)}, u32[]{:S(2)}, u32[]{:S(2)}) collective-permute-start(bf16[16,3584]{1,0:T(8,128)(2,1)S(1)} %get-tuple-element.49), channel_id=1, source_target_pairs={{0,2},{1,3},{2,0},{3,1},{4,6},{5,7},{6,4},{7,5},{8,10},{9,11},{10,... | collective-permute-start | bytes 344072 | tf_op jit(solution)/shard_map/ppermute | solution.py:51
  41.4 1.1 %collective-permute-start.15 = (bf16[16,3584]{1,0:T(8,128)(2,1)S(1)}, bf16[16,3584]{1,0:T(8,128)(2,1)S(1)}, u32[]{:S(2)}, u32[]{:S(2)}) collective-permute-start(bf16[16,3584]{1,0:T(8,128)(2,1)S(1)} %get-tuple-element.50), channel_id=1, source_target_pairs={{0,4},{1,5},{2,6},{3,7},{4,0},{5,1},{6,2},{7,3},{8,12},{9,13},{10,... | collective-permute-start | bytes 344072 | tf_op jit(solution)/shard_map/ppermute | solution.py:51
  42.5 1.4 %collective-permute-start.16 = (bf16[16,3584]{1,0:T(8,128)(2,1)S(1)}, bf16[16,3584]{1,0:T(8,128)(2,1)S(1)}, u32[]{:S(2)}, u32[]{:S(2)}) collective-permute-start(bf16[16,3584]{1,0:T(8,128)(2,1)S(1)} %get-tuple-element.51), channel_id=1, source_target_pairs={{0,6},{1,7},{2,4},{3,5},{4,2},{5,3},{6,0},{7,1},{8,14},{9,15},{10,... | collective-permute-start | bytes 344072 | tf_op jit(solution)/shard_map/ppermute | solution.py:51
  43.9 0.2 add_slices.2
  44.0 1.1 %collective-permute-start.10 = (bf16[16,3840]{1,0:T(8,128)(2,1)S(1)}, bf16[16,3840]{1,0:T(8,128)(2,1)S(1)}, u32[]{:S(2)}, u32[]{:S(2)}) collective-permute-start(bf16[16,3840]{1,0:T(8,128)(2,1)S(1)} %get-tuple-element.43), channel_id=1, source_target_pairs={{0,2},{1,3},{2,0},{3,1},{4,6},{5,7},{6,4},{7,5},{8,10},{9,11},{10,... | collective-permute-start | bytes 368648 | tf_op jit(solution)/shard_map/ppermute | solution.py:51
  45.1 2.0 %collective-permute-start.11 = (bf16[16,3840]{1,0:T(8,128)(2,1)S(1)}, bf16[16,3840]{1,0:T(8,128)(2,1)S(1)}, u32[]{:S(2)}, u32[]{:S(2)}) collective-permute-start(bf16[16,3840]{1,0:T(8,128)(2,1)S(1)} %get-tuple-element.44), channel_id=1, source_target_pairs={{0,4},{1,5},{2,6},{3,7},{4,0},{5,1},{6,2},{7,3},{8,12},{9,13},{10,... | collective-permute-start | bytes 368648 | tf_op jit(solution)/shard_map/ppermute | solution.py:51
  47.1 1.4 %collective-permute-start.12 = (bf16[16,3840]{1,0:T(8,128)(2,1)S(1)}, bf16[16,3840]{1,0:T(8,128)(2,1)S(1)}, u32[]{:S(2)}, u32[]{:S(2)}) collective-permute-start(bf16[16,3840]{1,0:T(8,128)(2,1)S(1)} %get-tuple-element.45), channel_id=1, source_target_pairs={{0,6},{1,7},{2,4},{3,5},{4,2},{5,3},{6,0},{7,1},{8,14},{9,15},{10,... | collective-permute-start | bytes 368648 | tf_op jit(solution)/shard_map/ppermute | solution.py:51
  48.5 0.1 select_reduce_fusion
  48.6 0.1 copy.25.weights_ref
  48.7 0.8 %settle.1 = (bf16[256,256]{1,0:T(8,128)(2,1)}, bf16[256,256]{1,0:T(8,128)(2,1)}, bf16[256,256]{1,0:T(8,128)(2,1)}, bf16[256,128]{1,0:T(8,128)(2,1)}) custom-call(bf16[256,896]{1,0:T(8,128)(2,1)S(1)} %collective-permute-done.8.refs_12_.moved_ref, bf16[16,3584]{1,0:T(8,128)(2,1)S(1)} %get-tuple-element.48.refs_4_.after_ref), custom_call_target="tpu_custom_call" | custom-call | bytes 917504 | tf_op jit(solution)/shard_map/settle/pallas_call | solution.py:251
  49.5 3.8 %collective-permute-done.15.refs_6_ = bf16[16,3584]{1,0:T(8,128)(2,1)S(1)} collective-permute-done((bf16[16,3584]{1,0:T(8,128)(2,1)S(1)}, bf16[16,3584]{1,0:T(8,128)(2,1)S(1)}, u32[]{:S(2)}, u32[]{:S(2)}) %collective-permute-start.15) | collective-permute-done | bytes 114720 | tf_op jit(solution)/shard_map/ppermute | solution.py:51
  53.3 10.4 %collective-permute-done.11.refs_2_ = bf16[16,3840]{1,0:T(8,128)(2,1)S(1)} collective-permute-done((bf16[16,3840]{1,0:T(8,128)(2,1)S(1)}, bf16[16,3840]{1,0:T(8,128)(2,1)S(1)}, u32[]{:S(2)}, u32[]{:S(2)}) %collective-permute-start.11) | collective-permute-done | bytes 122912 | tf_op jit(solution)/shard_map/ppermute | solution.py:51
  63.6 0.9 %mix.1 = (bf16[16,7168]{1,0:T(8,128)(2,1)}, f32[32,64]{1,0:T(8,128)}) custom-call(f32[16,4]{1,0:T(8,128)S(1)} %copy.25.weights_ref, bf16[16,3840]{1,0:T(8,128)(2,1)S(1)} %get-tuple-element.42.refs_0_, bf16[16,3840]{1,0:T(8,128)(2,1)S(1)} %collective-permute-done.10.refs_1_, bf16[16,3840]{1,0:T(8,128)(2,1)S(1)} %collective-permute-done.11.refs_2_, ...), custom_call_target="tpu_custom_call" | custom-call | flops 917504 | bytes 1146880 | tf_op jit(solution)/shard_map/mix/pallas_call | solution.py:451
  (19 shorter events, 0.0 us)
Async XLA Ops:
  0.6 21.0 %collective-permute-start = (bf16[16,7168]{1,0:T(8,128)(2,1)}, bf16[16,7168]{1,0:T(8,128)(2,1)S(1)}, u32[]{:S(2)}, u32[]{:S(2)}) collective-permute-start(bf16[16,7168]{1,0:T(8,128)(2,1)} %bitcast.21), channel_id=1, source_target_pairs={{0,2},{1,3},{2,0},{3,1},{4,6},{5,7},{6,4},{7,5},{8,10},{9,11},{10,... | collective-permute-start | bytes 688136 | tf_op jit(solution)/shard_map/ppermute | solution.py:51
  3.7 19.5 %collective-permute-start.1 = (bf16[16,7168]{1,0:T(8,128)(2,1)}, bf16[16,7168]{1,0:T(8,128)(2,1)S(1)}, u32[]{:S(2)}, u32[]{:S(2)}) collective-permute-start(bf16[16,7168]{1,0:T(8,128)(2,1)} %bitcast.22), channel_id=1, source_target_pairs={{0,4},{1,5},{2,6},{3,7},{4,0},{5,1},{6,2},{7,3},{8,12},{9,13},{10,... | collective-permute-start | bytes 688136 | tf_op jit(solution)/shard_map/ppermute | solution.py:51
  6.3 16.9 %collective-permute-start.2 = (bf16[16,7168]{1,0:T(8,128)(2,1)}, bf16[16,7168]{1,0:T(8,128)(2,1)S(1)}, u32[]{:S(2)}, u32[]{:S(2)}) collective-permute-start(bf16[16,7168]{1,0:T(8,128)(2,1)} %bitcast.23), channel_id=1, source_target_pairs={{0,6},{1,7},{2,4},{3,5},{4,2},{5,3},{6,0},{7,1},{8,14},{9,15},{10,... | collective-permute-start | bytes 688136 | tf_op jit(solution)/shard_map/ppermute | solution.py:51
  9.6 16.5 %collective-permute-start.8 = (bf16[256,896]{1,0:T(8,128)(2,1)S(1)}, bf16[256,896]{1,0:T(8,128)(2,1)S(1)}, u32[]{:S(2)}, u32[]{:S(2)}) collective-permute-start(bf16[256,896]{1,0:T(8,128)(2,1)S(1)} %get-tuple-element.39), channel_id=1, source_target_pairs={{8,0},{16,8},{24,16},{9,1},{17,9},{25,17},{10,2},{18,10},{26,18},{... | collective-permute-start | bytes 1376264 | tf_op jit(solution)/shard_map/ppermute | solution.py:46
  10.9 13.7 %collective-permute-start.7 = (bf16[256,128]{1,0:T(8,128)(2,1)S(1)}, bf16[256,128]{1,0:T(8,128)(2,1)S(1)}, u32[]{:S(2)}, u32[]{:S(2)}) collective-permute-start(bf16[256,128]{1,0:T(8,128)(2,1)S(1)} %get-tuple-element.32.after_ref), channel_id=1, source_target_pairs={{8,0},{16,8},{24,16},{9,1},{17,9},{25,17},{10,2},{18,10},{26,18},{... | collective-permute-start | bytes 196616 | tf_op jit(solution)/shard_map/ppermute | solution.py:46
  12.2 9.4 %copy-start = (bf16[1,16,7168]{2,1,0:T(8,128)(2,1)S(1)}, bf16[1,16,7168]{2,1,0:T(8,128)(2,1)}, u32[]{:S(2)}) copy-start(bf16[1,16,7168]{2,1,0:T(8,128)(2,1)} %param.15) | copy-start | bytes 688132
  21.7 3.0 %collective-permute-start.3 = (bf16[16,7168]{1,0:T(8,128)(2,1)S(1)}, bf16[16,7168]{1,0:T(8,128)(2,1)S(1)}, u32[]{:S(2)}, u32[]{:S(2)}) collective-permute-start(bf16[16,7168]{1,0:T(8,128)(2,1)S(1)} %bitcast.24), channel_id=1, source_target_pairs={{0,1},{1,0},{2,3},{3,2},{4,5},{5,4},{6,7},{7,6},{8,9},{9,8},{10,11... | collective-permute-start | bytes 688136 | tf_op jit(solution)/shard_map/ppermute | solution.py:51
  23.2 1.5 %collective-permute-start.4 = (bf16[16,7168]{1,0:T(8,128)(2,1)S(1)}, bf16[16,7168]{1,0:T(8,128)(2,1)S(1)}, u32[]{:S(2)}, u32[]{:S(2)}) collective-permute-start(bf16[16,7168]{1,0:T(8,128)(2,1)S(1)} %get-tuple-element.34.refs_1_), channel_id=1, source_target_pairs={{0,1},{1,0},{2,3},{3,2},{4,5},{5,4},{6,7},{7,6},{8,9},{9,8},{10,11... | collective-permute-start | bytes 688136 | tf_op jit(solution)/shard_map/ppermute | solution.py:51
  23.2 1.8 %collective-permute-start.5 = (bf16[16,7168]{1,0:T(8,128)(2,1)S(1)}, bf16[16,7168]{1,0:T(8,128)(2,1)S(1)}, u32[]{:S(2)}, u32[]{:S(2)}) collective-permute-start(bf16[16,7168]{1,0:T(8,128)(2,1)S(1)} %get-tuple-element.35.refs_2_), channel_id=1, source_target_pairs={{0,1},{1,0},{2,3},{3,2},{4,5},{5,4},{6,7},{7,6},{8,9},{9,8},{10,11... | collective-permute-start | bytes 688136 | tf_op jit(solution)/shard_map/ppermute | solution.py:51
  24.6 1.5 %collective-permute-start.6 = (bf16[16,7168]{1,0:T(8,128)(2,1)S(1)}, bf16[16,7168]{1,0:T(8,128)(2,1)S(1)}, u32[]{:S(2)}, u32[]{:S(2)}) collective-permute-start(bf16[16,7168]{1,0:T(8,128)(2,1)S(1)} %get-tuple-element.36.refs_3_), channel_id=1, source_target_pairs={{0,1},{1,0},{2,3},{3,2},{4,5},{5,4},{6,7},{7,6},{8,9},{9,8},{10,11... | collective-permute-start | bytes 688136 | tf_op jit(solution)/shard_map/ppermute | solution.py:51
  26.1 22.4 %copy-start.1 = (f32[1,16,2]{1,2,0:T(2,128)S(1)}, f32[1,16,2]{1,2,0:T(2,128)}, u32[]{:S(2)}) copy-start(f32[1,16,2]{1,2,0:T(2,128)} %param.17) | copy-start | bytes 388
  26.1 22.4 %copy-start.2 = (s32[1,16,2]{1,2,0:T(2,128)S(1)}, s32[1,16,2]{1,2,0:T(2,128)}, u32[]{:S(2)}) copy-start(s32[1,16,2]{1,2,0:T(2,128)} %param.16) | copy-start | bytes 388
  36.1 1.9 %collective-permute-start.13 = (bf16[64,3584]{1,0:T(8,128)(2,1)S(1)}, bf16[64,3584]{1,0:T(8,128)(2,1)S(1)}, u32[]{:S(2)}, u32[]{:S(2)}) collective-permute-start(bf16[64,3584]{1,0:T(8,128)(2,1)S(1)} %get-tuple-element.47), channel_id=1, source_target_pairs={{0,1},{1,0},{2,3},{3,2},{4,5},{5,4},{6,7},{7,6},{8,9},{9,8},{10,11... | collective-permute-start | bytes 1376264 | tf_op jit(solution)/shard_map/ppermute | solution.py:51
  36.3 7.6 %collective-permute-start.9 = (bf16[64,3840]{1,0:T(8,128)(2,1)}, bf16[64,3840]{1,0:T(8,128)(2,1)S(1)}, u32[]{:S(2)}, u32[]{:S(2)}) collective-permute-start(bf16[64,3840]{1,0:T(8,128)(2,1)} %get-tuple-element.41), channel_id=1, source_target_pairs={{0,1},{1,0},{2,3},{3,2},{4,5},{5,4},{6,7},{7,6},{8,9},{9,8},{10,11... | collective-permute-start | bytes 1474568 | tf_op jit(solution)/shard_map/ppermute | solution.py:51
  38.1 9.0 %collective-permute-start.14 = (bf16[16,3584]{1,0:T(8,128)(2,1)S(1)}, bf16[16,3584]{1,0:T(8,128)(2,1)S(1)}, u32[]{:S(2)}, u32[]{:S(2)}) collective-permute-start(bf16[16,3584]{1,0:T(8,128)(2,1)S(1)} %get-tuple-element.49), channel_id=1, source_target_pairs={{0,2},{1,3},{2,0},{3,1},{4,6},{5,7},{6,4},{7,5},{8,10},{9,11},{10,... | collective-permute-start | bytes 344072 | tf_op jit(solution)/shard_map/ppermute | solution.py:51
  41.4 11.8 %collective-permute-start.15 = (bf16[16,3584]{1,0:T(8,128)(2,1)S(1)}, bf16[16,3584]{1,0:T(8,128)(2,1)S(1)}, u32[]{:S(2)}, u32[]{:S(2)}) collective-permute-start(bf16[16,3584]{1,0:T(8,128)(2,1)S(1)} %get-tuple-element.50), channel_id=1, source_target_pairs={{0,4},{1,5},{2,6},{3,7},{4,0},{5,1},{6,2},{7,3},{8,12},{9,13},{10,... | collective-permute-start | bytes 344072 | tf_op jit(solution)/shard_map/ppermute | solution.py:51
  42.5 10.8 %collective-permute-start.16 = (bf16[16,3584]{1,0:T(8,128)(2,1)S(1)}, bf16[16,3584]{1,0:T(8,128)(2,1)S(1)}, u32[]{:S(2)}, u32[]{:S(2)}) collective-permute-start(bf16[16,3584]{1,0:T(8,128)(2,1)S(1)} %get-tuple-element.51), channel_id=1, source_target_pairs={{0,6},{1,7},{2,4},{3,5},{4,2},{5,3},{6,0},{7,1},{8,14},{9,15},{10,... | collective-permute-start | bytes 344072 | tf_op jit(solution)/shard_map/ppermute | solution.py:51
  44.0 9.2 %collective-permute-start.10 = (bf16[16,3840]{1,0:T(8,128)(2,1)S(1)}, bf16[16,3840]{1,0:T(8,128)(2,1)S(1)}, u32[]{:S(2)}, u32[]{:S(2)}) collective-permute-start(bf16[16,3840]{1,0:T(8,128)(2,1)S(1)} %get-tuple-element.43), channel_id=1, source_target_pairs={{0,2},{1,3},{2,0},{3,1},{4,6},{5,7},{6,4},{7,5},{8,10},{9,11},{10,... | collective-permute-start | bytes 368648 | tf_op jit(solution)/shard_map/ppermute | solution.py:51
  45.1 18.5 %collective-permute-start.11 = (bf16[16,3840]{1,0:T(8,128)(2,1)S(1)}, bf16[16,3840]{1,0:T(8,128)(2,1)S(1)}, u32[]{:S(2)}, u32[]{:S(2)}) collective-permute-start(bf16[16,3840]{1,0:T(8,128)(2,1)S(1)} %get-tuple-element.44), channel_id=1, source_target_pairs={{0,4},{1,5},{2,6},{3,7},{4,0},{5,1},{6,2},{7,3},{8,12},{9,13},{10,... | collective-permute-start | bytes 368648 | tf_op jit(solution)/shard_map/ppermute | solution.py:51
  47.1 16.5 %collective-permute-start.12 = (bf16[16,3840]{1,0:T(8,128)(2,1)S(1)}, bf16[16,3840]{1,0:T(8,128)(2,1)S(1)}, u32[]{:S(2)}, u32[]{:S(2)}) collective-permute-start(bf16[16,3840]{1,0:T(8,128)(2,1)S(1)} %get-tuple-element.45), channel_id=1, source_target_pairs={{0,6},{1,7},{2,4},{3,5},{4,2},{5,3},{6,0},{7,1},{8,14},{9,15},{10,... | collective-permute-start | bytes 368648 | tf_op jit(solution)/shard_map/ppermute | solution.py:51

commit v5 on v4

--- a/solution.py
+++ b/solution.py
@@ -24,12 +24,11 @@
 
 SPLITS = (0, 1, 2)
 TILE = 1024
-FETCHES = 2
 DOWN_TILE = 896
 AFTER = False
 LANES = 128
 VMEM = 8 * 1024 * 1024
-HELD_VMEM = 16 * 1024 * 1024
+HELD_VMEM = 9 * 1024 * 1024
 
 
 def in_hbm(array):
@@ -264,12 +263,12 @@
     return max(t for t in range(128, most + 1, 128) if extent % t == 0)
 
 
-def hold_kernel(gate_ref, up_ref, after_ref, gate_out, up_out, token_out, sems):
+def hold_kernel(up_ref, down_ref, after_ref, up_out, down_out, token_out, sems):
     del after_ref
     token_out[...] = jnp.zeros_like(token_out)
     copies = [
-        pltpu.make_async_copy(gate_ref, gate_out, sems.at[0]),
-        pltpu.make_async_copy(up_ref, up_out, sems.at[1]),
+        pltpu.make_async_copy(up_ref, up_out, sems.at[0]),
+        pltpu.make_async_copy(down_ref.at[:, : down_out.shape[1]], down_out, sems.at[1]),
     ]
     for copy in copies:
         copy.start()
@@ -277,44 +276,38 @@
         copy.wait()
 
 
-def hold(gate_part, up_part, after):
+def hold(up_part, down_part, width, after):
     here = pl.BlockSpec(memory_space=pltpu.VMEM)
     return pl.pallas_call(
         hold_kernel,
         in_specs=[pl.BlockSpec(memory_space=pl.ANY)] * 3,
         out_specs=(here, here, here),
         out_shape=(
-            pltpu.VMEM(gate_part.shape, gate_part.dtype),
             pltpu.VMEM(up_part.shape, up_part.dtype),
+            pltpu.VMEM((down_part.shape[0], width), down_part.dtype),
             jax.ShapeDtypeStruct((8, LANES), jnp.float32),
         ),
         scratch_shapes=[pltpu.SemaphoreType.DMA((2,))],
         compiler_params=pltpu.CompilerParams(vmem_limit_bytes=HELD_VMEM),
         cost_estimate=pl.CostEstimate(
-            flops=0, bytes_accessed=4 * gate_part.size, transcendentals=0
+            flops=0, bytes_accessed=2 * up_part.size, transcendentals=0
         ),
         name="hold",
-    )(in_hbm(gate_part), in_hbm(up_part), after)
+    )(in_hbm(up_part), in_hbm(down_part), after)
 
 
 def experts_kernel(count, folds, splits, *refs):
     blocks = refs[:count]
-    gate_ref, up_ref, down_ref, extra_ref, _ = refs[count : count + 5]
-    rest = refs[count + 5 :]
+    gate_ref, up_ref, first_ref, down_ref, extra_ref, _ = refs[count : count + 6]
+    rest = refs[count + 6 :]
     parts = len(splits) - 1
     kept_refs, sent_refs, rest = rest[:parts], rest[parts : 2 * parts], rest[2 * parts :]
-    gate_sum, up_sum, hidden_ref, held_ref, down_sems = rest
+    gate_sum, up_sum, hidden_ref, rest_ref, down_sem = rest
     width = blocks[0].shape[1]
     tile = tile_of(width, TILE)
-    share = width // FETCHES
-    fetches = []
-    for i in range(FETCHES):
-        there = slice(i * share, (i + 1) * share)
-        fetches.append(
-            pltpu.make_async_copy(down_ref.at[:, there], held_ref.at[:, there], down_sems.at[i])
-        )
-    for fetch in fetches:
-        fetch.start()
+    share = first_ref.shape[1]
+    fetch = pltpu.make_async_copy(down_ref.at[:, share:], rest_ref, down_sem)
+    fetch.start()
     for i in range(width // tile):
         there = slice(i * tile, (i + 1) * tile)
         rows = jnp.concatenate([b[:, there] for b in blocks], axis=0)
@@ -339,10 +332,10 @@
     part = 0
     tile = tile_of(share, DOWN_TILE)
     for i in range(width // tile):
-        if i * tile % share == 0:
-            fetches[i * tile // share].wait()
-        there = slice(i * tile, (i + 1) * tile)
-        out = jnp.dot(hidden_ref[...], held_ref[:, there], preferred_element_type=jnp.float32)
+        if i * tile == share:
+            fetch.wait()
+        weights, back = (first_ref, 0) if i * tile < share else (rest_ref, share)
+        out = jnp.dot(hidden_ref[...], weights[:, i * tile - back : (i + 1) * tile - back], preferred_element_type=jnp.float32)
         while splits[part + 1] <= i * tile:
             part += 1
         mine = slice(i * tile - splits[part], (i + 1) * tile - splits[part])
@@ -350,7 +343,7 @@
         sent_refs[part][:, mine] = out[half:].astype(jnp.bfloat16)
 
 
-def experts(blocks, gate_held, up_held, down_part, extra, folds, splits, after):
+def experts(blocks, gate_held, up_held, down_held, down_part, extra, folds, splits, after):
     count = len(blocks)
     block_rows, width = blocks[0].shape
     rows, hidden_width = count * block_rows, gate_held.shape[1]
@@ -361,14 +354,14 @@
     out = [jax.ShapeDtypeStruct((rows // 2, w), jnp.bfloat16) for w in widths]
     return pl.pallas_call(
         functools.partial(experts_kernel, count, folds, splits),
-        in_specs=[here] * (count + 2) + [anywhere, here, anywhere],
+        in_specs=[here] * (count + 3) + [anywhere, here, anywhere],
         out_shape=(*out, *out),
         scratch_shapes=[
             pltpu.VMEM((rows, hidden_width), jnp.float32),
             pltpu.VMEM((rows, hidden_width), jnp.float32),
             pltpu.VMEM((rows, hidden_width), jnp.bfloat16),
-            pltpu.VMEM((hidden_width, width), jnp.bfloat16),
-            pltpu.SemaphoreType.DMA((FETCHES,)),
+            pltpu.VMEM((hidden_width, width - down_held.shape[1]), jnp.bfloat16),
+            pltpu.SemaphoreType.DMA(()),
         ],
         compiler_params=pltpu.CompilerParams(vmem_limit_bytes=HELD_VMEM),
         cost_estimate=pl.CostEstimate(
@@ -377,7 +370,7 @@
             transcendentals=0,
         ),
         name="experts",
-    )(*blocks, in_vmem(gate_held), in_vmem(up_held), in_hbm(down_part), extra, after)
+    )(*blocks, in_vmem(gate_held), in_vmem(up_held), in_vmem(down_held), in_hbm(down_part), extra, after)
 
 
 def both_terms(value):
@@ -546,13 +539,16 @@
     )
     extra_moved = from_behind(extra, "section", -1)
     moved = from_behind(moving, "section", -1)
-    gate_held, up_held, token = hold(gate_part, up_part, extra)
+    up_held, down_held, token = hold(
+        up_part, down_part, model_width // 2, extra
+    )
+    gate_held = gate_part
     blocks = gathered(tokens, group, token)
     shared_rows = key_rope.shape[1] // lax.axis_size("expert")
     folds, _ = fold_of(shared_rows, tokens.shape[0])
     splits = tuple(model_width * part // SPLITS[-1] for part in SPLITS)
     outs = experts(
-        [blocks[j] for j in order], gate_held, up_held, down_part, extra_moved, folds, splits, moved
+        [blocks[j] for j in order], gate_held, up_held, down_held, down_part, extra_moved, folds, splits, moved
     )
     parts = len(splits) - 1
     mixed = [

time: 64.7 us -> 63 us (0.974)
  Pallas kernels: 24.7 us -> 21.1 us
  waiting for transfers between devices: 19.3 us -> 21.2 us
    pallas_call x1, Pallas kernels: 9.41 us -> 7.43 us  [hold(): pl.pallas_call(hold_kernel, in_specs=[pl.BlockSpec(memory_space=pl.ANY)]...]
    ppermute x15, waiting for transfers between devices: 18.4 us -> 20.2 us  [swap_xor(): return lax.ppermute(array, 'expert', [(i, i ^ offset) for i in range(size)])]
    pallas_call x1, Pallas kernels: 9.93 us -> 8.18 us  [experts(): pl.pallas_call(functools.partial(experts_kernel, count, folds, splits), i...]
  transfers between devices with their start and end apart: 17 -> 17, of which waited for: 7 -> 7; matrix products, arithmetic and copies ran while one was open for 0% -> 0% of each run, Pallas kernels for 21% -> 19%
where the time goes in v5:
time: 63 us; the launch traced here: 62.9 us
  waiting for transfers between devices  21.2 us (34%)
  Pallas kernels  21.1 us (33%)
  starting transfers between devices  19.5 us (31%)
  between operations  0.8 us (1%)
    ppermute x15, waiting for transfers between devices, swap_xor(): return lax.ppermute(array, 'expert', [(i, i ^ offset) for i in range(size)])  20.2 us
    ppermute x15, starting transfers between devices, swap_xor(): return lax.ppermute(array, 'expert', [(i, i ^ offset) for i in range(size)])  17 us
    pallas_call x1, Pallas kernels, experts(): pl.pallas_call(functools.partial(experts_kernel, count, folds, splits), i...  8.18 us
    pallas_call x1, Pallas kernels, hold(): pl.pallas_call(hold_kernel, in_specs=[pl.BlockSpec(memory_space=pl.ANY)]...  7.43 us
    pallas_call x1, Pallas kernels, attention_grads(): pl.pallas_call(functools.partial(attention_kernel, order=order, block_row...  3.46 us
    ppermute x2, starting transfers between devices, from_behind(): return lax.ppermute(array, axis, pairs)  2.58 us
  transfers between devices with their start and end apart: 17, of which 7 were waited for; matrix products, arithmetic and copies ran while one was open for 0% of the time, Pallas kernels for 19%

profile of v5, /device:TPU:0, one launch (start us, length us, event | category | flops | bytes accessed | tf_op | source)
XLA Modules:
  0.0 62.9 jit_solution(7210198844168163477)
XLA Ops:
  0.6 3.1 %collective-permute-start = (bf16[16,7168]{1,0:T(8,128)(2,1)}, bf16[16,7168]{1,0:T(8,128)(2,1)S(1)}, u32[]{:S(2)}, u32[]{:S(2)}) collective-permute-start(bf16[16,7168]{1,0:T(8,128)(2,1)} %bitcast.24), channel_id=1, source_target_pairs={{0,2},{1,3},{2,0},{3,1},{4,6},{5,7},{6,4},{7,5},{8,10},{9,11},{10,... | collective-permute-start | bytes 688136 | tf_op jit(solution)/shard_map/ppermute | solution.py:50
  3.7 2.6 %collective-permute-start.1 = (bf16[16,7168]{1,0:T(8,128)(2,1)}, bf16[16,7168]{1,0:T(8,128)(2,1)S(1)}, u32[]{:S(2)}, u32[]{:S(2)}) collective-permute-start(bf16[16,7168]{1,0:T(8,128)(2,1)} %bitcast.25), channel_id=1, source_target_pairs={{0,4},{1,5},{2,6},{3,7},{4,0},{5,1},{6,2},{7,3},{8,12},{9,13},{10,... | collective-permute-start | bytes 688136 | tf_op jit(solution)/shard_map/ppermute | solution.py:50
  6.3 3.5 %attention_grads.1 = (bf16[256,896]{1,0:T(8,128)(2,1)S(1)}, bf16[256,128]{1,0:T(8,128)(2,1)S(1)}) custom-call(bf16[256,256]{1,0:T(8,128)(2,1)} %bitcast.35, bf16[256,128]{1,0:T(8,128)(2,1)} %bitcast.42, bf16[256,256]{1,0:T(8,128)(2,1)} %bitcast.36, bf16[64,256]{1,0:T(8,128)(2,1)} %bitcast.44, bf16[256,256]{1,0:T(8,128)(2,1)} %bitcast.37, ...), custom_call_target="tpu_custom_call" | custom-call | flops 4000000000 | bytes 2000000 | tf_op jit(solution)/shard_map/attention_grads/pallas_call | solution.py:210
  9.8 1.3 %collective-permute-start.8 = (bf16[256,896]{1,0:T(8,128)(2,1)S(1)}, bf16[256,896]{1,0:T(8,128)(2,1)S(1)}, u32[]{:S(2)}, u32[]{:S(2)}) collective-permute-start(bf16[256,896]{1,0:T(8,128)(2,1)S(1)} %get-tuple-element.39), channel_id=1, source_target_pairs={{8,0},{16,8},{24,16},{9,1},{17,9},{25,17},{10,2},{18,10},{26,18},{... | collective-permute-start | bytes 1376264 | tf_op jit(solution)/shard_map/ppermute | solution.py:45
  11.1 1.3 %collective-permute-start.7 = (bf16[256,128]{1,0:T(8,128)(2,1)S(1)}, bf16[256,128]{1,0:T(8,128)(2,1)S(1)}, u32[]{:S(2)}, u32[]{:S(2)}) collective-permute-start(bf16[256,128]{1,0:T(8,128)(2,1)S(1)} %get-tuple-element.32.after_ref), channel_id=1, source_target_pairs={{8,0},{16,8},{24,16},{9,1},{17,9},{25,17},{10,2},{18,10},{26,18},{... | collective-permute-start | bytes 196616 | tf_op jit(solution)/shard_map/ppermute | solution.py:45
  12.4 0.0 copy-start
  12.4 0.0 slice-start.2
  12.4 7.4 %hold.1 = (bf16[7168,1024]{1,0:T(8,128)(2,1)S(1)}, bf16[1024,3584]{1,0:T(8,128)(2,1)S(1)}, f32[8,128]{1,0:T(8,128)S(1)}) custom-call(bf16[7168,1024]{1,0:T(8,128)(2,1)} %bitcast.31, bf16[1024,7168]{1,0:T(8,128)(2,1)} %bitcast.29, bf16[256,128]{1,0:T(8,128)(2,1)S(1)} %get-tuple-element.32.after_ref), custom_call_target="tpu_custom_call" | custom-call | bytes 14680064 | tf_op jit(solution)/shard_map/hold/pallas_call | solution.py:281
  19.9 0.1 collective-permute-start.3
  20.0 3.2 %collective-permute-done.1.refs_1_ = bf16[16,7168]{1,0:T(8,128)(2,1)S(1)} collective-permute-done((bf16[16,7168]{1,0:T(8,128)(2,1)}, bf16[16,7168]{1,0:T(8,128)(2,1)S(1)}, u32[]{:S(2)}, u32[]{:S(2)}) %collective-permute-start.1) | collective-permute-done | bytes 229408 | tf_op jit(solution)/shard_map/ppermute | solution.py:50
  23.2 0.5 collective-permute-start.5
  23.7 1.1 %collective-permute-done.7.refs_12_ = bf16[256,128]{1,0:T(8,128)(2,1)S(1)} collective-permute-done((bf16[256,128]{1,0:T(8,128)(2,1)S(1)}, bf16[256,128]{1,0:T(8,128)(2,1)S(1)}, u32[]{:S(2)}, u32[]{:S(2)}) %collective-permute-start.7) | collective-permute-done | bytes 65568 | tf_op jit(solution)/shard_map/ppermute | solution.py:45
  24.8 0.2 collective-permute-done.5.refs_6_
  25.0 1.3 %collective-permute-done.6.refs_7_ = bf16[16,7168]{1,0:T(8,128)(2,1)S(1)} collective-permute-done((bf16[16,7168]{1,0:T(8,128)(2,1)S(1)}, bf16[16,7168]{1,0:T(8,128)(2,1)S(1)}, u32[]{:S(2)}, u32[]{:S(2)}) %collective-permute-start.6) | collective-permute-done | bytes 229408 | tf_op jit(solution)/shard_map/ppermute | solution.py:50
  26.3 8.2 %experts.1 = (bf16[64,3840]{1,0:T(8,128)(2,1)S(1)}, bf16[64,3584]{1,0:T(8,128)(2,1)S(1)}, bf16[64,3840]{1,0:T(8,128)(2,1)}, bf16[64,3584]{1,0:T(8,128)(2,1)S(1)}) custom-call(bf16[16,7168]{1,0:T(8,128)(2,1)S(1)} %bitcast.28, bf16[16,7168]{1,0:T(8,128)(2,1)S(1)} %get-tuple-element.34.refs_1_, bf16[16,7168]{1,0:T(8,128)(2,1)S(1)} %get-tuple-element.35.refs_2_, ...), custom_call_target="tpu_custom_call" | custom-call | flops 5637144576 | bytes 14680064 | tf_op jit(solution)/shard_map/experts/pallas_call | solution.py:355
  34.5 0.2 collective-permute-start.13
  34.7 0.4 collective-permute-start.9
  35.1 1.3 %collective-permute-done.13.came_ref = bf16[64,3584]{1,0:T(8,128)(2,1)S(1)} collective-permute-done((bf16[64,3584]{1,0:T(8,128)(2,1)S(1)}, bf16[64,3584]{1,0:T(8,128)(2,1)S(1)}, u32[]{:S(2)}, u32[]{:S(2)}) %collective-permute-start.13) | collective-permute-done | bytes 458784 | tf_op jit(solution)/shard_map/ppermute | solution.py:50
  36.4 0.1 add_slices.3
  36.5 3.2 %collective-permute-start.14 = (bf16[16,3584]{1,0:T(8,128)(2,1)S(1)}, bf16[16,3584]{1,0:T(8,128)(2,1)S(1)}, u32[]{:S(2)}, u32[]{:S(2)}) collective-permute-start(bf16[16,3584]{1,0:T(8,128)(2,1)S(1)} %get-tuple-element.49), channel_id=1, source_target_pairs={{0,2},{1,3},{2,0},{3,1},{4,6},{5,7},{6,4},{7,5},{8,10},{9,11},{10,... | collective-permute-start | bytes 344072 | tf_op jit(solution)/shard_map/ppermute | solution.py:50
  39.7 1.1 %collective-permute-start.15 = (bf16[16,3584]{1,0:T(8,128)(2,1)S(1)}, bf16[16,3584]{1,0:T(8,128)(2,1)S(1)}, u32[]{:S(2)}, u32[]{:S(2)}) collective-permute-start(bf16[16,3584]{1,0:T(8,128)(2,1)S(1)} %get-tuple-element.50), channel_id=1, source_target_pairs={{0,4},{1,5},{2,6},{3,7},{4,0},{5,1},{6,2},{7,3},{8,12},{9,13},{10,... | collective-permute-start | bytes 344072 | tf_op jit(solution)/shard_map/ppermute | solution.py:50
  40.8 1.4 %collective-permute-start.16 = (bf16[16,3584]{1,0:T(8,128)(2,1)S(1)}, bf16[16,3584]{1,0:T(8,128)(2,1)S(1)}, u32[]{:S(2)}, u32[]{:S(2)}) collective-permute-start(bf16[16,3584]{1,0:T(8,128)(2,1)S(1)} %get-tuple-element.51), channel_id=1, source_target_pairs={{0,6},{1,7},{2,4},{3,5},{4,2},{5,3},{6,0},{7,1},{8,14},{9,15},{10,... | collective-permute-start | bytes 344072 | tf_op jit(solution)/shard_map/ppermute | solution.py:50
  42.2 0.2 add_slices.2
  42.4 1.1 %collective-permute-start.10 = (bf16[16,3840]{1,0:T(8,128)(2,1)S(1)}, bf16[16,3840]{1,0:T(8,128)(2,1)S(1)}, u32[]{:S(2)}, u32[]{:S(2)}) collective-permute-start(bf16[16,3840]{1,0:T(8,128)(2,1)S(1)} %get-tuple-element.43), channel_id=1, source_target_pairs={{0,2},{1,3},{2,0},{3,1},{4,6},{5,7},{6,4},{7,5},{8,10},{9,11},{10,... | collective-permute-start | bytes 368648 | tf_op jit(solution)/shard_map/ppermute | solution.py:50
  43.5 2.0 %collective-permute-start.11 = (bf16[16,3840]{1,0:T(8,128)(2,1)S(1)}, bf16[16,3840]{1,0:T(8,128)(2,1)S(1)}, u32[]{:S(2)}, u32[]{:S(2)}) collective-permute-start(bf16[16,3840]{1,0:T(8,128)(2,1)S(1)} %get-tuple-element.44), channel_id=1, source_target_pairs={{0,4},{1,5},{2,6},{3,7},{4,0},{5,1},{6,2},{7,3},{8,12},{9,13},{10,... | collective-permute-start | bytes 368648 | tf_op jit(solution)/shard_map/ppermute | solution.py:50
  45.4 1.4 %collective-permute-start.12 = (bf16[16,3840]{1,0:T(8,128)(2,1)S(1)}, bf16[16,3840]{1,0:T(8,128)(2,1)S(1)}, u32[]{:S(2)}, u32[]{:S(2)}) collective-permute-start(bf16[16,3840]{1,0:T(8,128)(2,1)S(1)} %get-tuple-element.45), channel_id=1, source_target_pairs={{0,6},{1,7},{2,4},{3,5},{4,2},{5,3},{6,0},{7,1},{8,14},{9,15},{10,... | collective-permute-start | bytes 368648 | tf_op jit(solution)/shard_map/ppermute | solution.py:50
  46.8 0.1 select_reduce_fusion
  46.9 0.1 copy.25.weights_ref
  47.0 0.8 %settle.1 = (bf16[256,256]{1,0:T(8,128)(2,1)}, bf16[256,256]{1,0:T(8,128)(2,1)}, bf16[256,256]{1,0:T(8,128)(2,1)}, bf16[256,128]{1,0:T(8,128)(2,1)}) custom-call(bf16[256,896]{1,0:T(8,128)(2,1)S(1)} %collective-permute-done.8.refs_13_.moved_ref, bf16[16,3584]{1,0:T(8,128)(2,1)S(1)} %get-tuple-element.48.refs_4_.after_ref), custom_call_target="tpu_custom_call" | custom-call | bytes 917504 | tf_op jit(solution)/shard_map/settle/pallas_call | solution.py:250
  47.8 3.8 %collective-permute-done.15.refs_6_ = bf16[16,3584]{1,0:T(8,128)(2,1)S(1)} collective-permute-done((bf16[16,3584]{1,0:T(8,128)(2,1)S(1)}, bf16[16,3584]{1,0:T(8,128)(2,1)S(1)}, u32[]{:S(2)}, u32[]{:S(2)}) %collective-permute-start.15) | collective-permute-done | bytes 114720 | tf_op jit(solution)/shard_map/ppermute | solution.py:50
  51.6 10.4 %collective-permute-done.11.refs_2_ = bf16[16,3840]{1,0:T(8,128)(2,1)S(1)} collective-permute-done((bf16[16,3840]{1,0:T(8,128)(2,1)S(1)}, bf16[16,3840]{1,0:T(8,128)(2,1)S(1)}, u32[]{:S(2)}, u32[]{:S(2)}) %collective-permute-start.11) | collective-permute-done | bytes 122912 | tf_op jit(solution)/shard_map/ppermute | solution.py:50
  61.9 0.9 %mix.1 = (bf16[16,7168]{1,0:T(8,128)(2,1)}, f32[32,64]{1,0:T(8,128)}) custom-call(f32[16,4]{1,0:T(8,128)S(1)} %copy.25.weights_ref, bf16[16,3840]{1,0:T(8,128)(2,1)S(1)} %get-tuple-element.42.refs_0_, bf16[16,3840]{1,0:T(8,128)(2,1)S(1)} %collective-permute-done.10.refs_1_, bf16[16,3840]{1,0:T(8,128)(2,1)S(1)} %collective-permute-done.11.refs_2_, ...), custom_call_target="tpu_custom_call" | custom-call | flops 917504 | bytes 1146880 | tf_op jit(solution)/shard_map/mix/pallas_call | solution.py:444
  (28 shorter events, 0.1 us)
Async XLA Ops:
  0.6 19.2 %collective-permute-start = (bf16[16,7168]{1,0:T(8,128)(2,1)}, bf16[16,7168]{1,0:T(8,128)(2,1)S(1)}, u32[]{:S(2)}, u32[]{:S(2)}) collective-permute-start(bf16[16,7168]{1,0:T(8,128)(2,1)} %bitcast.24), channel_id=1, source_target_pairs={{0,2},{1,3},{2,0},{3,1},{4,6},{5,7},{6,4},{7,5},{8,10},{9,11},{10,... | collective-permute-start | bytes 688136 | tf_op jit(solution)/shard_map/ppermute | solution.py:50
  3.7 19.5 %collective-permute-start.1 = (bf16[16,7168]{1,0:T(8,128)(2,1)}, bf16[16,7168]{1,0:T(8,128)(2,1)S(1)}, u32[]{:S(2)}, u32[]{:S(2)}) collective-permute-start(bf16[16,7168]{1,0:T(8,128)(2,1)} %bitcast.25), channel_id=1, source_target_pairs={{0,4},{1,5},{2,6},{3,7},{4,0},{5,1},{6,2},{7,3},{8,12},{9,13},{10,... | collective-permute-start | bytes 688136 | tf_op jit(solution)/shard_map/ppermute | solution.py:50
  6.3 16.9 %collective-permute-start.2 = (bf16[16,7168]{1,0:T(8,128)(2,1)}, bf16[16,7168]{1,0:T(8,128)(2,1)S(1)}, u32[]{:S(2)}, u32[]{:S(2)}) collective-permute-start(bf16[16,7168]{1,0:T(8,128)(2,1)} %bitcast.26), channel_id=1, source_target_pairs={{0,6},{1,7},{2,4},{3,5},{4,2},{5,3},{6,0},{7,1},{8,14},{9,15},{10,... | collective-permute-start | bytes 688136 | tf_op jit(solution)/shard_map/ppermute | solution.py:50
  6.3 20.0 %slice-start = ((s8[14680064]{0:T(1024)(128)(4,1)}), s8[4194304]{0:T(1024)(128)(4,1)S(1)}, s32[]{:S(2)}) async-start(s8[14680064]{0:T(1024)(128)(4,1)} %bitcast.21), calls=%async_computation | async-start | bytes 8388608
  6.3 20.0 %slice-start.1 = ((s8[14680064]{0:T(1024)(128)(4,1)}), s8[4194304]{0:T(1024)(128)(4,1)S(1)}, s32[]{:S(2)}) async-start(s8[14680064]{0:T(1024)(128)(4,1)} %bitcast.21), calls=%async_computation.1 | async-start | bytes 8388608
  9.8 16.5 %collective-permute-start.8 = (bf16[256,896]{1,0:T(8,128)(2,1)S(1)}, bf16[256,896]{1,0:T(8,128)(2,1)S(1)}, u32[]{:S(2)}, u32[]{:S(2)}) collective-permute-start(bf16[256,896]{1,0:T(8,128)(2,1)S(1)} %get-tuple-element.39), channel_id=1, source_target_pairs={{8,0},{16,8},{24,16},{9,1},{17,9},{25,17},{10,2},{18,10},{26,18},{... | collective-permute-start | bytes 1376264 | tf_op jit(solution)/shard_map/ppermute | solution.py:45
  11.1 13.7 %collective-permute-start.7 = (bf16[256,128]{1,0:T(8,128)(2,1)S(1)}, bf16[256,128]{1,0:T(8,128)(2,1)S(1)}, u32[]{:S(2)}, u32[]{:S(2)}) collective-permute-start(bf16[256,128]{1,0:T(8,128)(2,1)S(1)} %get-tuple-element.32.after_ref), channel_id=1, source_target_pairs={{8,0},{16,8},{24,16},{9,1},{17,9},{25,17},{10,2},{18,10},{26,18},{... | collective-permute-start | bytes 196616 | tf_op jit(solution)/shard_map/ppermute | solution.py:45
  12.4 7.5 %copy-start = (bf16[1,16,7168]{2,1,0:T(8,128)(2,1)S(1)}, bf16[1,16,7168]{2,1,0:T(8,128)(2,1)}, u32[]{:S(2)}) copy-start(bf16[1,16,7168]{2,1,0:T(8,128)(2,1)} %param.15) | copy-start | bytes 688132
  12.4 13.9 %slice-start.2 = ((s8[14680064]{0:T(1024)(128)(4,1)}), s8[4194304]{0:T(1024)(128)(4,1)S(1)}, s32[]{:S(2)}) async-start(s8[14680064]{0:T(1024)(128)(4,1)} %bitcast.21), calls=%async_computation.2 | async-start | bytes 8388608
  12.4 13.9 %slice-start.3 = ((s8[14680064]{0:T(1024)(128)(4,1)}), s8[2097152]{0:T(1024)(128)(4,1)S(1)}, s32[]{:S(2)}) async-start(s8[14680064]{0:T(1024)(128)(4,1)} %bitcast.21), calls=%async_computation.3 | async-start | bytes 4194304
  19.9 4.9 %collective-permute-start.3 = (bf16[16,7168]{1,0:T(8,128)(2,1)S(1)}, bf16[16,7168]{1,0:T(8,128)(2,1)S(1)}, u32[]{:S(2)}, u32[]{:S(2)}) collective-permute-start(bf16[16,7168]{1,0:T(8,128)(2,1)S(1)} %bitcast.27), channel_id=1, source_target_pairs={{0,1},{1,0},{2,3},{3,2},{4,5},{5,4},{6,7},{7,6},{8,9},{9,8},{10,11... | collective-permute-start | bytes 688136 | tf_op jit(solution)/shard_map/ppermute | solution.py:50
  23.2 1.6 %collective-permute-start.4 = (bf16[16,7168]{1,0:T(8,128)(2,1)S(1)}, bf16[16,7168]{1,0:T(8,128)(2,1)S(1)}, u32[]{:S(2)}, u32[]{:S(2)}) collective-permute-start(bf16[16,7168]{1,0:T(8,128)(2,1)S(1)} %get-tuple-element.34.refs_1_), channel_id=1, source_target_pairs={{0,1},{1,0},{2,3},{3,2},{4,5},{5,4},{6,7},{7,6},{8,9},{9,8},{10,11... | collective-permute-start | bytes 688136 | tf_op jit(solution)/shard_map/ppermute | solution.py:50
  23.2 1.8 %collective-permute-start.5 = (bf16[16,7168]{1,0:T(8,128)(2,1)S(1)}, bf16[16,7168]{1,0:T(8,128)(2,1)S(1)}, u32[]{:S(2)}, u32[]{:S(2)}) collective-permute-start(bf16[16,7168]{1,0:T(8,128)(2,1)S(1)} %get-tuple-element.35.refs_2_), channel_id=1, source_target_pairs={{0,1},{1,0},{2,3},{3,2},{4,5},{5,4},{6,7},{7,6},{8,9},{9,8},{10,11... | collective-permute-start | bytes 688136 | tf_op jit(solution)/shard_map/ppermute | solution.py:50
  24.8 1.5 %collective-permute-start.6 = (bf16[16,7168]{1,0:T(8,128)(2,1)S(1)}, bf16[16,7168]{1,0:T(8,128)(2,1)S(1)}, u32[]{:S(2)}, u32[]{:S(2)}) collective-permute-start(bf16[16,7168]{1,0:T(8,128)(2,1)S(1)} %get-tuple-element.36.refs_3_), channel_id=1, source_target_pairs={{0,1},{1,0},{2,3},{3,2},{4,5},{5,4},{6,7},{7,6},{8,9},{9,8},{10,11... | collective-permute-start | bytes 688136 | tf_op jit(solution)/shard_map/ppermute | solution.py:50
  26.3 20.5 %copy-start.1 = (f32[1,16,2]{1,2,0:T(2,128)S(1)}, f32[1,16,2]{1,2,0:T(2,128)}, u32[]{:S(2)}) copy-start(f32[1,16,2]{1,2,0:T(2,128)} %param.17) | copy-start | bytes 388
  26.3 20.5 %copy-start.2 = (s32[1,16,2]{1,2,0:T(2,128)S(1)}, s32[1,16,2]{1,2,0:T(2,128)}, u32[]{:S(2)}) copy-start(s32[1,16,2]{1,2,0:T(2,128)} %param.16) | copy-start | bytes 388
  34.5 1.9 %collective-permute-start.13 = (bf16[64,3584]{1,0:T(8,128)(2,1)S(1)}, bf16[64,3584]{1,0:T(8,128)(2,1)S(1)}, u32[]{:S(2)}, u32[]{:S(2)}) collective-permute-start(bf16[64,3584]{1,0:T(8,128)(2,1)S(1)} %get-tuple-element.47), channel_id=1, source_target_pairs={{0,1},{1,0},{2,3},{3,2},{4,5},{5,4},{6,7},{7,6},{8,9},{9,8},{10,11... | collective-permute-start | bytes 1376264 | tf_op jit(solution)/shard_map/ppermute | solution.py:50
  34.7 7.5 %collective-permute-start.9 = (bf16[64,3840]{1,0:T(8,128)(2,1)}, bf16[64,3840]{1,0:T(8,128)(2,1)S(1)}, u32[]{:S(2)}, u32[]{:S(2)}) collective-permute-start(bf16[64,3840]{1,0:T(8,128)(2,1)} %get-tuple-element.41), channel_id=1, source_target_pairs={{0,1},{1,0},{2,3},{3,2},{4,5},{5,4},{6,7},{7,6},{8,9},{9,8},{10,11... | collective-permute-start | bytes 1474568 | tf_op jit(solution)/shard_map/ppermute | solution.py:50
  36.5 8.9 %collective-permute-start.14 = (bf16[16,3584]{1,0:T(8,128)(2,1)S(1)}, bf16[16,3584]{1,0:T(8,128)(2,1)S(1)}, u32[]{:S(2)}, u32[]{:S(2)}) collective-permute-start(bf16[16,3584]{1,0:T(8,128)(2,1)S(1)} %get-tuple-element.49), channel_id=1, source_target_pairs={{0,2},{1,3},{2,0},{3,1},{4,6},{5,7},{6,4},{7,5},{8,10},{9,11},{10,... | collective-permute-start | bytes 344072 | tf_op jit(solution)/shard_map/ppermute | solution.py:50
  39.7 11.8 %collective-permute-start.15 = (bf16[16,3584]{1,0:T(8,128)(2,1)S(1)}, bf16[16,3584]{1,0:T(8,128)(2,1)S(1)}, u32[]{:S(2)}, u32[]{:S(2)}) collective-permute-start(bf16[16,3584]{1,0:T(8,128)(2,1)S(1)} %get-tuple-element.50), channel_id=1, source_target_pairs={{0,4},{1,5},{2,6},{3,7},{4,0},{5,1},{6,2},{7,3},{8,12},{9,13},{10,... | collective-permute-start | bytes 344072 | tf_op jit(solution)/shard_map/ppermute | solution.py:50
  40.8 10.8 %collective-permute-start.16 = (bf16[16,3584]{1,0:T(8,128)(2,1)S(1)}, bf16[16,3584]{1,0:T(8,128)(2,1)S(1)}, u32[]{:S(2)}, u32[]{:S(2)}) collective-permute-start(bf16[16,3584]{1,0:T(8,128)(2,1)S(1)} %get-tuple-element.51), channel_id=1, source_target_pairs={{0,6},{1,7},{2,4},{3,5},{4,2},{5,3},{6,0},{7,1},{8,14},{9,15},{10,... | collective-permute-start | bytes 344072 | tf_op jit(solution)/shard_map/ppermute | solution.py:50
  42.4 9.2 %collective-permute-start.10 = (bf16[16,3840]{1,0:T(8,128)(2,1)S(1)}, bf16[16,3840]{1,0:T(8,128)(2,1)S(1)}, u32[]{:S(2)}, u32[]{:S(2)}) collective-permute-start(bf16[16,3840]{1,0:T(8,128)(2,1)S(1)} %get-tuple-element.43), channel_id=1, source_target_pairs={{0,2},{1,3},{2,0},{3,1},{4,6},{5,7},{6,4},{7,5},{8,10},{9,11},{10,... | collective-permute-start | bytes 368648 | tf_op jit(solution)/shard_map/ppermute | solution.py:50
  43.5 18.5 %collective-permute-start.11 = (bf16[16,3840]{1,0:T(8,128)(2,1)S(1)}, bf16[16,3840]{1,0:T(8,128)(2,1)S(1)}, u32[]{:S(2)}, u32[]{:S(2)}) collective-permute-start(bf16[16,3840]{1,0:T(8,128)(2,1)S(1)} %get-tuple-element.44), channel_id=1, source_target_pairs={{0,4},{1,5},{2,6},{3,7},{4,0},{5,1},{6,2},{7,3},{8,12},{9,13},{10,... | collective-permute-start | bytes 368648 | tf_op jit(solution)/shard_map/ppermute | solution.py:50
  45.4 16.5 %collective-permute-start.12 = (bf16[16,3840]{1,0:T(8,128)(2,1)S(1)}, bf16[16,3840]{1,0:T(8,128)(2,1)S(1)}, u32[]{:S(2)}, u32[]{:S(2)}) collective-permute-start(bf16[16,3840]{1,0:T(8,128)(2,1)S(1)} %get-tuple-element.45), channel_id=1, source_target_pairs={{0,6},{1,7},{2,4},{3,5},{4,2},{5,3},{6,0},{7,1},{8,14},{9,15},{10,... | collective-permute-start | bytes 368648 | tf_op jit(solution)/shard_map/ppermute | solution.py:50
